TPU v7x, 32 devices: a whole 2x2x4 slice. The times are simulated.
32 devices in a mesh: seq: 8 (over z, x), head: 4 (over y, core).
Axes of the slice: x: 2, y: 2, z: 4, core: 2. Of those that a mesh axis runs over, the one named last changes fastest.
Arguments:
- patch_tokens: bfloat16 [32, 256, 3072], P('seq'), may hold values from -26 to 26
- projection: bfloat16 [3072, 2, 3, 1536], P(None, None, None, 'head'), may hold values from -0.14433757 to 0.14433757
Outputs:
- space_out: bfloat16 [32, 256, 1536], P('seq', None, 'head')
- time_out: bfloat16 [32, 256, 1536], P('seq', None, 'head')
- clip_factor: float32 [2, 12], P(None, 'head')
All inputs are finite; a program needn't handle non-finite values.
Results may differ from a plain program's by a relative error of at most 0.0085.
The roundings to bfloat16 on the way count: a program that leaves them out, or rounds other values in their place, can miss the bound.
Values may be sent and summed in bfloat16 or wider, within the bound.
No kernel may reach another device: no remote copies, remote signals or barrier semaphores. Data moves between devices by JAX's collectives and lax.ppermute only.
A program may use at most 192 MiB of HBM per device.

v0:
```python
import math

import jax
import jax.numpy as jnp
from jax import lax
from jax.sharding import PartitionSpec as P

HD = 128


clip_limit = 30.0


def mixing(scores):
    highest = jnp.max(scores, axis=-1, keepdims=True)
    expon = jnp.exp(scores - highest)
    return (expon / jnp.sum(expon, axis=-1, keepdims=True)).astype(jnp.bfloat16)


def attend_space(query_part, key_part, value_part):
    score_scale = 1.0 / math.sqrt(HD)
    scores = (
        jnp.einsum("fihd,fjhd->fhij", query_part, key_part, preferred_element_type=jnp.float32)
        * score_scale
    )
    highest = jnp.max(scores, axis=(0, 2, 3))
    result = jnp.einsum(
        "fhij,fjhd->fihd", mixing(scores), value_part, preferred_element_type=jnp.float32
    )
    return (result.astype(jnp.bfloat16), highest)


def attend_time(triple):
    query_part, key_part, value_part = triple
    score_scale = 1.0 / math.sqrt(HD)
    scores = (
        jnp.einsum("fphd,gphd->phfg", query_part, key_part, preferred_element_type=jnp.float32)
        * score_scale
    )
    highest = jnp.max(scores, axis=(0, 2, 3))
    result = jnp.einsum(
        "phfg,gphd->fphd", mixing(scores), value_part, preferred_element_type=jnp.float32
    )
    returned = lax.all_to_all(
        result.astype(jnp.bfloat16), "seq", split_axis=0, concat_axis=1, tiled=True
    )
    return (returned, highest.reshape(1, 1, -1, 1))


def body(patch_tokens, projection):
    frames_dev, positions, width = patch_tokens.shape
    heads_dev = projection.shape[-1] // HD
    token_rows = patch_tokens.reshape(frames_dev * positions, width)
    parts = jnp.dot(token_rows, projection.reshape(width, -1), preferred_element_type=jnp.float32)
    parts = parts.astype(jnp.bfloat16).reshape(frames_dev, positions, 2, 3, heads_dev, HD)
    space_parts = parts[:, :, 0]
    time_parts = parts[:, :, 1]

    def time_section():
        triple = (time_parts[:, :, 0], time_parts[:, :, 1], time_parts[:, :, 2])
        result, highest = attend_time(
            (
                lax.all_to_all(triple[0], "seq", split_axis=1, concat_axis=0, tiled=True),
                lax.all_to_all(triple[1], "seq", split_axis=1, concat_axis=0, tiled=True),
                lax.all_to_all(triple[2], "seq", split_axis=1, concat_axis=0, tiled=True),
            )
        )
        highest = highest.reshape(-1)
        highest = lax.pmax(highest, "seq")
        return (result, highest)

    result, highest = attend_space(space_parts[:, :, 0], space_parts[:, :, 1], space_parts[:, :, 2])
    highest = lax.pmax(highest, "seq")
    time_result, time_high = time_section()
    peak = jnp.stack([highest, time_high])
    clip_factor = jnp.sqrt(clip_limit / jnp.maximum(peak, clip_limit))
    space_out = result.reshape(frames_dev, positions, heads_dev * HD)
    time_out = time_result.reshape(frames_dev, positions, heads_dev * HD)
    return (space_out, time_out, clip_factor)


def solution(mesh):
    placed = (P("seq", None, None), P(None, None, None, "head"))
    return jax.shard_map(
        body,
        mesh=mesh,
        in_specs=placed,
        out_specs=(P("seq", None, "head"), P("seq", None, "head"), P(None, "head")),
        check_vma=False,
    )
```

profile of v0, /device:TPU:0, one launch (start us, length us, event | category | flops | bytes accessed | tf_op | source)
XLA Modules:
  0.0 198.5 jit_solution(4106261085940051248)
XLA Ops:
  0.6 35.0 %copy.57 = bf16[3072,2,3,384]{0,3,2,1:T(8,128)(2,1)} copy(bf16[3072,2,3,384]{3,1,2,0:T(2,128)(2,1)} %param.3) | data formatting | bytes 28311552 | tf_op args[1]
  35.7 20.7 %convolution_convert_fusion = bf16[1024,2304]{1,0:T(8,128)(2,1)} fusion(bf16[1024,3072]{1,0:T(8,128)(2,1)} %bitcast.71, bf16[3072,2304]{0,1:T(8,128)(2,1)} %bitcast.56), kind=kOutput, calls=%fused_computation.2 | convolution fusion | flops 14497873920 | bytes 25165824 | tf_op jit(solution)/shard_map/dot_general | solution.py:54
  56.3 6.6 %copy.58 = bf16[1024,2304]{0,1:T(8,128)(2,1)} copy(bf16[1024,2304]{1,0:T(8,128)(2,1)} %convolution_convert_fusion) | data formatting | bytes 9437184 | tf_op jit(solution)/shard_map/convert_element_type | solution.py:55
  63.0 8.9 %reshape.28 = bf16[4,256,2,3,3,128]{1,0,5,4,3,2:T(4,128)(2,1)} reshape(bf16[1024,2304]{0,1:T(8,128)(2,1)} %copy.58) | data formatting | bytes 9437184 | tf_op jit(solution)/shard_map/reshape | solution.py:55
  71.9 4.0 %slice_bitcast_fusion = (bf16[4,256,3,3,128]{1,0,4,3,2:T(4,128)(2,1)S(1)}, bf16[4,256,1,3,3,128]{1,0,5,4,3,2:T(4,128)(2,1)S(1)}) fusion(bf16[4,256,2,3,3,128]{1,0,5,4,3,2:T(4,128)(2,1)} %reshape.28), kind=kLoop, calls=%fused_computation.8 | loop fusion | bytes 9437184 | tf_op jit(solution)/shard_map/squeeze | solution.py:57
  75.9 2.0 %slice_bitcast_fusion.1 = (bf16[4,256,3,128]{1,0,3,2:T(4,128)(2,1)}, bf16[4,256,3,128]{1,0,3,2:T(4,128)(2,1)}, bf16[4,256,3,128]{1,0,3,2:T(4,128)(2,1)S(1)}) fusion(bf16[4,256,3,3,128]{1,0,4,3,2:T(4,128)(2,1)S(1)} %get-tuple-element.20), kind=kLoop, calls=%fused_computation.19 | loop fusion | bytes 4718592 | tf_op jit(solution)/shard_map/squeeze | solution.py:60
  77.9 2.4 %copy.68 = bf16[4,256,3,128]{3,0,2,1:T(4,128)(2,1)} copy(bf16[4,256,3,128]{1,0,3,2:T(4,128)(2,1)} %get-tuple-element.22) | data formatting | bytes 1572864 | tf_op jit(solution)/shard_map/squeeze | solution.py:60
  80.3 7.2 %all-to-all-start.2 = ((bf16[4,256,3,128]{3,0,2,1:T(4,128)(2,1)}), bf16[4,256,3,128]{3,0,2,1:T(4,128)(2,1)}, u32[]{:S(2)}, u32[]{:S(2)}) async-start(bf16[4,256,3,128]{3,0,2,1:T(4,128)(2,1)} %copy.68), calls=%async_computation.2 | async-start | bytes 1572864 | tf_op jit(solution)/shard_map/all_to_all | solution.py:64
  87.5 2.4 %copy.65 = bf16[4,256,3,128]{3,0,2,1:T(4,128)(2,1)} copy(bf16[4,256,3,128]{1,0,3,2:T(4,128)(2,1)} %get-tuple-element.23) | data formatting | bytes 1572864 | tf_op jit(solution)/shard_map/squeeze | solution.py:60
  89.9 17.9 %all-to-all-done.2 = bf16[4,256,3,128]{3,0,2,1:T(4,128)(2,1)} async-done(((bf16[4,256,3,128]{3,0,2,1:T(4,128)(2,1)}), bf16[4,256,3,128]{3,0,2,1:T(4,128)(2,1)}, u32[]{:S(2)}, u32[]{:S(2)}) %all-to-all-start.2) | async-done | bytes 786464 | tf_op jit(solution)/shard_map/all_to_all | solution.py:64
  107.8 4.2 %all-to-all-start.1 = ((bf16[4,256,3,128]{3,0,2,1:T(4,128)(2,1)}), bf16[4,256,3,128]{3,0,2,1:T(4,128)(2,1)}, u32[]{:S(2)}, u32[]{:S(2)}) async-start(bf16[4,256,3,128]{3,0,2,1:T(4,128)(2,1)} %copy.65), calls=%async_computation.1 | async-start | bytes 1572864 | tf_op jit(solution)/shard_map/all_to_all | solution.py:63
  112.0 1.5 copy.62
  113.5 18.4 %all-to-all-done.1 = bf16[4,256,3,128]{3,0,2,1:T(4,128)(2,1)} async-done(((bf16[4,256,3,128]{3,0,2,1:T(4,128)(2,1)}), bf16[4,256,3,128]{3,0,2,1:T(4,128)(2,1)}, u32[]{:S(2)}, u32[]{:S(2)}) %all-to-all-start.1) | async-done | bytes 786464 | tf_op jit(solution)/shard_map/all_to_all | solution.py:63
  131.9 3.7 %all-to-all-start = ((bf16[4,256,3,128]{3,0,2,1:T(4,128)(2,1)}), bf16[4,256,3,128]{3,0,2,1:T(4,128)(2,1)S(1)}, u32[]{:S(2)}, u32[]{:S(2)}) async-start(bf16[4,256,3,128]{3,0,2,1:T(4,128)(2,1)} %copy.62), calls=%async_computation | async-start | bytes 1572864 | tf_op jit(solution)/shard_map/all_to_all | solution.py:65
  135.7 3.7 %copy.78 = bf16[4,256,1,3,3,128]{5,1,4,0,3,2:T(8,128)(2,1)} copy(bf16[4,256,1,3,3,128]{1,0,5,4,3,2:T(4,128)(2,1)S(1)} %get-tuple-element.21) | data formatting | bytes 4718592
  139.4 1.3 copy.69
  140.7 0.6 copy.70
  141.3 1.6 copy.66
  142.9 0.6 copy.67
  143.5 12.3 %all-to-all-done = bf16[4,256,3,128]{3,0,2,1:T(4,128)(2,1)S(1)} async-done(((bf16[4,256,3,128]{3,0,2,1:T(4,128)(2,1)}), bf16[4,256,3,128]{3,0,2,1:T(4,128)(2,1)S(1)}, u32[]{:S(2)}, u32[]{:S(2)}) %all-to-all-start) | async-done | bytes 786464 | tf_op jit(solution)/shard_map/all_to_all | solution.py:65
  155.9 0.6 copy.64
  156.6 1.9 fusion.18
  158.5 2.0 %fusion.10 = bf16[32,32,3,128]{3,0,2,1:T(8,128)(2,1)S(1)} fusion(bf16[32,32,3,128]{3,0,2,1:T(8,128)(2,1)S(1)} %bitcast.68, f32[32,3,32,32]{2,3,1,0:T(8,128)} %get-tuple-element.28, f32[32,3,32]{2,1,0:T(4,128)S(1)} %get-tuple-element.27), kind=kOutput, calls=%fused_computation.17 | convolution fusion | flops 25755648 | bytes 1978368 | tf_op jit(solution)/shard_map/phfg,gphd->fphd/dot_general | solution.py:41
  160.5 1.2 copy.72
  161.7 3.6 %all-to-all-start.3 = ((bf16[32,32,3,128]{3,1,2,0:T(8,128)(2,1)}), bf16[32,32,3,128]{3,1,2,0:T(8,128)(2,1)S(1)}, u32[]{:S(2)}, u32[]{:S(2)}) async-start(bf16[32,32,3,128]{3,1,2,0:T(8,128)(2,1)} %copy.72), calls=%async_computation.3 | async-start | bytes 1572864 | tf_op jit(solution)/shard_map/all_to_all | solution.py:44
  165.2 0.7 multiply_reduce_fusion
  165.9 2.4 %fusion.17 = (f32[4,3,256]{2,1,0:T(4,128)S(1)}, f32[4,3,256,256]{2,3,1,0:T(8,128)S(1)}) fusion(f32[4,3,256,256]{2,3,1,0:T(8,128)S(1)} %get-tuple-element.30), kind=kOutput, calls=%fused_computation.32 | output fusion | flops 3145983 | bytes 6303744 | tf_op jit(solution)/shard_map/sub | solution.py:16
  168.3 1.4 fusion.9
  169.7 2.3 %copy.74 = bf16[4,256,384]{2,1,0:T(8,128)(2,1)} copy(bf16[4,256,384]{1,2,0:T(8,128)(2,1)} %bitcast.69) | data formatting | bytes 1572864
  172.0 2.0 %fusion.19 = f32[3]{0:T(128)S(1)} fusion(bf16[32,32,3,128]{3,0,2,1:T(8,128)(2,1)} %bitcast.67, bf16[32,32,3,128]{3,0,2,1:T(8,128)(2,1)} %bitcast.65), kind=kOutput, calls=%fused_computation.34 | convolution fusion | flops 25362428 | bytes 1572876 | tf_op jit(solution)/shard_map/fphd,gphd->phfg/dot_general | solution.py:37
  174.0 21.9 %all-reduce = (f32[1,3]{1,0:T(1,128)S(1)}, f32[1,3]{1,0:T(1,128)S(1)}) all-reduce(f32[1,3]{1,0:T(1,128)S(1)} %bitcast.72, f32[1,3]{1,0:T(1,128)S(1)} %bitcast.70), channel_id=1, replica_groups=mesh['seq'=8,'head'=4] {'seq'}, use_global_device_ids=true, to_apply=%region_7.0 | all-reduce | flops 6 | bytes 48 | tf_op jit(solution)/shard_map/pmax | solution.py:69
  197.1 1.4 reshape.30
  (10 shorter events, 1.3 us)
Async XLA Ops:
  80.3 27.5 %all-to-all-start.2 = ((bf16[4,256,3,128]{3,0,2,1:T(4,128)(2,1)}), bf16[4,256,3,128]{3,0,2,1:T(4,128)(2,1)}, u32[]{:S(2)}, u32[]{:S(2)}) async-start(bf16[4,256,3,128]{3,0,2,1:T(4,128)(2,1)} %copy.68), calls=%async_computation.2 | async-start | bytes 1572864 | tf_op jit(solution)/shard_map/all_to_all | solution.py:64
  107.8 24.1 %all-to-all-start.1 = ((bf16[4,256,3,128]{3,0,2,1:T(4,128)(2,1)}), bf16[4,256,3,128]{3,0,2,1:T(4,128)(2,1)}, u32[]{:S(2)}, u32[]{:S(2)}) async-start(bf16[4,256,3,128]{3,0,2,1:T(4,128)(2,1)} %copy.65), calls=%async_computation.1 | async-start | bytes 1572864 | tf_op jit(solution)/shard_map/all_to_all | solution.py:63
  131.9 23.9 %all-to-all-start = ((bf16[4,256,3,128]{3,0,2,1:T(4,128)(2,1)}), bf16[4,256,3,128]{3,0,2,1:T(4,128)(2,1)S(1)}, u32[]{:S(2)}, u32[]{:S(2)}) async-start(bf16[4,256,3,128]{3,0,2,1:T(4,128)(2,1)} %copy.62), calls=%async_computation | async-start | bytes 1572864 | tf_op jit(solution)/shard_map/all_to_all | solution.py:65
  141.3 15.3 %copy-start.1 = (bf16[8,4,32,3,128]{4,1,0,3,2:T(4,128)(2,1)}, bf16[8,4,32,3,128]{4,1,0,3,2:T(4,128)(2,1)S(1)}, u32[]{:S(2)}) copy-start(bf16[8,4,32,3,128]{4,1,0,3,2:T(4,128)(2,1)S(1)} %copy.70) | copy-start | bytes 2359300
  143.5 15.0 %copy-start.2 = (bf16[8,4,32,3,128]{4,1,0,3,2:T(4,128)(2,1)}, bf16[8,4,32,3,128]{4,1,0,3,2:T(4,128)(2,1)S(1)}, u32[]{:S(2)}) copy-start(bf16[8,4,32,3,128]{4,1,0,3,2:T(4,128)(2,1)S(1)} %copy.67) | copy-start | bytes 2359300
  158.5 6.8 %copy-start = (bf16[4,256,1,3,3,128]{5,1,4,0,3,2:T(8,128)(2,1)S(1)}, bf16[4,256,1,3,3,128]{5,1,4,0,3,2:T(8,128)(2,1)}, u32[]{:S(2)}) copy-start(bf16[4,256,1,3,3,128]{5,1,4,0,3,2:T(8,128)(2,1)} %copy.78) | copy-start | bytes 7077892
  161.7 34.9 %all-to-all-start.3 = ((bf16[32,32,3,128]{3,1,2,0:T(8,128)(2,1)}), bf16[32,32,3,128]{3,1,2,0:T(8,128)(2,1)S(1)}, u32[]{:S(2)}, u32[]{:S(2)}) async-start(bf16[32,32,3,128]{3,1,2,0:T(8,128)(2,1)} %copy.72), calls=%async_computation.3 | async-start | bytes 1572864 | tf_op jit(solution)/shard_map/all_to_all | solution.py:44
where the time goes:
time: 200 us; the launch traced here: 199 us
  local copies, waits for them, and re-layouts  76.8 us (38%)
  waiting for transfers between devices  48.6 us (24%)
  matrix products  28.6 us (14%)
  blocking collectives  21.9 us (11%)
  starting transfers between devices  18.7 us (9%)
  other arithmetic  3 us (2%)
    unnamed x9, local copies, waits for them, and re-layouts  41.1 us
    pmax x1, blocking collectives, time_section(): highest = lax.pmax(highest, 'seq')  21.9 us
    dot_general x1, matrix products, body(): jnp.dot(token_rows, projection.reshape(width, -1), preferred_element_type...  20.7 us
    all_to_all x1, waiting for transfers between devices, time_section(): lax.all_to_all(triple[0], 'seq', split_axis=1, concat_axis=0, tiled=True)  18.4 us
    all_to_all x1, waiting for transfers between devices, time_section(): lax.all_to_all(triple[1], 'seq', split_axis=1, concat_axis=0, tiled=True)  17.9 us
    all_to_all x1, waiting for transfers between devices, time_section(): lax.all_to_all(triple[2], 'seq', split_axis=1, concat_axis=0, tiled=True)  12.3 us
    reshape x1, local copies, waits for them, and re-layouts, body(): parts.astype(jnp.bfloat16)  8.93 us
    squeeze x4, local copies, waits for them, and re-layouts, time_section(): triple = (time_parts[:, :, 0], time_parts[:, :, 1], time_parts[:, :, 2])  8.25 us
  transfers between devices with their start and end apart: 4, of which 3 were waited for; matrix products, arithmetic and copies ran while one was open for 11% of the time, Pallas kernels for 0%

commit v1 on v0

v1 whole, which is shorter than its diff:
```python
import math

import jax
import jax.numpy as jnp
from jax import lax
from jax.experimental import pallas as pl
from jax.experimental.pallas import tpu as pltpu
from jax.sharding import PartitionSpec as P

HD = 128
ROLES = 3
clip_limit = 30.0
score_scale = 1.0 / math.sqrt(HD)
exp_scale = score_scale * math.log2(math.e)
VMEM = pl.BlockSpec(memory_space=pltpu.VMEM)
PARAMS = pltpu.CompilerParams(vmem_limit_bytes=48 * 1024 * 1024)


def dot_nt(a, b):
    return lax.dot_general(a, b, (((1,), (1,)), ((), ())), preferred_element_type=jnp.float32)


def attend(query_part, key_part, value_part, mask=None):
    raw = dot_nt(query_part, key_part)
    if mask is not None:
        raw = jnp.where(mask, raw, -jnp.inf)
    highest = jnp.max(raw, axis=-1, keepdims=True)
    expon = jnp.exp2((raw - highest) * exp_scale)
    weights = (expon * (1.0 / jnp.sum(expon, axis=-1, keepdims=True))).astype(jnp.bfloat16)
    result = jnp.dot(weights, value_part, preferred_element_type=jnp.float32)
    return result, jnp.max(highest, axis=0, keepdims=True)


def space_kernel(heads, x_ref, w_ref, out_ref, peak_ref):
    frame = pl.program_id(0)
    parts = jnp.dot(x_ref[0], w_ref[...], preferred_element_type=jnp.float32).astype(jnp.bfloat16)
    width = heads * HD

    @pl.when(frame == 0)
    def _():
        peak_ref[...] = jnp.full(peak_ref.shape, -jnp.inf, jnp.float32)

    for h in range(heads):
        cols = [parts[:, r * width + h * HD : r * width + (h + 1) * HD] for r in range(ROLES)]
        result, highest = attend(*cols)
        out_ref[0, :, h * HD : (h + 1) * HD] = result.astype(jnp.bfloat16)
        cell = peak_ref.at[:, h * HD : (h + 1) * HD]
        cell[...] = jnp.maximum(cell[...], highest * score_scale)


def space_attention(tokens, weights, heads):
    frames, positions, depth = tokens.shape
    cols = weights.shape[1]
    width = heads * HD
    return pl.pallas_call(
        lambda *refs: space_kernel(heads, *refs),
        grid=(frames,),
        in_specs=[
            pl.BlockSpec((1, positions, depth), lambda f: (f, 0, 0)),
            pl.BlockSpec((depth, cols), lambda f: (0, 0)),
        ],
        out_specs=(
            pl.BlockSpec((1, positions, width), lambda f: (f, 0, 0)),
            pl.BlockSpec((8, width), lambda f: (0, 0)),
        ),
        out_shape=(
            jax.ShapeDtypeStruct((frames, positions, width), jnp.bfloat16),
            jax.ShapeDtypeStruct((8, width), jnp.float32),
        ),
        compiler_params=PARAMS,
        cost_estimate=pl.CostEstimate(
            flops=2 * frames * positions * depth * cols,
            bytes_accessed=2 * (frames * positions * depth + depth * cols),
            transcendentals=frames * heads * positions * positions,
        ),
        name="space_attention",
    )(tokens, weights)


def project_kernel(blocks, rows, x0, x1, x2, x3, w_ref, out_ref):
    groups = rows // 8
    for pair, (one, two) in enumerate(((x0, x1), (x2, x3))):
        both = [
            jnp.dot(x[...].reshape(blocks * rows, x.shape[-1]), w_ref[...], preferred_element_type=jnp.float32)
            for x in (one, two)
        ]
        for b in range(blocks):
            for g in range(groups):
                at = b * rows + g * 8
                tile = jnp.concatenate([y[at : at + 8] for y in both], axis=0)
                start = (pair * blocks + b) * 16
                out_ref[g, start : start + 16, :] = tile.astype(jnp.bfloat16)


def project(sources, weights):
    blocks, rows, depth = sources[0].shape
    cols = weights.shape[1]
    step = cols // ROLES
    whole = pl.BlockSpec((blocks, rows, depth), lambda c: (0, 0, 0))
    groups = rows // 8
    return pl.pallas_call(
        lambda *refs: project_kernel(blocks, rows, *refs),
        grid=(ROLES,),
        in_specs=[whole] * 4 + [pl.BlockSpec((depth, step), lambda c: (1, c))],
        out_specs=pl.BlockSpec((groups, blocks * 32, step), lambda c: (0, 0, c)),
        out_shape=jax.ShapeDtypeStruct((groups, blocks * 32, cols), jnp.bfloat16),
        compiler_params=PARAMS,
        cost_estimate=pl.CostEstimate(
            flops=8 * blocks * rows * depth * cols,
            bytes_accessed=2 * (4 * blocks * rows * depth + depth * cols),
            transcendentals=0,
        ),
        name="project",
    )(*sources, weights)


def pieces(value):
    high = value.astype(jnp.bfloat16).astype(jnp.float32)
    mid = (value - high).astype(jnp.bfloat16).astype(jnp.float32)
    return high, mid, value - high - mid


def time_kernel(heads, sizes, *refs):
    ins, space_peak, outs = refs[: len(sizes)], refs[len(sizes)], refs[len(sizes) + 1 :]
    groups = ins[0].shape[0]
    width = heads * HD
    total = sum(sizes) * 32
    row = lax.broadcasted_iota(jnp.int32, (total, total), 0)
    col = lax.broadcasted_iota(jnp.int32, (total, total), 1)
    mask = ((row ^ col) & 7) == 0
    line = lax.broadcasted_iota(jnp.int32, (16, HD), 0)
    for h in range(heads):
        peak = jnp.full((1, 1), -jnp.inf, jnp.float32)
        for g in range(groups):
            cols = []
            for r in range(ROLES):
                at = r * width + h * HD
                cols.append(jnp.concatenate([x[g, :, at : at + HD] for x in ins], axis=0))
            result, highest = attend(*cols, mask)
            peak = jnp.maximum(peak, highest * score_scale)
            result = result.astype(jnp.bfloat16)
            base, which = 0, 0
            for size in sizes:
                for b in range(size):
                    for pair in range(2):
                        at = base + (pair * size + b) * 16
                        spot = g * 32 + pair * 16
                        outs[which + b][spot : spot + 16, h * HD : (h + 1) * HD] = result[at : at + 16]
                base += size * 32
                which += size
        tail = jnp.zeros((16, HD), jnp.float32)
        mine = space_peak[0:1, h * HD : (h + 1) * HD]
        for i, value in enumerate(pieces(mine) + pieces(jnp.broadcast_to(peak, (1, HD)))):
            tail = jnp.where(line == i, value, tail)
        for out in outs:
            out[groups * 32 : groups * 32 + 16, h * HD : (h + 1) * HD] = tail.astype(jnp.bfloat16)


def time_attention(parts, space_peak, heads):
    sizes = [p.shape[1] // 32 for p in parts]
    groups = parts[0].shape[0]
    width = heads * HD
    total = sum(sizes) * 32
    shape = jax.ShapeDtypeStruct((groups * 32 + 16, width), jnp.bfloat16)
    return pl.pallas_call(
        lambda *refs: time_kernel(heads, sizes, *refs),
        in_specs=[VMEM] * (len(parts) + 1),
        out_specs=[VMEM] * sum(sizes),
        out_shape=[shape] * sum(sizes),
        compiler_params=PARAMS,
        cost_estimate=pl.CostEstimate(
            flops=4 * groups * heads * total * total * HD,
            bytes_accessed=8 * groups * total * width,
            transcendentals=groups * heads * total * total,
        ),
        name="time_attention",
    )(*parts, space_peak)


def finish_kernel(frames_of, heads, index_ref, *refs):
    ins, out_ref, clip_ref = refs[:-2], refs[-2], refs[-1]
    groups = (ins[0].shape[0] - 16) // 32
    me, mine = index_ref[0], index_ref[1]
    peak = None
    for d, source in enumerate(ins):
        for two in range(groups // 2):
            for pair in range(2):
                a, b = (
                    source[(2 * two + k) * 32 + pair * 16 : (2 * two + k) * 32 + pair * 16 + 16, :].astype(jnp.float32)
                    for k in range(2)
                )
                for k in range(2):
                    tile = jnp.concatenate([a[8 * k : 8 * k + 8], b[8 * k : 8 * k + 8]], axis=0)
                    frame = mine ^ frames_of[2 * pair + k]
                    start = pl.multiple_of((me ^ d) * (groups * 8) + two * 16, 16)
                    out_ref[frame, pl.ds(start, 16), :] = tile.astype(jnp.bfloat16)
        tail = source[groups * 32 : groups * 32 + 16, :].astype(jnp.float32)
        values = [tail[3 * a : 3 * a + 1] + tail[3 * a + 1 : 3 * a + 2] + tail[3 * a + 2 : 3 * a + 3] for a in range(2)]
        peak = values if peak is None else [jnp.maximum(p, v) for p, v in zip(peak, values)]
    for a in range(2):
        clip_ref[a : a + 1, :] = jnp.sqrt(clip_limit / jnp.maximum(peak[a], clip_limit))


def finish(index, received, frames, positions, width, frames_of, heads):
    return pl.pallas_call(
        lambda *refs: finish_kernel(frames_of, heads, *refs),
        in_specs=[pl.BlockSpec(memory_space=pltpu.SMEM)] + [VMEM] * len(received),
        out_specs=[VMEM, VMEM],
        out_shape=[
            jax.ShapeDtypeStruct((frames, positions, width), jnp.bfloat16),
            jax.ShapeDtypeStruct((2, width), jnp.float32),
        ],
        compiler_params=PARAMS,
        name="finish",
    )(index, *received)


def swap(value, axis, size, distance):
    return lax.ppermute(value, axis, [(i, i ^ distance) for i in range(size)])


def fast_body(seq, head, patch_tokens, projection):
    frames, positions, depth = patch_tokens.shape
    heads = projection.shape[-1] // HD
    width = heads * HD
    rows = positions // seq
    me, mine = lax.axis_index("seq"), lax.axis_index("head")
    frames_of = (0, 2, 1, 3)

    def piece(frame, owner):
        return lax.dynamic_slice(patch_tokens, (frame, owner * rows, 0), (1, rows, depth))

    got = {d: swap(piece(mine, me ^ d), "seq", seq, d) for d in (4, 5, 6, 7, 2, 3, 1)}
    weights = jnp.transpose(projection, (1, 0, 2, 3)).reshape(2 * depth, ROLES * width)

    own = [piece(mine ^ f, me) for f in frames_of]
    space_out, space_peak = space_attention(patch_tokens, weights, heads)
    parts = [project(own, weights)]
    order = [0]
    for group in ((1, 2, 3), (4, 5, 6, 7)):
        here = jnp.concatenate([got[d] for d in group], axis=0)
        there = swap(here, "head", head, 2)
        sources = (here, there, swap(here, "head", head, 1), swap(there, "head", head, 1))
        parts.append(project(sources, weights))
        order += list(group)
    outs = time_attention(parts, space_peak, heads)
    received = [out if d == 0 else swap(out, "seq", seq, d) for d, out in zip(order, outs)]
    index = jnp.stack([me, mine]).astype(jnp.int32)
    time_out, clip = finish(index, received, frames, positions, width, frames_of, heads)
    return space_out, time_out, clip[:, ::HD]


def mixing(scores):
    highest = jnp.max(scores, axis=-1, keepdims=True)
    expon = jnp.exp(scores - highest)
    return (expon / jnp.sum(expon, axis=-1, keepdims=True)).astype(jnp.bfloat16)


def plain_attention(form, query_part, key_part, value_part):
    scores = jnp.einsum(form[0], query_part, key_part, preferred_element_type=jnp.float32) * score_scale
    result = jnp.einsum(form[1], mixing(scores), value_part, preferred_element_type=jnp.float32)
    return result.astype(jnp.bfloat16), jnp.max(scores, axis=(0, 2, 3))


def plain_body(patch_tokens, projection):
    frames, positions, depth = patch_tokens.shape
    heads = projection.shape[-1] // HD
    parts = jnp.dot(
        patch_tokens.reshape(-1, depth), projection.reshape(depth, -1), preferred_element_type=jnp.float32
    )
    parts = parts.astype(jnp.bfloat16).reshape(frames, positions, 2, ROLES, heads, HD)
    space_out, space_high = plain_attention(
        ("fihd,fjhd->fhij", "fhij,fjhd->fihd"), *(parts[:, :, 0, r] for r in range(ROLES))
    )
    moved = [lax.all_to_all(parts[:, :, 1, r], "seq", split_axis=1, concat_axis=0, tiled=True) for r in range(ROLES)]
    time_out, time_high = plain_attention(("fphd,gphd->phfg", "phfg,gphd->fphd"), *moved)
    time_out = lax.all_to_all(time_out, "seq", split_axis=0, concat_axis=1, tiled=True)
    peak = lax.pmax(jnp.stack([space_high, time_high]), "seq")
    clip_factor = jnp.sqrt(clip_limit / jnp.maximum(peak, clip_limit))
    flat = (frames, positions, heads * HD)
    return space_out.reshape(flat), time_out.reshape(flat), clip_factor


def solution(mesh):
    seq, head = mesh.shape["seq"], mesh.shape["head"]

    def body(patch_tokens, projection):
        frames, positions, _ = patch_tokens.shape
        if seq == 8 and head == 4 and frames == 4 and positions % (16 * seq) == 0:
            return fast_body(seq, head, patch_tokens, projection)
        return plain_body(patch_tokens, projection)

    return jax.shard_map(
        body,
        mesh=mesh,
        in_specs=(P("seq", None, None), P(None, None, None, "head")),
        out_specs=(P("seq", None, "head"), P("seq", None, "head"), P(None, "head")),
        check_vma=False,
    )
```

time: 200 us -> 142 us (0.71)
  local copies, waits for them, and re-layouts: 76.8 us -> 34.5 us
  Pallas kernels: 0 us -> 40.2 us
  matrix products: 28.6 us -> 0 us
  blocking collectives: 21.9 us -> 0 us
  waiting for transfers between devices: 48.6 us -> 37.7 us
  starting transfers between devices: 18.7 us -> 27.3 us
  other arithmetic: 3 us -> 0.07 us
    all_to_all x4 -> x0, waiting for transfers between devices: 48.6 us -> none  [the longest x1 18.4 us: time_section(): lax.all_to_all(triple[0], 'seq', split_axis=1, concat_axis=0, tiled=True)]
    pallas_call x0 -> x6, Pallas kernels: none -> 40.2 us  [the longest x3 20.5 us: project(): pl.pallas_call(lambda *refs: project_kernel(blocks, rows, *refs), grid=(R...]
    ppermute x0 -> x20, waiting for transfers between devices: none -> 37.7 us  [swap(): return lax.ppermute(value, axis, [(i, i ^ distance) for i in range(size)])]
    ppermute x0 -> x20, starting transfers between devices: none -> 27.3 us  [swap(): return lax.ppermute(value, axis, [(i, i ^ distance) for i in range(size)])]
    dot_general x5 -> x0, matrix products: 26.7 us -> none  [the longest x1 20.7 us: body(): jnp.dot(token_rows, projection.reshape(width, -1), preferred_element_type...]
    unnamed x9 -> x6, local copies, waits for them, and re-layouts: 41.1 us -> 17 us
    pmax x1 -> x0, blocking collectives: 21.9 us -> none  [time_section(): highest = lax.pmax(highest, 'seq')]
    all_to_all x4 -> x0, starting transfers between devices: 18.7 us -> none  [the longest x1 7.25 us: time_section(): lax.all_to_all(triple[1], 'seq', split_axis=1, concat_axis=0, tiled=True)]
  transfers between devices with their start and end apart: 4 -> 20, of which waited for: 3 -> 4; matrix products, arithmetic and copies ran while one was open for 11% -> 23% of each run, Pallas kernels for 0% -> 21%
where the time goes in v1:
time: 142 us; the launch traced here: 141 us
  Pallas kernels  40.2 us (28%)
  waiting for transfers between devices  37.7 us (27%)
  local copies, waits for them, and re-layouts  34.5 us (24%)
  starting transfers between devices  27.3 us (19%)
    ppermute x20, waiting for transfers between devices, swap(): return lax.ppermute(value, axis, [(i, i ^ distance) for i in range(size)])  37.7 us
    ppermute x20, starting transfers between devices, swap(): return lax.ppermute(value, axis, [(i, i ^ distance) for i in range(size)])  27.3 us
    pallas_call x3, Pallas kernels, project(): pl.pallas_call(lambda *refs: project_kernel(blocks, rows, *refs), grid=(R...  20.5 us
    unnamed x6, local copies, waits for them, and re-layouts  17 us
    pallas_call x1, Pallas kernels, space_attention(): pl.pallas_call(lambda *refs: space_kernel(heads, *refs), grid=(frames,),...  16.1 us
    reshape x1, local copies, waits for them, and re-layouts, fast_body(): jnp.transpose(projection, (1, 0, 2, 3)).reshape(2 * depth, ROLES * width)  15 us
  transfers between devices with their start and end apart: 20, of which 4 were waited for; matrix products, arithmetic and copies ran while one was open for 23% of the time, Pallas kernels for 21%

profile of v1, /device:TPU:0, one launch (start us, length us, event | category | flops | bytes accessed | tf_op | source)
XLA Modules:
  0.0 140.6 jit_solution(8550212334975933161)
XLA Ops:
  0.7 1.8 %constant_dynamic-slice_fusion = (bf16[1,32,3072]{2,1,0:T(8,128)(2,1)S(1)}, bf16[1,32,3072]{2,1,0:T(8,128)(2,1)S(1)}, bf16[1,32,3072]{2,1,0:T(8,128)(2,1)S(1)}, ...) fusion(bf16[4,256,3072]{2,1,0:T(8,128)(2,1)} %refs_0_.1, ...), kind=kLoop, calls=%fused_computation.7 | loop fusion | bytes 4325424 | tf_op jit(solution)/shard_map/dynamic_slice | solution.py:231
  2.5 4.1 %collective-permute-start.6 = (bf16[1,32,3072]{2,1,0:T(8,128)(2,1)S(1)}, bf16[1,32,3072]{2,1,0:T(8,128)(2,1)S(1)}, u32[]{:S(2)}, u32[]{:S(2)}) collective-permute-start(bf16[1,32,3072]{2,1,0:T(8,128)(2,1)S(1)} %get-tuple-element.29), channel_id=1, source_target_pairs={{0,16},{4,20},{8,24},{12,28},{16,0},{20,4},{24,8},{28,12},{1,17},{... | collective-permute-start | bytes 589832 | tf_op jit(solution)/shard_map/ppermute | solution.py:219
  6.6 1.5 %collective-permute-start = (bf16[1,32,3072]{2,1,0:T(8,128)(2,1)S(1)}, bf16[1,32,3072]{2,1,0:T(8,128)(2,1)S(1)}, u32[]{:S(2)}, u32[]{:S(2)}) collective-permute-start(bf16[1,32,3072]{2,1,0:T(8,128)(2,1)S(1)} %get-tuple-element.32), channel_id=1, source_target_pairs={{0,4},{4,0},{8,12},{12,8},{16,20},{20,16},{24,28},{28,24},{1,5},{5... | collective-permute-start | bytes 589832 | tf_op jit(solution)/shard_map/ppermute | solution.py:219
  8.1 1.6 %collective-permute-start.1 = (bf16[1,32,3072]{2,1,0:T(8,128)(2,1)S(1)}, bf16[1,32,3072]{2,1,0:T(8,128)(2,1)S(1)}, u32[]{:S(2)}, u32[]{:S(2)}) collective-permute-start(bf16[1,32,3072]{2,1,0:T(8,128)(2,1)S(1)} %get-tuple-element.31), channel_id=1, source_target_pairs={{0,8},{4,12},{8,0},{12,4},{16,24},{20,28},{24,16},{28,20},{1,9},{5... | collective-permute-start | bytes 589832 | tf_op jit(solution)/shard_map/ppermute | solution.py:219
  9.7 0.4 collective-permute-start.2
  10.1 1.3 collective-permute-start.7
  11.4 5.3 %collective-permute-done.6 = bf16[1,32,3072]{2,1,0:T(8,128)(2,1)S(1)} collective-permute-done((bf16[1,32,3072]{2,1,0:T(8,128)(2,1)S(1)}, bf16[1,32,3072]{2,1,0:T(8,128)(2,1)S(1)}, u32[]{:S(2)}, u32[]{:S(2)}) %collective-permute-start.6) | collective-permute-done | bytes 196640 | tf_op jit(solution)/shard_map/ppermute | solution.py:219
  16.7 2.8 %collective-permute-start.8 = (bf16[1,32,3072]{2,1,0:T(8,128)(2,1)S(1)}, bf16[1,32,3072]{2,1,0:T(8,128)(2,1)S(1)}, u32[]{:S(2)}, u32[]{:S(2)}) collective-permute-start(bf16[1,32,3072]{2,1,0:T(8,128)(2,1)S(1)} %get-tuple-element.37), channel_id=1, source_target_pairs={{0,24},{4,28},{8,16},{12,20},{16,8},{20,12},{24,0},{28,4},{1,25},{... | collective-permute-start | bytes 589832 | tf_op jit(solution)/shard_map/ppermute | solution.py:219
  19.5 13.1 %collective-permute-done.7 = bf16[1,32,3072]{2,1,0:T(8,128)(2,1)S(1)} collective-permute-done((bf16[1,32,3072]{2,1,0:T(8,128)(2,1)S(1)}, bf16[1,32,3072]{2,1,0:T(8,128)(2,1)S(1)}, u32[]{:S(2)}, u32[]{:S(2)}) %collective-permute-start.7) | collective-permute-done | bytes 196640 | tf_op jit(solution)/shard_map/ppermute | solution.py:219
  32.7 8.4 %collective-permute-done.9 = bf16[1,32,3072]{2,1,0:T(8,128)(2,1)S(1)} collective-permute-done((bf16[1,32,3072]{2,1,0:T(8,128)(2,1)S(1)}, bf16[1,32,3072]{2,1,0:T(8,128)(2,1)S(1)}, u32[]{:S(2)}, u32[]{:S(2)}) %collective-permute-start.9) | collective-permute-done | bytes 196640 | tf_op jit(solution)/shard_map/ppermute | solution.py:219
  41.1 1.6 %collective-permute-start.10 = (bf16[4,32,3072]{2,1,0:T(8,128)(2,1)S(1)}, bf16[4,32,3072]{2,1,0:T(8,128)(2,1)S(1)}, u32[]{:S(2)}, u32[]{:S(2)}) collective-permute-start(bf16[4,32,3072]{2,1,0:T(8,128)(2,1)S(1)} %constant_dynamic-update-slice_fusion.3.refs_0_), channel_id=1, source_target_pairs={{0,2},{1,3},{2,0},{3,1},{4,6},{5,7},{6,4},{7,5},{8,10},{9,11},{10,... | collective-permute-start | bytes 2359304 | tf_op jit(solution)/shard_map/ppermute | solution.py:219
  42.8 0.6 collective-permute-start.3
  43.4 15.0 %copy.11 = bf16[2,3072,3,384]{3,2,1,0:T(4,128)(2,1)} copy(bf16[2,3072,3,384]{3,0,2,1:T(2,128)(2,1)} %bitcast.11) | data formatting | bytes 28311552 | tf_op jit(solution)/shard_map/reshape | solution.py:234
  58.4 16.9 %copy.13 = bf16[768,8,3,384]{3,1,2,0:T(8,128)(2,1)} copy(bf16[768,8,3,384]{3,2,1,0:T(4,128)(2,1)} %bitcast.10) | data formatting | bytes 28311552
  75.3 6.3 %project.3.refs_0_ = bf16[4,32,1152]{2,1,0:T(8,128)(2,1)S(1)} custom-call(bf16[1,32,3072]{2,1,0:T(8,128)(2,1)S(1)} %get-tuple-element.36.refs_0_, bf16[1,32,3072]{2,1,0:T(8,128)(2,1)S(1)} %get-tuple-element.35.refs_1_, bf16[1,32,3072]{2,1,0:T(8,128)(2,1)S(1)} %get-tuple-element.34.refs_2_, bf16[1,32,3072]{2,1,0:T(8,128)(2,1)S(1)} %get-tuple-element.33.refs_3_, ...), custom_call_target="tpu_custom_call" | custom-call | flops 905969664 | bytes 7864320 | tf_op jit(solution)/shard_map/project/pallas_call | solution.py:101
  81.7 0.5 collective-permute-start.11
  82.2 0.1 collective-permute-start.5
  82.3 0.4 collective-permute-start.12
  82.7 16.1 %space_attention.1 = (bf16[4,256,384]{2,1,0:T(8,128)(2,1)}, f32[8,384]{1,0:T(8,128)S(1)}) custom-call(bf16[4,256,3072]{2,1,0:T(8,128)(2,1)} %refs_0_.1, bf16[6144,1152]{1,0:T(8,128)(2,1)} %bitcast.7), custom_call_target="tpu_custom_call" | custom-call | flops 7247757312 | bytes 13369344 | tf_op jit(solution)/shard_map/space_attention/pallas_call | solution.py:55
  98.8 6.9 %project.4.refs_1_ = bf16[4,96,1152]{2,1,0:T(8,128)(2,1)S(1)} custom-call(bf16[3,32,3072]{2,1,0:T(8,128)(2,1)S(1)} %constant_dynamic-update-slice_fusion.refs_0_, bf16[3,32,3072]{2,1,0:T(8,128)(2,1)S(1)} %collective-permute-done.3.refs_1_, bf16[3,32,3072]{2,1,0:T(8,128)(2,1)S(1)} %collective-permute-done.4.refs_2_, ...), custom_call_target="tpu_custom_call" | custom-call | flops 2717908992 | bytes 9437184 | tf_op jit(solution)/shard_map/project/pallas_call | solution.py:101
  105.7 7.3 %project.5.refs_2_ = bf16[4,128,1152]{2,1,0:T(8,128)(2,1)S(1)} custom-call(bf16[4,32,3072]{2,1,0:T(8,128)(2,1)S(1)} %constant_dynamic-update-slice_fusion.3.refs_0_, bf16[4,32,3072]{2,1,0:T(8,128)(2,1)S(1)} %collective-permute-done.10.refs_1_, bf16[4,32,3072]{2,1,0:T(8,128)(2,1)S(1)} %collective-permute-done.11.refs_2_, ...), custom_call_target="tpu_custom_call" | custom-call | flops 3623878656 | bytes 10223616 | tf_op jit(solution)/shard_map/project/pallas_call | solution.py:101
  113.0 2.1 %time_attention.1 = (bf16[144,384]{1,0:T(8,128)(2,1)S(1)}, bf16[144,384]{1,0:T(8,128)(2,1)S(1)}, bf16[144,384]{1,0:T(8,128)(2,1)S(1)}, bf16[144,384]{1,0:T(8,128...) custom-call(bf16[4,32,1152]{2,1,0:T(8,128)(2,1)S(1)} %project.3.refs, ...), custom_call_target="tpu_custom_call" | custom-call | flops 402653184 | bytes 3145728 | tf_op jit(solution)/shard_map/time_attention/pallas_call | solution.py:165
  115.1 0.2 collective-permute-start.13
  115.3 2.0 %collective-permute-start.14 = (bf16[144,384]{1,0:T(8,128)(2,1)S(1)}, bf16[144,384]{1,0:T(8,128)(2,1)S(1)}, u32[]{:S(2)}, u32[]{:S(2)}) collective-permute-start(bf16[144,384]{1,0:T(8,128)(2,1)S(1)} %get-tuple-element.19), channel_id=1, source_target_pairs={{0,8},{4,12},{8,0},{12,4},{16,24},{20,28},{24,16},{28,20},{1,9},{5... | collective-permute-start | bytes 331784 | tf_op jit(solution)/shard_map/ppermute | solution.py:219
  117.3 1.3 collective-permute-start.15
  118.6 3.5 %collective-permute-start.16 = (bf16[144,384]{1,0:T(8,128)(2,1)S(1)}, bf16[144,384]{1,0:T(8,128)(2,1)S(1)}, u32[]{:S(2)}, u32[]{:S(2)}) collective-permute-start(bf16[144,384]{1,0:T(8,128)(2,1)S(1)} %get-tuple-element.21), channel_id=1, source_target_pairs={{0,16},{4,20},{8,24},{12,28},{16,0},{20,4},{24,8},{28,12},{1,17},{... | collective-permute-start | bytes 331784 | tf_op jit(solution)/shard_map/ppermute | solution.py:219
  122.2 2.4 %collective-permute-start.18 = (bf16[144,384]{1,0:T(8,128)(2,1)S(1)}, bf16[144,384]{1,0:T(8,128)(2,1)S(1)}, u32[]{:S(2)}, u32[]{:S(2)}) collective-permute-start(bf16[144,384]{1,0:T(8,128)(2,1)S(1)} %get-tuple-element.23), channel_id=1, source_target_pairs={{0,24},{4,28},{8,16},{12,20},{16,8},{20,12},{24,0},{28,4},{1,25},{... | collective-permute-start | bytes 331784 | tf_op jit(solution)/shard_map/ppermute | solution.py:219
  124.5 3.0 %collective-permute-start.19 = (bf16[144,384]{1,0:T(8,128)(2,1)S(1)}, bf16[144,384]{1,0:T(8,128)(2,1)S(1)}, u32[]{:S(2)}, u32[]{:S(2)}) collective-permute-start(bf16[144,384]{1,0:T(8,128)(2,1)S(1)} %get-tuple-element.24), channel_id=1, source_target_pairs={{0,28},{4,24},{8,20},{12,16},{16,12},{20,8},{24,4},{28,0},{1,29},{... | collective-permute-start | bytes 331784 | tf_op jit(solution)/shard_map/ppermute | solution.py:219
  127.5 0.1 pad_add_fusion.refs_0_
  127.6 10.9 %collective-permute-done.17.refs_6_ = bf16[144,384]{1,0:T(8,128)(2,1)S(1)} collective-permute-done((bf16[144,384]{1,0:T(8,128)(2,1)S(1)}, bf16[144,384]{1,0:T(8,128)(2,1)S(1)}, u32[]{:S(2)}, u32[]{:S(2)}) %collective-permute-start.17) | collective-permute-done | bytes 110624 | tf_op jit(solution)/shard_map/ppermute | solution.py:219
  138.4 1.5 %finish.1 = (bf16[4,256,384]{2,1,0:T(8,128)(2,1)}, f32[2,384]{1,0:T(2,128)S(1)}) custom-call(s32[2]{0:T(128)S(1)} %pad_add_fusion.refs_0_, bf16[144,384]{1,0:T(8,128)(2,1)S(1)} %get-tuple-element.17.refs_1_, bf16[144,384]{1,0:T(8,128)(2,1)S(1)} %collective-permute-done.13.refs_2_, bf16[144,384]{1,0:T(8,128)(2,1)S(1)} %collective-permute-done.14.refs_3_, ...), custom_call_target="tpu_custom_call" | custom-call | tf_op jit(solution)/shard_map/finish/pallas_call | solution.py:205
  140.0 0.6 slice.3
  (26 shorter events, 0.2 us)
Async XLA Ops:
  2.5 14.1 %collective-permute-start.6 = (bf16[1,32,3072]{2,1,0:T(8,128)(2,1)S(1)}, bf16[1,32,3072]{2,1,0:T(8,128)(2,1)S(1)}, u32[]{:S(2)}, u32[]{:S(2)}) collective-permute-start(bf16[1,32,3072]{2,1,0:T(8,128)(2,1)S(1)} %get-tuple-element.29), channel_id=1, source_target_pairs={{0,16},{4,20},{8,24},{12,28},{16,0},{20,4},{24,8},{28,12},{1,17},{... | collective-permute-start | bytes 589832 | tf_op jit(solution)/shard_map/ppermute | solution.py:219
  6.6 36.1 %collective-permute-start = (bf16[1,32,3072]{2,1,0:T(8,128)(2,1)S(1)}, bf16[1,32,3072]{2,1,0:T(8,128)(2,1)S(1)}, u32[]{:S(2)}, u32[]{:S(2)}) collective-permute-start(bf16[1,32,3072]{2,1,0:T(8,128)(2,1)S(1)} %get-tuple-element.32), channel_id=1, source_target_pairs={{0,4},{4,0},{8,12},{12,8},{16,20},{20,16},{24,28},{28,24},{1,5},{5... | collective-permute-start | bytes 589832 | tf_op jit(solution)/shard_map/ppermute | solution.py:219
  8.1 34.6 %collective-permute-start.1 = (bf16[1,32,3072]{2,1,0:T(8,128)(2,1)S(1)}, bf16[1,32,3072]{2,1,0:T(8,128)(2,1)S(1)}, u32[]{:S(2)}, u32[]{:S(2)}) collective-permute-start(bf16[1,32,3072]{2,1,0:T(8,128)(2,1)S(1)} %get-tuple-element.31), channel_id=1, source_target_pairs={{0,8},{4,12},{8,0},{12,4},{16,24},{20,28},{24,16},{28,20},{1,9},{5... | collective-permute-start | bytes 589832 | tf_op jit(solution)/shard_map/ppermute | solution.py:219
  9.7 33.1 %collective-permute-start.2 = (bf16[1,32,3072]{2,1,0:T(8,128)(2,1)S(1)}, bf16[1,32,3072]{2,1,0:T(8,128)(2,1)S(1)}, u32[]{:S(2)}, u32[]{:S(2)}) collective-permute-start(bf16[1,32,3072]{2,1,0:T(8,128)(2,1)S(1)} %get-tuple-element.30), channel_id=1, source_target_pairs={{0,12},{4,8},{8,4},{12,0},{16,28},{20,24},{24,20},{28,16},{1,13},{... | collective-permute-start | bytes 589832 | tf_op jit(solution)/shard_map/ppermute | solution.py:219
  10.1 22.5 %collective-permute-start.7 = (bf16[1,32,3072]{2,1,0:T(8,128)(2,1)S(1)}, bf16[1,32,3072]{2,1,0:T(8,128)(2,1)S(1)}, u32[]{:S(2)}, u32[]{:S(2)}) collective-permute-start(bf16[1,32,3072]{2,1,0:T(8,128)(2,1)S(1)} %get-tuple-element.28), channel_id=1, source_target_pairs={{0,20},{4,16},{8,28},{12,24},{16,4},{20,0},{24,12},{28,8},{1,21},{... | collective-permute-start | bytes 589832 | tf_op jit(solution)/shard_map/ppermute | solution.py:219
  16.7 16.0 %collective-permute-start.8 = (bf16[1,32,3072]{2,1,0:T(8,128)(2,1)S(1)}, bf16[1,32,3072]{2,1,0:T(8,128)(2,1)S(1)}, u32[]{:S(2)}, u32[]{:S(2)}) collective-permute-start(bf16[1,32,3072]{2,1,0:T(8,128)(2,1)S(1)} %get-tuple-element.37), channel_id=1, source_target_pairs={{0,24},{4,28},{8,16},{12,20},{16,8},{20,12},{24,0},{28,4},{1,25},{... | collective-permute-start | bytes 589832 | tf_op jit(solution)/shard_map/ppermute | solution.py:219
  32.7 8.5 %collective-permute-start.9 = (bf16[1,32,3072]{2,1,0:T(8,128)(2,1)S(1)}, bf16[1,32,3072]{2,1,0:T(8,128)(2,1)S(1)}, u32[]{:S(2)}, u32[]{:S(2)}) collective-permute-start(bf16[1,32,3072]{2,1,0:T(8,128)(2,1)S(1)} %get-tuple-element.27), channel_id=1, source_target_pairs={{0,28},{4,24},{8,20},{12,16},{16,12},{20,8},{24,4},{28,0},{1,29},{... | collective-permute-start | bytes 589832 | tf_op jit(solution)/shard_map/ppermute | solution.py:219
  41.1 41.2 %collective-permute-start.10 = (bf16[4,32,3072]{2,1,0:T(8,128)(2,1)S(1)}, bf16[4,32,3072]{2,1,0:T(8,128)(2,1)S(1)}, u32[]{:S(2)}, u32[]{:S(2)}) collective-permute-start(bf16[4,32,3072]{2,1,0:T(8,128)(2,1)S(1)} %constant_dynamic-update-slice_fusion.3.refs_0_), channel_id=1, source_target_pairs={{0,2},{1,3},{2,0},{3,1},{4,6},{5,7},{6,4},{7,5},{8,10},{9,11},{10,... | collective-permute-start | bytes 2359304 | tf_op jit(solution)/shard_map/ppermute | solution.py:219
  42.8 39.4 %collective-permute-start.3 = (bf16[3,32,3072]{2,1,0:T(8,128)(2,1)S(1)}, bf16[3,32,3072]{2,1,0:T(8,128)(2,1)S(1)}, u32[]{:S(2)}, u32[]{:S(2)}) collective-permute-start(bf16[3,32,3072]{2,1,0:T(8,128)(2,1)S(1)} %constant_dynamic-update-slice_fusion.refs_0_), channel_id=1, source_target_pairs={{0,2},{1,3},{2,0},{3,1},{4,6},{5,7},{6,4},{7,5},{8,10},{9,11},{10,... | collective-permute-start | bytes 1769480 | tf_op jit(solution)/shard_map/ppermute | solution.py:219
  81.6 17.1 %collective-permute-start.4 = (bf16[3,32,3072]{2,1,0:T(8,128)(2,1)S(1)}, bf16[3,32,3072]{2,1,0:T(8,128)(2,1)S(1)}, u32[]{:S(2)}, u32[]{:S(2)}) collective-permute-start(bf16[3,32,3072]{2,1,0:T(8,128)(2,1)S(1)} %constant_dynamic-update-slice_fusion.refs_0_), channel_id=1, source_target_pairs={{0,1},{1,0},{2,3},{3,2},{4,5},{5,4},{6,7},{7,6},{8,9},{9,8},{10,11... | collective-permute-start | bytes 1769480 | tf_op jit(solution)/shard_map/ppermute | solution.py:219
  81.7 24.0 %collective-permute-start.11 = (bf16[4,32,3072]{2,1,0:T(8,128)(2,1)S(1)}, bf16[4,32,3072]{2,1,0:T(8,128)(2,1)S(1)}, u32[]{:S(2)}, u32[]{:S(2)}) collective-permute-start(bf16[4,32,3072]{2,1,0:T(8,128)(2,1)S(1)} %constant_dynamic-update-slice_fusion.3.refs_0_), channel_id=1, source_target_pairs={{0,1},{1,0},{2,3},{3,2},{4,5},{5,4},{6,7},{7,6},{8,9},{9,8},{10,11... | collective-permute-start | bytes 2359304 | tf_op jit(solution)/shard_map/ppermute | solution.py:219
  82.2 16.6 %collective-permute-start.5 = (bf16[3,32,3072]{2,1,0:T(8,128)(2,1)S(1)}, bf16[3,32,3072]{2,1,0:T(8,128)(2,1)S(1)}, u32[]{:S(2)}, u32[]{:S(2)}) collective-permute-start(bf16[3,32,3072]{2,1,0:T(8,128)(2,1)S(1)} %collective-permute-done.3.refs_1_), channel_id=1, source_target_pairs={{0,1},{1,0},{2,3},{3,2},{4,5},{5,4},{6,7},{7,6},{8,9},{9,8},{10,11... | collective-permute-start | bytes 1769480 | tf_op jit(solution)/shard_map/ppermute | solution.py:219
  82.3 23.4 %collective-permute-start.12 = (bf16[4,32,3072]{2,1,0:T(8,128)(2,1)S(1)}, bf16[4,32,3072]{2,1,0:T(8,128)(2,1)S(1)}, u32[]{:S(2)}, u32[]{:S(2)}) collective-permute-start(bf16[4,32,3072]{2,1,0:T(8,128)(2,1)S(1)} %collective-permute-done.10.refs_1_), channel_id=1, source_target_pairs={{0,1},{1,0},{2,3},{3,2},{4,5},{5,4},{6,7},{7,6},{8,9},{9,8},{10,11... | collective-permute-start | bytes 2359304 | tf_op jit(solution)/shard_map/ppermute | solution.py:219
  115.1 7.1 %collective-permute-start.13 = (bf16[144,384]{1,0:T(8,128)(2,1)S(1)}, bf16[144,384]{1,0:T(8,128)(2,1)S(1)}, u32[]{:S(2)}, u32[]{:S(2)}) collective-permute-start(bf16[144,384]{1,0:T(8,128)(2,1)S(1)} %get-tuple-element.18), channel_id=1, source_target_pairs={{0,4},{4,0},{8,12},{12,8},{16,20},{20,16},{24,28},{28,24},{1,5},{5... | collective-permute-start | bytes 331784 | tf_op jit(solution)/shard_map/ppermute | solution.py:219
  115.3 9.2 %collective-permute-start.14 = (bf16[144,384]{1,0:T(8,128)(2,1)S(1)}, bf16[144,384]{1,0:T(8,128)(2,1)S(1)}, u32[]{:S(2)}, u32[]{:S(2)}) collective-permute-start(bf16[144,384]{1,0:T(8,128)(2,1)S(1)} %get-tuple-element.19), channel_id=1, source_target_pairs={{0,8},{4,12},{8,0},{12,4},{16,24},{20,28},{24,16},{28,20},{1,9},{5... | collective-permute-start | bytes 331784 | tf_op jit(solution)/shard_map/ppermute | solution.py:219
  117.3 10.3 %collective-permute-start.15 = (bf16[144,384]{1,0:T(8,128)(2,1)S(1)}, bf16[144,384]{1,0:T(8,128)(2,1)S(1)}, u32[]{:S(2)}, u32[]{:S(2)}) collective-permute-start(bf16[144,384]{1,0:T(8,128)(2,1)S(1)} %get-tuple-element.20), channel_id=1, source_target_pairs={{0,12},{4,8},{8,4},{12,0},{16,28},{20,24},{24,20},{28,16},{1,13},{... | collective-permute-start | bytes 331784 | tf_op jit(solution)/shard_map/ppermute | solution.py:219
  118.6 8.9 %collective-permute-start.16 = (bf16[144,384]{1,0:T(8,128)(2,1)S(1)}, bf16[144,384]{1,0:T(8,128)(2,1)S(1)}, u32[]{:S(2)}, u32[]{:S(2)}) collective-permute-start(bf16[144,384]{1,0:T(8,128)(2,1)S(1)} %get-tuple-element.21), channel_id=1, source_target_pairs={{0,16},{4,20},{8,24},{12,28},{16,0},{20,4},{24,8},{28,12},{1,17},{... | collective-permute-start | bytes 331784 | tf_op jit(solution)/shard_map/ppermute | solution.py:219
  122.2 16.3 %collective-permute-start.17 = (bf16[144,384]{1,0:T(8,128)(2,1)S(1)}, bf16[144,384]{1,0:T(8,128)(2,1)S(1)}, u32[]{:S(2)}, u32[]{:S(2)}) collective-permute-start(bf16[144,384]{1,0:T(8,128)(2,1)S(1)} %get-tuple-element.22), channel_id=1, source_target_pairs={{0,20},{4,16},{8,28},{12,24},{16,4},{20,0},{24,12},{28,8},{1,21},{... | collective-permute-start | bytes 331784 | tf_op jit(solution)/shard_map/ppermute | solution.py:219
  122.2 16.3 %collective-permute-start.18 = (bf16[144,384]{1,0:T(8,128)(2,1)S(1)}, bf16[144,384]{1,0:T(8,128)(2,1)S(1)}, u32[]{:S(2)}, u32[]{:S(2)}) collective-permute-start(bf16[144,384]{1,0:T(8,128)(2,1)S(1)} %get-tuple-element.23), channel_id=1, source_target_pairs={{0,24},{4,28},{8,16},{12,20},{16,8},{20,12},{24,0},{28,4},{1,25},{... | collective-permute-start | bytes 331784 | tf_op jit(solution)/shard_map/ppermute | solution.py:219
  124.5 13.9 %collective-permute-start.19 = (bf16[144,384]{1,0:T(8,128)(2,1)S(1)}, bf16[144,384]{1,0:T(8,128)(2,1)S(1)}, u32[]{:S(2)}, u32[]{:S(2)}) collective-permute-start(bf16[144,384]{1,0:T(8,128)(2,1)S(1)} %get-tuple-element.24), channel_id=1, source_target_pairs={{0,28},{4,24},{8,20},{12,16},{16,12},{20,8},{24,4},{28,0},{1,29},{... | collective-permute-start | bytes 331784 | tf_op jit(solution)/shard_map/ppermute | solution.py:219

commit v2 on v1

v2 whole, which is shorter than its diff:
```python
import math

import jax
import jax.numpy as jnp
from jax import lax
from jax.experimental import pallas as pl
from jax.experimental.pallas import tpu as pltpu
from jax.sharding import PartitionSpec as P

HD = 128
ROLES = 3
clip_limit = 30.0
score_scale = 1.0 / math.sqrt(HD)
exp_scale = score_scale * math.log2(math.e)
VMEM = pl.BlockSpec(memory_space=pltpu.VMEM)
PARAMS = pltpu.CompilerParams(vmem_limit_bytes=48 * 1024 * 1024)


def dot_nt(a, b):
    return lax.dot_general(a, b, (((1,), (1,)), ((), ())), preferred_element_type=jnp.float32)


def attend(query_part, key_part, value_part, mask=None):
    raw = dot_nt(query_part, key_part)
    if mask is not None:
        raw = jnp.where(mask, raw, -jnp.inf)
    highest = jnp.max(raw, axis=-1, keepdims=True)
    expon = jnp.exp2((raw - highest) * exp_scale)
    weights = (expon * (1.0 / jnp.sum(expon, axis=-1, keepdims=True))).astype(jnp.bfloat16)
    result = jnp.dot(weights, value_part, preferred_element_type=jnp.float32)
    return result, jnp.max(highest, axis=0, keepdims=True)


def pick_matrix(which, chunk):
    rows = lax.broadcasted_iota(jnp.int32, (ROLES * chunk, ROLES * 2 * chunk), 0)
    cols = lax.broadcasted_iota(jnp.int32, (ROLES * chunk, ROLES * 2 * chunk), 1)
    source = ((rows % chunk) * ROLES + rows // chunk) * 2 + which
    return jnp.where(cols == source, 1.0, 0.0).astype(jnp.bfloat16)


def pick(pick_ref, w_ref, out_ref):
    depth, _, _, width = w_ref.shape
    chunk = pick_ref.shape[0] // ROLES
    span = 2 * ROLES * chunk
    flat = w_ref.reshape(depth * ROLES * 2, width)
    for i in range(depth // chunk):
        found = jnp.dot(pick_ref[...], flat[i * span : (i + 1) * span, :], preferred_element_type=jnp.float32)
        found = found.astype(jnp.bfloat16)
        for r in range(ROLES):
            out_ref[i * chunk : (i + 1) * chunk, r * width : (r + 1) * width] = found[r * chunk : (r + 1) * chunk]


def pair_rows(one, two, blocks, rows, store):
    for b in range(blocks):
        for g in range(rows // 8):
            at = b * rows + g * 8
            tile = jnp.concatenate([one[at : at + 8], two[at : at + 8]], axis=0)
            store(b, g, tile.astype(jnp.bfloat16))


def early_kernel(count, index_ref, *refs):
    xs, w_ref, weights_ref = refs[:count], refs[count], refs[count + 1]
    outs, (pick_ref, total) = refs[count + 2 : -2], refs[-2:]
    step = pl.program_id(0)

    @pl.when(step == 0)
    def _():
        pick_ref[...] = pick_matrix(1, CHUNK)
        total[...] = jnp.zeros_like(total)

    pick(pick_ref, w_ref, weights_ref)
    frames, rows, block = xs[0].shape
    tokens = jnp.concatenate([x[...].reshape(frames * rows, block) for x in xs], axis=0)
    total[...] += jnp.dot(tokens, weights_ref[...], preferred_element_type=jnp.float32)

    @pl.when(step == pl.num_programs(0) - 1)
    def _():
        for i, out in enumerate(outs):
            for pair in range(frames // 2):
                at = (i * frames + 2 * pair) * rows

                def store(b, g, tile):
                    out[g, pair * 16 : pair * 16 + 16, :] = tile

                pair_rows(total[at : at + rows], total[at + rows : at + 2 * rows], 1, rows, store)


CHUNK = 64


def early(index, tokens, paired, rows, count):
    frames, _, depth = tokens.shape
    width = paired.shape[-1]
    cols = ROLES * width
    block = 512
    out = jax.ShapeDtypeStruct((rows // 8, frames * 8, cols), jnp.bfloat16)
    return pl.pallas_call(
        lambda *refs: early_kernel(count, *refs),
        grid_spec=pltpu.PrefetchScalarGridSpec(
            num_scalar_prefetch=1,
            grid=(depth // block,),
            in_specs=[
                pl.BlockSpec((frames, rows, block), lambda k, index, i=i: (0, index[i], k)) for i in range(count)
            ]
            + [pl.BlockSpec((block, ROLES, 2, width), lambda k, index: (k, 0, 0, 0))],
            out_specs=[pl.BlockSpec((block, cols), lambda k, index: (k, 0))]
            + [pl.BlockSpec(out.shape, lambda k, index: (0, 0, 0))] * count,
            scratch_shapes=[
                pltpu.VMEM((ROLES * CHUNK, 2 * ROLES * CHUNK), jnp.bfloat16),
                pltpu.VMEM((count * frames * rows, cols), jnp.float32),
            ],
        ),
        out_shape=[jax.ShapeDtypeStruct((depth, cols), jnp.bfloat16)] + [out] * count,
        compiler_params=PARAMS,
        cost_estimate=pl.CostEstimate(
            flops=2 * count * frames * rows * depth * cols + 12 * CHUNK * depth * cols,
            bytes_accessed=6 * depth * cols,
            transcendentals=0,
        ),
        name="early",
    )(index, *[tokens] * count, paired)


def space_peak_kernel(heads, x_ref, w_ref, parts_ref, last_ref, peak_ref, pick_ref, weights_ref, total):
    step = pl.program_id(0)
    frames, positions, block = x_ref.shape
    width = heads * HD

    @pl.when(step == 0)
    def _():
        pick_ref[...] = pick_matrix(0, CHUNK)
        total[...] = jnp.zeros_like(total)

    pick(pick_ref, w_ref, weights_ref)
    last_ref[...] = weights_ref[:, 2 * width :]
    tokens = x_ref[...].reshape(frames * positions, block)
    total[...] += jnp.dot(tokens, weights_ref[:, : 2 * width], preferred_element_type=jnp.float32)

    @pl.when(step == pl.num_programs(0) - 1)
    def _():
        parts_ref[...] = total[...].astype(jnp.bfloat16)
        for h in range(heads):
            peak = jnp.full((1, 1), -jnp.inf, jnp.float32)
            for f in range(frames):
                query_part, key_part = (
                    parts_ref[f * positions : (f + 1) * positions, r * width + h * HD : r * width + (h + 1) * HD]
                    for r in range(2)
                )
                peak = jnp.maximum(peak, jnp.max(dot_nt(query_part, key_part), keepdims=True))
            peak_ref[:, h * HD : (h + 1) * HD] = jnp.broadcast_to(peak * score_scale, (8, HD))


def space_peak(tokens, paired, heads):
    frames, positions, depth = tokens.shape
    width = heads * HD
    block = 512
    rows = frames * positions
    return pl.pallas_call(
        lambda *refs: space_peak_kernel(heads, *refs),
        grid=(depth // block,),
        in_specs=[
            pl.BlockSpec((frames, positions, block), lambda k: (0, 0, k)),
            pl.BlockSpec((block, ROLES, 2, width), lambda k: (k, 0, 0, 0)),
        ],
        out_specs=[
            pl.BlockSpec((rows, 2 * width), lambda k: (0, 0)),
            pl.BlockSpec((block, width), lambda k: (k, 0)),
            pl.BlockSpec((8, width), lambda k: (0, 0)),
        ],
        out_shape=[
            jax.ShapeDtypeStruct((rows, 2 * width), jnp.bfloat16),
            jax.ShapeDtypeStruct((depth, width), jnp.bfloat16),
            jax.ShapeDtypeStruct((8, width), jnp.float32),
        ],
        scratch_shapes=[
            pltpu.VMEM((ROLES * CHUNK, 2 * ROLES * CHUNK), jnp.bfloat16),
            pltpu.VMEM((block, ROLES * width), jnp.bfloat16),
            pltpu.VMEM((rows, 2 * width), jnp.float32),
        ],
        compiler_params=PARAMS,
        cost_estimate=pl.CostEstimate(
            flops=4 * rows * depth * width + 12 * CHUNK * depth * ROLES * width,
            bytes_accessed=2 * rows * depth + 14 * depth * width,
            transcendentals=0,
        ),
        name="space_peak",
    )(tokens, paired)


def space_kernel(heads, x_ref, w_ref, parts_ref, out_ref):
    frames, positions, depth = x_ref.shape
    width = heads * HD
    tokens = x_ref[...].reshape(frames * positions, depth)
    values = jnp.dot(tokens, w_ref[...], preferred_element_type=jnp.float32).astype(jnp.bfloat16)
    for f in range(frames):
        rows = slice(f * positions, (f + 1) * positions)
        for h in range(heads):
            cols = [parts_ref[rows, r * width + h * HD : r * width + (h + 1) * HD] for r in range(2)]
            result, _ = attend(*cols, values[rows, h * HD : (h + 1) * HD])
            out_ref[f, :, h * HD : (h + 1) * HD] = result.astype(jnp.bfloat16)


def space_attention(tokens, weights, parts, heads):
    frames, positions, depth = tokens.shape
    width = heads * HD
    block = 2
    return pl.pallas_call(
        lambda *refs: space_kernel(heads, *refs),
        grid=(frames // block,),
        in_specs=[
            pl.BlockSpec((block, positions, depth), lambda f: (f, 0, 0)),
            pl.BlockSpec((depth, width), lambda f: (0, 0)),
            pl.BlockSpec((block * positions, 2 * width), lambda f: (f, 0)),
        ],
        out_specs=pl.BlockSpec((block, positions, width), lambda f: (f, 0, 0)),
        out_shape=jax.ShapeDtypeStruct((frames, positions, width), jnp.bfloat16),
        compiler_params=PARAMS,
        cost_estimate=pl.CostEstimate(
            flops=2 * frames * positions * depth * width,
            bytes_accessed=2 * (frames * positions * depth + depth * width),
            transcendentals=frames * heads * positions * positions,
        ),
        name="space_attention",
    )(tokens, weights, parts)


def project_kernel(blocks, rows, one_ref, two_ref, w_ref, out_ref, held, sems):
    here = blocks * rows

    @pl.when(pl.program_id(0) == 0)
    def _():
        copies = [
            pltpu.make_async_copy(source, held.at[pl.ds(i * here, here)], sems.at[i])
            for i, source in enumerate((one_ref, two_ref))
        ]
        for copy in copies:
            copy.start()
        for copy in copies:
            copy.wait()

    result = jnp.dot(held[...], w_ref[...], preferred_element_type=jnp.float32)

    def store(b, g, tile):
        out_ref[g, b * 16 : b * 16 + 16, :] = tile

    pair_rows(result[:here], result[here:], blocks, rows, store)


def project(one, two, weights):
    blocks, rows, depth = one.shape
    cols = weights.shape[1]
    step = cols // ROLES
    groups = rows // 8
    return pl.pallas_call(
        lambda *refs: project_kernel(blocks, rows, *refs),
        grid=(ROLES,),
        in_specs=[pl.BlockSpec(memory_space=pl.ANY)] * 2 + [pl.BlockSpec((depth, step), lambda r: (0, r))],
        out_specs=pl.BlockSpec((groups, blocks * 16, step), lambda r: (0, 0, r)),
        out_shape=jax.ShapeDtypeStruct((groups, blocks * 16, cols), jnp.bfloat16),
        scratch_shapes=[pltpu.VMEM((2 * blocks * rows, depth), jnp.bfloat16), pltpu.SemaphoreType.DMA((2,))],
        compiler_params=PARAMS,
        cost_estimate=pl.CostEstimate(
            flops=4 * blocks * rows * depth * cols,
            bytes_accessed=2 * (2 * blocks * rows * depth + depth * cols),
            transcendentals=0,
        ),
        name="project",
    )(*[source.reshape(blocks * rows, depth) for source in (one, two)], weights)


def pieces(value):
    high = value.astype(jnp.bfloat16).astype(jnp.float32)
    mid = (value - high).astype(jnp.bfloat16).astype(jnp.float32)
    return high, mid, value - high - mid


def time_kernel(heads, spots, *refs):
    ins, peak_ref, outs = refs[: len(spots)], refs[len(spots)], refs[len(spots) + 1 :]
    groups = ins[0].shape[0]
    width = heads * HD
    total = sum(16 * len(spot) for spot in spots)
    row = lax.broadcasted_iota(jnp.int32, (total, total), 0)
    col = lax.broadcasted_iota(jnp.int32, (total, total), 1)
    mask = ((row ^ col) & 7) == 0
    line = lax.broadcasted_iota(jnp.int32, (16, HD), 0)
    for h in range(heads):
        peak = jnp.full((1, 1), -jnp.inf, jnp.float32)
        here = slice(h * HD, (h + 1) * HD)
        for g in range(groups):
            cols = []
            for r in range(ROLES):
                at = r * width + h * HD
                cols.append(jnp.concatenate([x[g, :, at : at + HD] for x in ins], axis=0))
            result, highest = attend(*cols, mask)
            peak = jnp.maximum(peak, highest * score_scale)
            result = result.astype(jnp.bfloat16)
            at = 0
            for out, pair in (place for spot in spots for place in spot):
                outs[out][g * 32 + pair * 16 : g * 32 + pair * 16 + 16, here] = result[at : at + 16]
                at += 16
        tail = jnp.zeros((16, HD), jnp.float32)
        both = pieces(peak_ref[0:1, here]) + pieces(jnp.broadcast_to(peak, (1, HD)))
        for i, value in enumerate(both):
            tail = jnp.where(line == i, value, tail)
        for out in outs:
            out[groups * 32 : groups * 32 + 16, here] = tail.astype(jnp.bfloat16)


def time_attention(parts, spots, peaks, heads, count):
    groups = parts[0].shape[0]
    width = heads * HD
    total = sum(16 * len(spot) for spot in spots)
    shape = jax.ShapeDtypeStruct((groups * 32 + 16, width), jnp.bfloat16)
    return pl.pallas_call(
        lambda *refs: time_kernel(heads, spots, *refs),
        in_specs=[VMEM] * (len(parts) + 1),
        out_specs=[VMEM] * count,
        out_shape=[shape] * count,
        compiler_params=PARAMS,
        cost_estimate=pl.CostEstimate(
            flops=4 * groups * heads * total * total * HD,
            bytes_accessed=8 * groups * total * width,
            transcendentals=groups * heads * total * total,
        ),
        name="time_attention",
    )(*parts, peaks)


def finish_kernel(direct, heads, index_ref, *refs):
    ins, out_ref, clip_ref = refs[:-2], refs[-2], refs[-1]
    groups = (ins[0].shape[0] - 16) // 32
    mine = index_ref[0]
    peak = None
    for d, source in enumerate(ins):
        for two in range(groups // 2):
            for pair in range(2):
                starts = [(2 * two + k) * 32 + pair * 16 for k in range(2)]
                a, b = (source[start : start + 16, :].astype(jnp.float32) for start in starts)
                for k in range(2):
                    tile = jnp.concatenate([a[8 * k : 8 * k + 8], b[8 * k : 8 * k + 8]], axis=0)
                    frame = 2 * pair + k if d in direct else mine ^ (2 * pair + k)
                    start = pl.multiple_of(index_ref[1 + d] * (groups * 8) + two * 16, 16)
                    out_ref[frame, pl.ds(start, 16), :] = tile.astype(jnp.bfloat16)
        tail = source[groups * 32 : groups * 32 + 16, :].astype(jnp.float32)
        values = [tail[3 * a : 3 * a + 1] + tail[3 * a + 1 : 3 * a + 2] + tail[3 * a + 2 : 3 * a + 3] for a in range(2)]
        peak = values if peak is None else [jnp.maximum(p, v) for p, v in zip(peak, values)]
    for a in range(2):
        clip_ref[a : a + 1, :] = jnp.sqrt(clip_limit / jnp.maximum(peak[a], clip_limit))


def finish(index, received, frames, positions, width, direct, heads):
    return pl.pallas_call(
        lambda *refs: finish_kernel(direct, heads, *refs),
        in_specs=[pl.BlockSpec(memory_space=pltpu.SMEM)] + [VMEM] * len(received),
        out_specs=[VMEM, VMEM],
        out_shape=[
            jax.ShapeDtypeStruct((frames, positions, width), jnp.bfloat16),
            jax.ShapeDtypeStruct((2, width), jnp.float32),
        ],
        compiler_params=PARAMS,
        name="finish",
    )(index, *received)


def swap(value, axis, size, distance):
    return lax.ppermute(value, axis, [(i, i ^ distance) for i in range(size)])


def fast_body(seq, head, patch_tokens, projection):
    frames, positions, depth = patch_tokens.shape
    heads = projection.shape[-1] // HD
    width = heads * HD
    rows = positions // seq
    me, mine = lax.axis_index("seq"), lax.axis_index("head")
    token_group, direct = (4, 5, 2, 3, 1), (0, 6, 7)
    owners = jnp.stack([me ^ d for d in range(seq)]).astype(jnp.int32)
    paired = jnp.transpose(projection, (0, 2, 1, 3))

    def piece(frame, owner):
        return lax.dynamic_slice(patch_tokens, (frame, owner * rows, 0), (1, rows, depth))

    got = [swap(piece(mine, me ^ d), "seq", seq, d) for d in token_group]
    index = jnp.stack([me ^ d for d in direct]).astype(jnp.int32)
    weights, own, *away = early(index, patch_tokens, paired, rows, len(direct))
    away = [swap(part, "seq", seq, d) for d, part in zip(direct[1:], away)]

    *got, weights = lax.optimization_barrier([*got, weights])
    here = jnp.concatenate(got, axis=0)
    there = swap(here, "head", head, 2)
    here_other = swap(here, "head", head, 1)
    parts, last, peaks = space_peak(patch_tokens, paired, heads)
    first = project(here, here_other, weights)
    there, peaks, first, *away = lax.optimization_barrier([there, peaks, first, *away])
    there_other = swap(there, "head", head, 1)
    second = project(there, there_other, weights)
    spots = [[(d, 0), (d, 1)] for d in direct] + [[(d, pair) for d in token_group] for pair in range(2)]
    outs = time_attention([own, *away, first, second], spots, peaks, heads, seq)
    *outs, parts = lax.optimization_barrier([*outs, parts])
    received = [out if d == 0 else swap(out, "seq", seq, d) for d, out in enumerate(outs)]
    space_out = space_attention(patch_tokens, last, parts, heads)
    finish_index = jnp.concatenate([mine.astype(jnp.int32)[None], owners])
    time_out, clip = finish(finish_index, received, frames, positions, width, direct, heads)
    return space_out, time_out, clip[:, ::HD]


def mixing(scores):
    highest = jnp.max(scores, axis=-1, keepdims=True)
    expon = jnp.exp(scores - highest)
    return (expon / jnp.sum(expon, axis=-1, keepdims=True)).astype(jnp.bfloat16)


def plain_attention(form, query_part, key_part, value_part):
    scores = jnp.einsum(form[0], query_part, key_part, preferred_element_type=jnp.float32) * score_scale
    result = jnp.einsum(form[1], mixing(scores), value_part, preferred_element_type=jnp.float32)
    return result.astype(jnp.bfloat16), jnp.max(scores, axis=(0, 2, 3))


def plain_body(patch_tokens, projection):
    frames, positions, depth = patch_tokens.shape
    heads = projection.shape[-1] // HD
    parts = jnp.dot(
        patch_tokens.reshape(-1, depth), projection.reshape(depth, -1), preferred_element_type=jnp.float32
    )
    parts = parts.astype(jnp.bfloat16).reshape(frames, positions, 2, ROLES, heads, HD)
    space_out, space_high = plain_attention(
        ("fihd,fjhd->fhij", "fhij,fjhd->fihd"), *(parts[:, :, 0, r] for r in range(ROLES))
    )
    moved = [lax.all_to_all(parts[:, :, 1, r], "seq", split_axis=1, concat_axis=0, tiled=True) for r in range(ROLES)]
    time_out, time_high = plain_attention(("fphd,gphd->phfg", "phfg,gphd->fphd"), *moved)
    time_out = lax.all_to_all(time_out, "seq", split_axis=0, concat_axis=1, tiled=True)
    peak = lax.pmax(jnp.stack([space_high, time_high]), "seq")
    clip_factor = jnp.sqrt(clip_limit / jnp.maximum(peak, clip_limit))
    flat = (frames, positions, heads * HD)
    return space_out.reshape(flat), time_out.reshape(flat), clip_factor


def solution(mesh):
    seq, head = mesh.shape["seq"], mesh.shape["head"]

    def body(patch_tokens, projection):
        frames, positions, _ = patch_tokens.shape
        if seq == 8 and head == 4 and frames == 4 and positions % (16 * seq) == 0:
            return fast_body(seq, head, patch_tokens, projection)
        return plain_body(patch_tokens, projection)

    return jax.shard_map(
        body,
        mesh=mesh,
        in_specs=(P("seq", None, None), P(None, None, None, "head")),
        out_specs=(P("seq", None, "head"), P("seq", None, "head"), P(None, "head")),
        check_vma=False,
    )
```

time: 142 us -> 93.8 us (0.66)
  waiting for transfers between devices: 37.7 us -> 6.61 us
  local copies, waits for them, and re-layouts: 34.5 us -> 4.82 us
  Pallas kernels: 40.2 us -> 53.4 us
    ppermute x20 -> x17, waiting for transfers between devices: 37.7 us -> 6.61 us  [swap(): return lax.ppermute(value, axis, [(i, i ^ distance) for i in range(size)])]
    pallas_call x3 -> x5, Pallas kernels: 19.7 us -> 40.6 us  [the longest x1 14.5 us: early(): pl.pallas_call(lambda *refs: early_kernel(count, *refs), grid_spec=pltpu....]
    reshape x1 -> x0, local copies, waits for them, and re-layouts: 15 us -> none  [fast_body(): jnp.transpose(projection, (1, 0, 2, 3)).reshape(2 * depth, ROLES * width)]
    unnamed x6 -> x8, local copies, waits for them, and re-layouts: 17 us -> 2.71 us
    pallas_call x3 -> x2, Pallas kernels: 20.5 us -> 12.7 us  [project(): pl.pallas_call(lambda *refs: project_kernel(blocks, rows, *refs), grid=(R...]
    ppermute x20 -> x17, starting transfers between devices: 27.3 us -> 26.6 us  [swap(): return lax.ppermute(value, axis, [(i, i ^ distance) for i in range(size)])]
  transfers between devices with their start and end apart: 20 -> 17, of which waited for: 4 -> 3; matrix products, arithmetic and copies ran while one was open for 23% -> 0% of each run, Pallas kernels for 21% -> 47%
where the time goes in v2:
time: 93.8 us; the launch traced here: 92.3 us
  Pallas kernels  53.4 us (57%)
  starting transfers between devices  26.6 us (28%)
  waiting for transfers between devices  6.61 us (7%)
  local copies, waits for them, and re-layouts  4.82 us (5%)
    ppermute x17, starting transfers between devices, swap(): return lax.ppermute(value, axis, [(i, i ^ distance) for i in range(size)])  26.6 us
    pallas_call x1, Pallas kernels, early(): pl.pallas_call(lambda *refs: early_kernel(count, *refs), grid_spec=pltpu....  14.5 us
    pallas_call x1, Pallas kernels, space_peak(): pl.pallas_call(lambda *refs: space_peak_kernel(heads, *refs), grid=(depth...  14.3 us
    pallas_call x2, Pallas kernels, project(): pl.pallas_call(lambda *refs: project_kernel(blocks, rows, *refs), grid=(R...  12.7 us
    pallas_call x1, Pallas kernels, space_attention(): pl.pallas_call(lambda *refs: space_kernel(heads, *refs), grid=(frames //...  8.26 us
    ppermute x17, waiting for transfers between devices, swap(): return lax.ppermute(value, axis, [(i, i ^ distance) for i in range(size)])  6.61 us
    unnamed x8, local copies, waits for them, and re-layouts  2.71 us
    pallas_call x1, Pallas kernels, time_attention(): pl.pallas_call(lambda *refs: time_kernel(heads, spots, *refs), in_specs=[...  2.05 us
  transfers between devices with their start and end apart: 17, of which 3 were waited for; matrix products, arithmetic and copies ran while one was open for 0% of the time, Pallas kernels for 47%

profile of v2, /device:TPU:0, one launch (start us, length us, event | category | flops | bytes accessed | tf_op | source)
XLA Modules:
  0.0 92.3 jit_solution(6243173157296138704)
XLA Ops:
  0.7 1.4 %constant_dynamic-slice_fusion = (bf16[1,32,3072]{2,1,0:T(8,128)(2,1)S(1)}, bf16[1,32,3072]{2,1,0:T(8,128)(2,1)S(1)}, bf16[1,32,3072]{2,1,0:T(8,128)(2,1)S(1)}, ...) fusion(bf16[4,256,3072]{2,1,0:T(8,128)(2,1)} %refs_0_.3, s32[]{:T(128)S(6)} %select_n.22, s32[]{:T(128)S(6)} %select_n.27, ...), kind=kLoop, calls=%fused_computation.5 | loop fusion | bytes 1966104 | tf_op jit(solution)/shard_map/dynamic_slice | solution.py:380
  2.0 3.0 %collective-permute-start.4 = (bf16[1,32,3072]{2,1,0:T(8,128)(2,1)S(1)}, bf16[1,32,3072]{2,1,0:T(8,128)(2,1)S(1)}, u32[]{:S(2)}, u32[]{:S(2)}) collective-permute-start(bf16[1,32,3072]{2,1,0:T(8,128)(2,1)S(1)} %get-tuple-element.77), channel_id=1, source_target_pairs={{0,4},{4,0},{8,12},{12,8},{16,20},{20,16},{24,28},{28,24},{1,5},{5... | collective-permute-start | bytes 589832 | tf_op jit(solution)/shard_map/ppermute | solution.py:366
  5.0 1.5 %collective-permute-start.3 = (bf16[1,32,3072]{2,1,0:T(8,128)(2,1)S(1)}, bf16[1,32,3072]{2,1,0:T(8,128)(2,1)S(1)}, u32[]{:S(2)}, u32[]{:S(2)}) collective-permute-start(bf16[1,32,3072]{2,1,0:T(8,128)(2,1)S(1)} %get-tuple-element.78), channel_id=1, source_target_pairs={{0,12},{4,8},{8,4},{12,0},{16,28},{20,24},{24,20},{28,16},{1,13},{... | collective-permute-start | bytes 589832 | tf_op jit(solution)/shard_map/ppermute | solution.py:366
  6.6 0.0 collective-permute-start.2
  6.6 3.9 %collective-permute-start.1 = (bf16[1,32,3072]{2,1,0:T(8,128)(2,1)S(1)}, bf16[1,32,3072]{2,1,0:T(8,128)(2,1)S(1)}, u32[]{:S(2)}, u32[]{:S(2)}) collective-permute-start(bf16[1,32,3072]{2,1,0:T(8,128)(2,1)S(1)} %get-tuple-element.80), channel_id=1, source_target_pairs={{0,20},{4,16},{8,28},{12,24},{16,4},{20,0},{24,12},{28,8},{1,21},{... | collective-permute-start | bytes 589832 | tf_op jit(solution)/shard_map/ppermute | solution.py:366
  10.5 0.3 collective-permute-start
  10.9 0.1 pad_add_fusion.refs_0_
  11.0 14.5 %early.1 = (bf16[3072,1152]{1,0:T(8,128)(2,1)}, bf16[4,32,1152]{2,1,0:T(8,128)(2,1)S(1)}, bf16[4,32,1152]{2,1,0:T(8,128)(2,1)S(1)}, bf16[4,32,1152]{2,1,0:T(8,128)(2,1)S(1)}) custom-call(s32[3]{0:T(128)S(1)} %pad_add_fusion.refs_0_, bf16[4,256,3072]{2,1,0:T(8,128)(2,1)} %refs_0_.3, bf16[4,256,3072]{2,1,0:T(8,128)(2,1)} %refs_0_.3, ...), custom_call_target="tpu_custom_call" | custom-call | flops 5435817984 | bytes 21233664 | tf_op jit(solution)/shard_map/early/pallas_call | solution.py:97
  25.4 1.9 %collective-permute-done = bf16[1,32,3072]{2,1,0:T(8,128)(2,1)S(1)} collective-permute-done((bf16[1,32,3072]{2,1,0:T(8,128)(2,1)S(1)}, bf16[1,32,3072]{2,1,0:T(8,128)(2,1)S(1)}, u32[]{:S(2)}, u32[]{:S(2)}) %collective-permute-start) | collective-permute-done | bytes 196640 | tf_op jit(solution)/shard_map/ppermute | solution.py:366
  27.4 0.1 collective-permute-start.6
  27.5 1.6 %collective-permute-start.5 = (bf16[5,32,3072]{2,1,0:T(8,128)(2,1)S(1)}, bf16[5,32,3072]{2,1,0:T(8,128)(2,1)S(1)}, u32[]{:S(2)}, u32[]{:S(2)}) collective-permute-start(bf16[5,32,3072]{2,1,0:T(8,128)(2,1)S(1)} %constant_dynamic-update-slice_fusion), channel_id=1, source_target_pairs={{0,2},{1,3},{2,0},{3,1},{4,6},{5,7},{6,4},{7,5},{8,10},{9,11},{10,... | collective-permute-start | bytes 2949128 | tf_op jit(solution)/shard_map/ppermute | solution.py:366
  29.1 3.6 %collective-permute-start.7 = (bf16[4,32,1152]{2,1,0:T(8,128)(2,1)S(1)}, bf16[4,32,1152]{2,1,0:T(8,128)(2,1)S(1)}, u32[]{:S(2)}, u32[]{:S(2)}) collective-permute-start(bf16[4,32,1152]{2,1,0:T(8,128)(2,1)S(1)} %get-tuple-element.50), channel_id=1, source_target_pairs={{0,24},{4,28},{8,16},{12,20},{16,8},{20,12},{24,0},{28,4},{1,25},{... | collective-permute-start | bytes 884744 | tf_op jit(solution)/shard_map/ppermute | solution.py:366
  32.7 0.2 collective-permute-start.8
  32.9 14.3 %space_peak.1 = (bf16[1024,768]{1,0:T(8,128)(2,1)S(1)}, bf16[3072,384]{1,0:T(8,128)(2,1)S(1)}, f32[8,384]{1,0:T(8,128)S(1)}) custom-call(bf16[4,256,3072]{2,1,0:T(8,128)(2,1)} %refs_0_.3, bf16[3072,3,2,384]{3,2,1,0:T(2,128)(2,1)} %bitcast.19), custom_call_target="tpu_custom_call" | custom-call | flops 7549747200 | bytes 22806528 | tf_op jit(solution)/shard_map/space_peak/pallas_call | solution.py:158
  47.3 1.2 %copy-done = bf16[1024,768]{1,0:T(8,128)(2,1)} copy-done((bf16[1024,768]{1,0:T(8,128)(2,1)}, bf16[1024,768]{1,0:T(8,128)(2,1)S(1)}, u32[]{:S(2)}) %copy-start) | copy-done | bytes 1572888
  48.5 6.4 %project.2.refs_3_ = bf16[4,80,1152]{2,1,0:T(8,128)(2,1)S(1)} custom-call(bf16[160,3072]{1,0:T(8,128)(2,1)S(1)} %bitcast.14, bf16[160,3072]{1,0:T(8,128)(2,1)S(1)} %bitcast.16, bf16[3072,1152]{1,0:T(8,128)(2,1)} %get-tuple-element.49.refs_2_), custom_call_target="tpu_custom_call" | custom-call | flops 2264924160 | bytes 9043968 | tf_op jit(solution)/shard_map/project/pallas_call | solution.py:254
  54.9 0.1 collective-permute-start.9
  55.0 2.6 %collective-permute-done.9 = bf16[5,32,3072]{2,1,0:T(8,128)(2,1)S(1)} collective-permute-done((bf16[5,32,3072]{2,1,0:T(8,128)(2,1)S(1)}, bf16[5,32,3072]{2,1,0:T(8,128)(2,1)S(1)}, u32[]{:S(2)}, u32[]{:S(2)}) %collective-permute-start.9) | collective-permute-done | bytes 983072 | tf_op jit(solution)/shard_map/ppermute | solution.py:366
  57.6 6.4 %project.3.refs_4_ = bf16[4,80,1152]{2,1,0:T(8,128)(2,1)S(1)} custom-call(bf16[160,3072]{1,0:T(8,128)(2,1)S(1)} %bitcast.15, bf16[160,3072]{1,0:T(8,128)(2,1)S(1)} %bitcast.17, bf16[3072,1152]{1,0:T(8,128)(2,1)} %get-tuple-element.49.refs_2_), custom_call_target="tpu_custom_call" | custom-call | flops 2264924160 | bytes 9043968 | tf_op jit(solution)/shard_map/project/pallas_call | solution.py:254
  63.9 2.1 %time_attention.1 = (bf16[144,384]{1,0:T(8,128)(2,1)S(1)}, bf16[144,384]{1,0:T(8,128)(2,1)S(1)}, bf16[144,384]{1,0:T(8,128)(2,1)S(1)}, bf16[144,384]{1,0:T(8,128...) custom-call(bf16[4,32,1152]{2,1,0:T(8,128)(2,1)S(1)} %get-tuple-elem, ...), custom_call_target="tpu_custom_call" | custom-call | flops 402653184 | bytes 3145728 | tf_op jit(solution)/shard_map/time_attention/pallas_call | solution.py:314
  66.0 1.6 %collective-permute-start.10 = (bf16[144,384]{1,0:T(8,128)(2,1)S(1)}, bf16[144,384]{1,0:T(8,128)(2,1)S(1)}, u32[]{:S(2)}, u32[]{:S(2)}) collective-permute-start(bf16[144,384]{1,0:T(8,128)(2,1)S(1)} %get-tuple-element.68), channel_id=1, source_target_pairs={{0,4},{4,0},{8,12},{12,8},{16,20},{20,16},{24,28},{28,24},{1,5},{5... | collective-permute-start | bytes 331784 | tf_op jit(solution)/shard_map/ppermute | solution.py:366
  67.6 2.9 %collective-permute-start.11 = (bf16[144,384]{1,0:T(8,128)(2,1)S(1)}, bf16[144,384]{1,0:T(8,128)(2,1)S(1)}, u32[]{:S(2)}, u32[]{:S(2)}) collective-permute-start(bf16[144,384]{1,0:T(8,128)(2,1)S(1)} %get-tuple-element.69), channel_id=1, source_target_pairs={{0,8},{4,12},{8,0},{12,4},{16,24},{20,28},{24,16},{28,20},{1,9},{5... | collective-permute-start | bytes 331784 | tf_op jit(solution)/shard_map/ppermute | solution.py:366
  70.5 0.1 concatenate.7.refs_0_
  70.6 1.9 %collective-permute-start.13 = (bf16[144,384]{1,0:T(8,128)(2,1)S(1)}, bf16[144,384]{1,0:T(8,128)(2,1)S(1)}, u32[]{:S(2)}, u32[]{:S(2)}) collective-permute-start(bf16[144,384]{1,0:T(8,128)(2,1)S(1)} %get-tuple-element.71), channel_id=1, source_target_pairs={{0,16},{4,20},{8,24},{12,28},{16,0},{20,4},{24,8},{28,12},{1,17},{... | collective-permute-start | bytes 331784 | tf_op jit(solution)/shard_map/ppermute | solution.py:366
  72.5 1.9 %collective-permute-start.14 = (bf16[144,384]{1,0:T(8,128)(2,1)S(1)}, bf16[144,384]{1,0:T(8,128)(2,1)S(1)}, u32[]{:S(2)}, u32[]{:S(2)}) collective-permute-start(bf16[144,384]{1,0:T(8,128)(2,1)S(1)} %get-tuple-element.72), channel_id=1, source_target_pairs={{0,20},{4,16},{8,28},{12,24},{16,4},{20,0},{24,12},{28,8},{1,21},{... | collective-permute-start | bytes 331784 | tf_op jit(solution)/shard_map/ppermute | solution.py:366
  74.4 2.7 %collective-permute-start.15 = (bf16[144,384]{1,0:T(8,128)(2,1)S(1)}, bf16[144,384]{1,0:T(8,128)(2,1)S(1)}, u32[]{:S(2)}, u32[]{:S(2)}) collective-permute-start(bf16[144,384]{1,0:T(8,128)(2,1)S(1)} %get-tuple-element.73), channel_id=1, source_target_pairs={{0,24},{4,28},{8,16},{12,20},{16,8},{20,12},{24,0},{28,4},{1,25},{... | collective-permute-start | bytes 331784 | tf_op jit(solution)/shard_map/ppermute | solution.py:366
  77.1 1.2 %collective-permute-start.16 = (bf16[144,384]{1,0:T(8,128)(2,1)S(1)}, bf16[144,384]{1,0:T(8,128)(2,1)S(1)}, u32[]{:S(2)}, u32[]{:S(2)}) collective-permute-start(bf16[144,384]{1,0:T(8,128)(2,1)S(1)} %get-tuple-element.74), channel_id=1, source_target_pairs={{0,28},{4,24},{8,20},{12,16},{16,12},{20,8},{24,4},{28,0},{1,29},{... | collective-permute-start | bytes 331784 | tf_op jit(solution)/shard_map/ppermute | solution.py:366
  78.3 1.4 %copy-done.1 = bf16[1024,768]{1,0:T(8,128)(2,1)S(1)} copy-done((bf16[1024,768]{1,0:T(8,128)(2,1)S(1)}, bf16[1024,768]{1,0:T(8,128)(2,1)}, u32[]{:S(2)}) %copy-start.1) | copy-done | bytes 1572888
  79.7 8.3 %space_attention.1 = bf16[4,256,384]{2,1,0:T(8,128)(2,1)} custom-call(bf16[4,256,3072]{2,1,0:T(8,128)(2,1)} %refs_0_.3, bf16[3072,384]{1,0:T(8,128)(2,1)S(1)} %get-tuple-element.40.refs_1_, bf16[1024,768]{1,0:T(8,128)(2,1)S(1)} %copy-done.1), custom_call_target="tpu_custom_call" | custom-call | flops 2415919104 | bytes 8650752 | tf_op jit(solution)/shard_map/space_attention/pallas_call | solution.py:207
  88.0 2.1 %collective-permute-done.14.refs_6_ = bf16[144,384]{1,0:T(8,128)(2,1)S(1)} collective-permute-done((bf16[144,384]{1,0:T(8,128)(2,1)S(1)}, bf16[144,384]{1,0:T(8,128)(2,1)S(1)}, u32[]{:S(2)}, u32[]{:S(2)}) %collective-permute-start.14) | collective-permute-done | bytes 110624 | tf_op jit(solution)/shard_map/ppermute | solution.py:366
  90.1 1.5 %finish.1 = (bf16[4,256,384]{2,1,0:T(8,128)(2,1)}, f32[2,384]{1,0:T(2,128)S(1)}) custom-call(s32[9]{0:T(128)S(1)} %concatenate.7.refs_0_, bf16[144,384]{1,0:T(8,128)(2,1)S(1)} %get-tuple-element.67.refs_1_, bf16[144,384]{1,0:T(8,128)(2,1)S(1)} %collective-permute-done.10.refs_2_, bf16[144,384]{1,0:T(8,128)(2,1)S(1)} %collective-permute-done.11.refs_3_, ...), custom_call_target="tpu_custom_call" | custom-call | tf_op jit(solution)/shard_map/finish/pallas_call | solution.py:352
  91.6 0.6 slice.3
  (22 shorter events, 0.1 us)
Async XLA Ops:
  2.0 23.4 %collective-permute-start.4 = (bf16[1,32,3072]{2,1,0:T(8,128)(2,1)S(1)}, bf16[1,32,3072]{2,1,0:T(8,128)(2,1)S(1)}, u32[]{:S(2)}, u32[]{:S(2)}) collective-permute-start(bf16[1,32,3072]{2,1,0:T(8,128)(2,1)S(1)} %get-tuple-element.77), channel_id=1, source_target_pairs={{0,4},{4,0},{8,12},{12,8},{16,20},{20,16},{24,28},{28,24},{1,5},{5... | collective-permute-start | bytes 589832 | tf_op jit(solution)/shard_map/ppermute | solution.py:366
  5.0 20.4 %collective-permute-start.3 = (bf16[1,32,3072]{2,1,0:T(8,128)(2,1)S(1)}, bf16[1,32,3072]{2,1,0:T(8,128)(2,1)S(1)}, u32[]{:S(2)}, u32[]{:S(2)}) collective-permute-start(bf16[1,32,3072]{2,1,0:T(8,128)(2,1)S(1)} %get-tuple-element.78), channel_id=1, source_target_pairs={{0,12},{4,8},{8,4},{12,0},{16,28},{20,24},{24,20},{28,16},{1,13},{... | collective-permute-start | bytes 589832 | tf_op jit(solution)/shard_map/ppermute | solution.py:366
  6.6 18.8 %collective-permute-start.2 = (bf16[1,32,3072]{2,1,0:T(8,128)(2,1)S(1)}, bf16[1,32,3072]{2,1,0:T(8,128)(2,1)S(1)}, u32[]{:S(2)}, u32[]{:S(2)}) collective-permute-start(bf16[1,32,3072]{2,1,0:T(8,128)(2,1)S(1)} %get-tuple-element.79), channel_id=1, source_target_pairs={{0,8},{4,12},{8,0},{12,4},{16,24},{20,28},{24,16},{28,20},{1,9},{5... | collective-permute-start | bytes 589832 | tf_op jit(solution)/shard_map/ppermute | solution.py:366
  6.6 18.8 %collective-permute-start.1 = (bf16[1,32,3072]{2,1,0:T(8,128)(2,1)S(1)}, bf16[1,32,3072]{2,1,0:T(8,128)(2,1)S(1)}, u32[]{:S(2)}, u32[]{:S(2)}) collective-permute-start(bf16[1,32,3072]{2,1,0:T(8,128)(2,1)S(1)} %get-tuple-element.80), channel_id=1, source_target_pairs={{0,20},{4,16},{8,28},{12,24},{16,4},{20,0},{24,12},{28,8},{1,21},{... | collective-permute-start | bytes 589832 | tf_op jit(solution)/shard_map/ppermute | solution.py:366
  10.5 16.8 %collective-permute-start = (bf16[1,32,3072]{2,1,0:T(8,128)(2,1)S(1)}, bf16[1,32,3072]{2,1,0:T(8,128)(2,1)S(1)}, u32[]{:S(2)}, u32[]{:S(2)}) collective-permute-start(bf16[1,32,3072]{2,1,0:T(8,128)(2,1)S(1)} %get-tuple-element.81), channel_id=1, source_target_pairs={{0,16},{4,20},{8,24},{12,28},{16,0},{20,4},{24,8},{28,12},{1,17},{... | collective-permute-start | bytes 589832 | tf_op jit(solution)/shard_map/ppermute | solution.py:366
  27.4 21.1 %collective-permute-start.6 = (bf16[5,32,3072]{2,1,0:T(8,128)(2,1)S(1)}, bf16[5,32,3072]{2,1,0:T(8,128)(2,1)S(1)}, u32[]{:S(2)}, u32[]{:S(2)}) collective-permute-start(bf16[5,32,3072]{2,1,0:T(8,128)(2,1)S(1)} %constant_dynamic-update-slice_fusion), channel_id=1, source_target_pairs={{0,1},{1,0},{2,3},{3,2},{4,5},{5,4},{6,7},{7,6},{8,9},{9,8},{10,11... | collective-permute-start | bytes 2949128 | tf_op jit(solution)/shard_map/ppermute | solution.py:366
  27.5 27.4 %collective-permute-start.5 = (bf16[5,32,3072]{2,1,0:T(8,128)(2,1)S(1)}, bf16[5,32,3072]{2,1,0:T(8,128)(2,1)S(1)}, u32[]{:S(2)}, u32[]{:S(2)}) collective-permute-start(bf16[5,32,3072]{2,1,0:T(8,128)(2,1)S(1)} %constant_dynamic-update-slice_fusion), channel_id=1, source_target_pairs={{0,2},{1,3},{2,0},{3,1},{4,6},{5,7},{6,4},{7,5},{8,10},{9,11},{10,... | collective-permute-start | bytes 2949128 | tf_op jit(solution)/shard_map/ppermute | solution.py:366
  29.1 25.8 %collective-permute-start.7 = (bf16[4,32,1152]{2,1,0:T(8,128)(2,1)S(1)}, bf16[4,32,1152]{2,1,0:T(8,128)(2,1)S(1)}, u32[]{:S(2)}, u32[]{:S(2)}) collective-permute-start(bf16[4,32,1152]{2,1,0:T(8,128)(2,1)S(1)} %get-tuple-element.50), channel_id=1, source_target_pairs={{0,24},{4,28},{8,16},{12,20},{16,8},{20,12},{24,0},{28,4},{1,25},{... | collective-permute-start | bytes 884744 | tf_op jit(solution)/shard_map/ppermute | solution.py:366
  32.7 22.2 %collective-permute-start.8 = (bf16[4,32,1152]{2,1,0:T(8,128)(2,1)S(1)}, bf16[4,32,1152]{2,1,0:T(8,128)(2,1)S(1)}, u32[]{:S(2)}, u32[]{:S(2)}) collective-permute-start(bf16[4,32,1152]{2,1,0:T(8,128)(2,1)S(1)} %get-tuple-element.51), channel_id=1, source_target_pairs={{0,28},{4,24},{8,20},{12,16},{16,12},{20,8},{24,4},{28,0},{1,29},{... | collective-permute-start | bytes 884744 | tf_op jit(solution)/shard_map/ppermute | solution.py:366
  47.3 1.3 %copy-start = (bf16[1024,768]{1,0:T(8,128)(2,1)}, bf16[1024,768]{1,0:T(8,128)(2,1)S(1)}, u32[]{:S(2)}) copy-start(bf16[1024,768]{1,0:T(8,128)(2,1)S(1)} %get-tuple-element.66.refs_2_) | copy-start | bytes 4718596
  54.9 2.6 %collective-permute-start.9 = (bf16[5,32,3072]{2,1,0:T(8,128)(2,1)S(1)}, bf16[5,32,3072]{2,1,0:T(8,128)(2,1)S(1)}, u32[]{:S(2)}, u32[]{:S(2)}) collective-permute-start(bf16[5,32,3072]{2,1,0:T(8,128)(2,1)S(1)} %collective-permute-done.5), channel_id=1, source_target_pairs={{0,1},{1,0},{2,3},{3,2},{4,5},{5,4},{6,7},{7,6},{8,9},{9,8},{10,11... | collective-permute-start | bytes 2949128 | tf_op jit(solution)/shard_map/ppermute | solution.py:366
  66.0 8.4 %collective-permute-start.10 = (bf16[144,384]{1,0:T(8,128)(2,1)S(1)}, bf16[144,384]{1,0:T(8,128)(2,1)S(1)}, u32[]{:S(2)}, u32[]{:S(2)}) collective-permute-start(bf16[144,384]{1,0:T(8,128)(2,1)S(1)} %get-tuple-element.68), channel_id=1, source_target_pairs={{0,4},{4,0},{8,12},{12,8},{16,20},{20,16},{24,28},{28,24},{1,5},{5... | collective-permute-start | bytes 331784 | tf_op jit(solution)/shard_map/ppermute | solution.py:366
  67.6 9.5 %collective-permute-start.11 = (bf16[144,384]{1,0:T(8,128)(2,1)S(1)}, bf16[144,384]{1,0:T(8,128)(2,1)S(1)}, u32[]{:S(2)}, u32[]{:S(2)}) collective-permute-start(bf16[144,384]{1,0:T(8,128)(2,1)S(1)} %get-tuple-element.69), channel_id=1, source_target_pairs={{0,8},{4,12},{8,0},{12,4},{16,24},{20,28},{24,16},{28,20},{1,9},{5... | collective-permute-start | bytes 331784 | tf_op jit(solution)/shard_map/ppermute | solution.py:366
  70.6 17.4 %collective-permute-start.12 = (bf16[144,384]{1,0:T(8,128)(2,1)S(1)}, bf16[144,384]{1,0:T(8,128)(2,1)S(1)}, u32[]{:S(2)}, u32[]{:S(2)}) collective-permute-start(bf16[144,384]{1,0:T(8,128)(2,1)S(1)} %get-tuple-element.70), channel_id=1, source_target_pairs={{0,12},{4,8},{8,4},{12,0},{16,28},{20,24},{24,20},{28,16},{1,13},{... | collective-permute-start | bytes 331784 | tf_op jit(solution)/shard_map/ppermute | solution.py:366
  70.6 17.4 %collective-permute-start.13 = (bf16[144,384]{1,0:T(8,128)(2,1)S(1)}, bf16[144,384]{1,0:T(8,128)(2,1)S(1)}, u32[]{:S(2)}, u32[]{:S(2)}) collective-permute-start(bf16[144,384]{1,0:T(8,128)(2,1)S(1)} %get-tuple-element.71), channel_id=1, source_target_pairs={{0,16},{4,20},{8,24},{12,28},{16,0},{20,4},{24,8},{28,12},{1,17},{... | collective-permute-start | bytes 331784 | tf_op jit(solution)/shard_map/ppermute | solution.py:366
  72.5 17.6 %collective-permute-start.14 = (bf16[144,384]{1,0:T(8,128)(2,1)S(1)}, bf16[144,384]{1,0:T(8,128)(2,1)S(1)}, u32[]{:S(2)}, u32[]{:S(2)}) collective-permute-start(bf16[144,384]{1,0:T(8,128)(2,1)S(1)} %get-tuple-element.72), channel_id=1, source_target_pairs={{0,20},{4,16},{8,28},{12,24},{16,4},{20,0},{24,12},{28,8},{1,21},{... | collective-permute-start | bytes 331784 | tf_op jit(solution)/shard_map/ppermute | solution.py:366
  74.4 15.7 %collective-permute-start.15 = (bf16[144,384]{1,0:T(8,128)(2,1)S(1)}, bf16[144,384]{1,0:T(8,128)(2,1)S(1)}, u32[]{:S(2)}, u32[]{:S(2)}) collective-permute-start(bf16[144,384]{1,0:T(8,128)(2,1)S(1)} %get-tuple-element.73), channel_id=1, source_target_pairs={{0,24},{4,28},{8,16},{12,20},{16,8},{20,12},{24,0},{28,4},{1,25},{... | collective-permute-start | bytes 331784 | tf_op jit(solution)/shard_map/ppermute | solution.py:366
  77.1 13.0 %collective-permute-start.16 = (bf16[144,384]{1,0:T(8,128)(2,1)S(1)}, bf16[144,384]{1,0:T(8,128)(2,1)S(1)}, u32[]{:S(2)}, u32[]{:S(2)}) collective-permute-start(bf16[144,384]{1,0:T(8,128)(2,1)S(1)} %get-tuple-element.74), channel_id=1, source_target_pairs={{0,28},{4,24},{8,20},{12,16},{16,12},{20,8},{24,4},{28,0},{1,29},{... | collective-permute-start | bytes 331784 | tf_op jit(solution)/shard_map/ppermute | solution.py:366
  78.3 1.4 %copy-start.1 = (bf16[1024,768]{1,0:T(8,128)(2,1)S(1)}, bf16[1024,768]{1,0:T(8,128)(2,1)}, u32[]{:S(2)}) copy-start(bf16[1024,768]{1,0:T(8,128)(2,1)} %copy-done) | copy-start | bytes 4718596

commit v3 on v2

--- a/solution.py
+++ b/solution.py
@@ -13,6 +13,9 @@
 score_scale = 1.0 / math.sqrt(HD)
 exp_scale = score_scale * math.log2(math.e)
 VMEM = pl.BlockSpec(memory_space=pltpu.VMEM)
+SMALL = pl.CostEstimate(flops=3000000000, bytes_accessed=8000000, transcendentals=0)
+LARGE = pl.CostEstimate(flops=16000000000, bytes_accessed=40000000, transcendentals=0)
+STEPS = 2
 PARAMS = pltpu.CompilerParams(vmem_limit_bytes=48 * 1024 * 1024)
 
 
@@ -92,7 +95,7 @@
     frames, _, depth = tokens.shape
     width = paired.shape[-1]
     cols = ROLES * width
-    block = 512
+    block = 1024
     out = jax.ShapeDtypeStruct((rows // 8, frames * 8, cols), jnp.bfloat16)
     return pl.pallas_call(
         lambda *refs: early_kernel(count, *refs),
@@ -178,11 +181,7 @@
             pltpu.VMEM((rows, 2 * width), jnp.float32),
         ],
         compiler_params=PARAMS,
-        cost_estimate=pl.CostEstimate(
-            flops=4 * rows * depth * width + 12 * CHUNK * depth * ROLES * width,
-            bytes_accessed=2 * rows * depth + 14 * depth * width,
-            transcendentals=0,
-        ),
+        cost_estimate=SMALL,
         name="space_peak",
     )(tokens, paired)
 
@@ -215,57 +214,9 @@
         out_specs=pl.BlockSpec((block, positions, width), lambda f: (f, 0, 0)),
         out_shape=jax.ShapeDtypeStruct((frames, positions, width), jnp.bfloat16),
         compiler_params=PARAMS,
-        cost_estimate=pl.CostEstimate(
-            flops=2 * frames * positions * depth * width,
-            bytes_accessed=2 * (frames * positions * depth + depth * width),
-            transcendentals=frames * heads * positions * positions,
-        ),
+        cost_estimate=LARGE,
         name="space_attention",
     )(tokens, weights, parts)
-
-
-def project_kernel(blocks, rows, one_ref, two_ref, w_ref, out_ref, held, sems):
-    here = blocks * rows
-
-    @pl.when(pl.program_id(0) == 0)
-    def _():
-        copies = [
-            pltpu.make_async_copy(source, held.at[pl.ds(i * here, here)], sems.at[i])
-            for i, source in enumerate((one_ref, two_ref))
-        ]
-        for copy in copies:
-            copy.start()
-        for copy in copies:
-            copy.wait()
-
-    result = jnp.dot(held[...], w_ref[...], preferred_element_type=jnp.float32)
-
-    def store(b, g, tile):
-        out_ref[g, b * 16 : b * 16 + 16, :] = tile
-
-    pair_rows(result[:here], result[here:], blocks, rows, store)
-
-
-def project(one, two, weights):
-    blocks, rows, depth = one.shape
-    cols = weights.shape[1]
-    step = cols // ROLES
-    groups = rows // 8
-    return pl.pallas_call(
-        lambda *refs: project_kernel(blocks, rows, *refs),
-        grid=(ROLES,),
-        in_specs=[pl.BlockSpec(memory_space=pl.ANY)] * 2 + [pl.BlockSpec((depth, step), lambda r: (0, r))],
-        out_specs=pl.BlockSpec((groups, blocks * 16, step), lambda r: (0, 0, r)),
-        out_shape=jax.ShapeDtypeStruct((groups, blocks * 16, cols), jnp.bfloat16),
-        scratch_shapes=[pltpu.VMEM((2 * blocks * rows, depth), jnp.bfloat16), pltpu.SemaphoreType.DMA((2,))],
-        compiler_params=PARAMS,
-        cost_estimate=pl.CostEstimate(
-            flops=4 * blocks * rows * depth * cols,
-            bytes_accessed=2 * (2 * blocks * rows * depth + depth * cols),
-            transcendentals=0,
-        ),
-        name="project",
-    )(*[source.reshape(blocks * rows, depth) for source in (one, two)], weights)
 
 
 def pieces(value):
@@ -274,18 +225,88 @@
     return high, mid, value - high - mid
 
 
-def time_kernel(heads, spots, *refs):
-    ins, peak_ref, outs = refs[: len(spots)], refs[len(spots)], refs[len(spots) + 1 :]
+def pair_tiles(total, one, two, group):
+    tile = jnp.concatenate([total[at + group * 8 : at + group * 8 + 8] for at in (one, two)], axis=0)
+    return tile.astype(jnp.bfloat16)
+
+
+def add_product(total, sources, w_ref):
+    @pl.when(pl.program_id(0) == 0)
+    def _():
+        total[...] = jnp.zeros_like(total)
+
+    tokens = jnp.concatenate([x[...].reshape(-1, x.shape[-1]) for x in sources], axis=0)
+    total[...] += jnp.dot(tokens, w_ref[...], preferred_element_type=jnp.float32)
+
+
+def project_kernel(index_ref, one_ref, two_ref, own_ref, w_ref, out_ref, total):
+    blocks, rows, _ = one_ref.shape
+    frames = own_ref.shape[0]
+    add_product(total, (one_ref, two_ref, own_ref), w_ref)
+
+    @pl.when(pl.program_id(0) == pl.num_programs(0) - 1)
+    def _():
+        pairs = [(b, blocks + b) for b in range(blocks)]
+        pairs += [(2 * blocks + f, 2 * blocks + f + 1) for f in range(0, frames, 2)]
+        for g in range(rows // 8):
+            for i, (one, two) in enumerate(pairs):
+                out_ref[g, i * 16 : i * 16 + 16, :] = pair_tiles(total, one * rows, two * rows, g)
+
+
+def project(index, one, two, tokens, weights):
+    blocks, rows, depth = one.shape
+    frames = tokens.shape[0]
+    cols = weights.shape[1]
+    block = depth // STEPS
+    here = (2 * blocks + frames) * rows
+    shape = (rows // 8, (2 * blocks + frames) * 8, cols)
+    return pl.pallas_call(
+        project_kernel,
+        grid_spec=pltpu.PrefetchScalarGridSpec(
+            num_scalar_prefetch=1,
+            grid=(STEPS,),
+            in_specs=[pl.BlockSpec((blocks, rows, block), lambda k, index: (0, 0, k))] * 2
+            + [
+                pl.BlockSpec((frames, rows, block), lambda k, index: (0, index[0], k)),
+                pl.BlockSpec((block, cols), lambda k, index: (k, 0)),
+            ],
+            out_specs=pl.BlockSpec(shape, lambda k, index: (0, 0, 0)),
+            scratch_shapes=[pltpu.VMEM((here, cols), jnp.float32)],
+        ),
+        out_shape=jax.ShapeDtypeStruct(shape, jnp.bfloat16),
+        compiler_params=PARAMS,
+        cost_estimate=LARGE,
+        name="project",
+    )(index, one, two, tokens, weights)
+
+
+def late_kernel(heads, spots, blocks_to, *refs):
+    (one_ref, two_ref, w_ref), ins, peak_ref = refs[:3], refs[3 : 3 + len(spots)], refs[3 + len(spots)]
+    outs, (total, parts_ref) = refs[4 + len(spots) : -2], refs[-2:]
+    blocks, rows, _ = one_ref.shape
+    add_product(total, (one_ref, two_ref), w_ref)
+
+    @pl.when(pl.program_id(0) == pl.num_programs(0) - 1)
+    def _():
+        for b in range(blocks):
+            for g in range(rows // 8):
+                parts_ref[g, b * 16 : b * 16 + 16, :] = pair_tiles(total, b * rows, (blocks + b) * rows, g)
+        places = [place for spot in spots for place in spot] + [(d, 1) for d in blocks_to]
+        attend_time(heads, places, [*ins, parts_ref], peak_ref, outs)
+
+
+def attend_time(heads, spots, ins, peak_ref, outs):
     groups = ins[0].shape[0]
     width = heads * HD
-    total = sum(16 * len(spot) for spot in spots)
-    row = lax.broadcasted_iota(jnp.int32, (total, total), 0)
-    col = lax.broadcasted_iota(jnp.int32, (total, total), 1)
+    size = 16 * len(spots)
+    row = lax.broadcasted_iota(jnp.int32, (size, size), 0)
+    col = lax.broadcasted_iota(jnp.int32, (size, size), 1)
     mask = ((row ^ col) & 7) == 0
     line = lax.broadcasted_iota(jnp.int32, (16, HD), 0)
+    lane = lax.broadcasted_iota(jnp.int32, (16, HD), 1) // TAIL
+    tail = jnp.zeros((16, HD), jnp.float32)
     for h in range(heads):
         peak = jnp.full((1, 1), -jnp.inf, jnp.float32)
-        here = slice(h * HD, (h + 1) * HD)
         for g in range(groups):
             cols = []
             for r in range(ROLES):
@@ -294,68 +315,79 @@
             result, highest = attend(*cols, mask)
             peak = jnp.maximum(peak, highest * score_scale)
             result = result.astype(jnp.bfloat16)
-            at = 0
-            for out, pair in (place for spot in spots for place in spot):
-                outs[out][g * 32 + pair * 16 : g * 32 + pair * 16 + 16, here] = result[at : at + 16]
-                at += 16
-        tail = jnp.zeros((16, HD), jnp.float32)
-        both = pieces(peak_ref[0:1, here]) + pieces(jnp.broadcast_to(peak, (1, HD)))
+            for i, (out, pair) in enumerate(spots):
+                start = (h * groups + g) * 32 + pair * 16
+                outs[out][start : start + 16, :] = result[i * 16 : i * 16 + 16]
+        both = pieces(peak_ref[0:1, h * HD : (h + 1) * HD]) + pieces(jnp.broadcast_to(peak, (1, HD)))
         for i, value in enumerate(both):
-            tail = jnp.where(line == i, value, tail)
-        for out in outs:
-            out[groups * 32 : groups * 32 + 16, here] = tail.astype(jnp.bfloat16)
-
-
-def time_attention(parts, spots, peaks, heads, count):
-    groups = parts[0].shape[0]
-    width = heads * HD
-    total = sum(16 * len(spot) for spot in spots)
-    shape = jax.ShapeDtypeStruct((groups * 32 + 16, width), jnp.bfloat16)
-    return pl.pallas_call(
-        lambda *refs: time_kernel(heads, spots, *refs),
-        in_specs=[VMEM] * (len(parts) + 1),
-        out_specs=[VMEM] * count,
-        out_shape=[shape] * count,
-        compiler_params=PARAMS,
-        cost_estimate=pl.CostEstimate(
-            flops=4 * groups * heads * total * total * HD,
-            bytes_accessed=8 * groups * total * width,
-            transcendentals=groups * heads * total * total,
-        ),
-        name="time_attention",
-    )(*parts, peaks)
+            tail = jnp.where((line == i) & (lane == h), value, tail)
+    for out in outs:
+        out[heads * groups * 32 :, :] = tail.astype(jnp.bfloat16)
+
+
+TAIL = 32
+
+
+def late(one, two, weights, parts, spots, peaks, heads, count, blocks_to):
+    blocks, rows, depth = one.shape
+    cols = weights.shape[1]
+    groups = rows // 8
+    block = depth // STEPS
+    shape = (heads * groups * 32 + 16, HD)
+
+    def whole(shape):
+        return pl.BlockSpec(shape, lambda k: (0,) * len(shape))
+
+    return pl.pallas_call(
+        lambda *refs: late_kernel(heads, spots, blocks_to, *refs),
+        grid=(STEPS,),
+        in_specs=[pl.BlockSpec((blocks, rows, block), lambda k: (0, 0, k))] * 2
+        + [pl.BlockSpec((block, cols), lambda k: (k, 0))]
+        + [whole(part.shape) for part in (*parts, peaks)],
+        out_specs=[whole(shape)] * count,
+        out_shape=[jax.ShapeDtypeStruct(shape, jnp.bfloat16)] * count,
+        scratch_shapes=[
+            pltpu.VMEM((2 * blocks * rows, cols), jnp.float32),
+            pltpu.VMEM((groups, blocks * 16, cols), jnp.bfloat16),
+        ],
+        compiler_params=PARAMS,
+        cost_estimate=LARGE,
+        name="late",
+    )(one, two, weights, *parts, peaks)
 
 
 def finish_kernel(direct, heads, index_ref, *refs):
     ins, out_ref, clip_ref = refs[:-2], refs[-2], refs[-1]
-    groups = (ins[0].shape[0] - 16) // 32
+    groups = (ins[0].shape[0] - 16) // (32 * heads)
     mine = index_ref[0]
     peak = None
     for d, source in enumerate(ins):
-        for two in range(groups // 2):
-            for pair in range(2):
-                starts = [(2 * two + k) * 32 + pair * 16 for k in range(2)]
-                a, b = (source[start : start + 16, :].astype(jnp.float32) for start in starts)
-                for k in range(2):
-                    tile = jnp.concatenate([a[8 * k : 8 * k + 8], b[8 * k : 8 * k + 8]], axis=0)
-                    frame = 2 * pair + k if d in direct else mine ^ (2 * pair + k)
-                    start = pl.multiple_of(index_ref[1 + d] * (groups * 8) + two * 16, 16)
-                    out_ref[frame, pl.ds(start, 16), :] = tile.astype(jnp.bfloat16)
-        tail = source[groups * 32 : groups * 32 + 16, :].astype(jnp.float32)
+        for h in range(heads):
+            for two in range(groups // 2):
+                for pair in range(2):
+                    starts = [(h * groups + 2 * two + k) * 32 + pair * 16 for k in range(2)]
+                    a, b = (source[start : start + 16, :].astype(jnp.float32) for start in starts)
+                    for k in range(2):
+                        tile = jnp.concatenate([a[8 * k : 8 * k + 8], b[8 * k : 8 * k + 8]], axis=0)
+                        frame = 2 * pair + k if d in direct else mine ^ (pair + 2 * k)
+                        start = pl.multiple_of(index_ref[1 + d] * (groups * 8) + two * 16, 16)
+                        out_ref[frame, pl.ds(start, 16), h * HD : (h + 1) * HD] = tile.astype(jnp.bfloat16)
+        tail = source[heads * groups * 32 :, :].astype(jnp.float32)
         values = [tail[3 * a : 3 * a + 1] + tail[3 * a + 1 : 3 * a + 2] + tail[3 * a + 2 : 3 * a + 3] for a in range(2)]
         peak = values if peak is None else [jnp.maximum(p, v) for p, v in zip(peak, values)]
     for a in range(2):
-        clip_ref[a : a + 1, :] = jnp.sqrt(clip_limit / jnp.maximum(peak[a], clip_limit))
-
-
-def finish(index, received, frames, positions, width, direct, heads):
+        clip = jnp.sqrt(clip_limit / jnp.maximum(peak[a], clip_limit))
+        clip_ref[a : a + 1, :] = jnp.concatenate([clip[:, h * TAIL : h * TAIL + 1] for h in range(heads)], axis=1)
+
+
+def finish(index, received, frames, positions, direct, heads):
     return pl.pallas_call(
         lambda *refs: finish_kernel(direct, heads, *refs),
         in_specs=[pl.BlockSpec(memory_space=pltpu.SMEM)] + [VMEM] * len(received),
         out_specs=[VMEM, VMEM],
         out_shape=[
-            jax.ShapeDtypeStruct((frames, positions, width), jnp.bfloat16),
-            jax.ShapeDtypeStruct((2, width), jnp.float32),
+            jax.ShapeDtypeStruct((frames, positions, heads * HD), jnp.bfloat16),
+            jax.ShapeDtypeStruct((2, heads), jnp.float32),
         ],
         compiler_params=PARAMS,
         name="finish",
@@ -372,8 +404,7 @@
     width = heads * HD
     rows = positions // seq
     me, mine = lax.axis_index("seq"), lax.axis_index("head")
-    token_group, direct = (4, 5, 2, 3, 1), (0, 6, 7)
-    owners = jnp.stack([me ^ d for d in range(seq)]).astype(jnp.int32)
+    token_group, direct = (3, 2, 5, 4), (6, 7, 1)
     paired = jnp.transpose(projection, (0, 2, 1, 3))
 
     def piece(frame, owner):
@@ -381,26 +412,27 @@
 
     got = [swap(piece(mine, me ^ d), "seq", seq, d) for d in token_group]
     index = jnp.stack([me ^ d for d in direct]).astype(jnp.int32)
-    weights, own, *away = early(index, patch_tokens, paired, rows, len(direct))
-    away = [swap(part, "seq", seq, d) for d, part in zip(direct[1:], away)]
+    weights, *away = early(index, patch_tokens, paired, rows, len(direct))
+    away = [swap(part, "seq", seq, d) for d, part in zip(direct, away)]
 
     *got, weights = lax.optimization_barrier([*got, weights])
     here = jnp.concatenate(got, axis=0)
     there = swap(here, "head", head, 2)
+    parts, last, peaks = space_peak(patch_tokens, paired, heads)
+    here, there, peaks = lax.optimization_barrier([here, there, peaks])
     here_other = swap(here, "head", head, 1)
-    parts, last, peaks = space_peak(patch_tokens, paired, heads)
-    first = project(here, here_other, weights)
-    there, peaks, first, *away = lax.optimization_barrier([there, peaks, first, *away])
     there_other = swap(there, "head", head, 1)
-    second = project(there, there_other, weights)
-    spots = [[(d, 0), (d, 1)] for d in direct] + [[(d, pair) for d in token_group] for pair in range(2)]
-    outs = time_attention([own, *away, first, second], spots, peaks, heads, seq)
+    first = project(me.astype(jnp.int32)[None], here, there, patch_tokens, weights)
+    spots = [[(d, 0), (d, 1)] for d in direct] + [[(d, 0) for d in token_group] + [(0, 0), (0, 1)]]
+    outs = late(here_other, there_other, weights, [*away, first], spots, peaks, heads, seq, token_group)
     *outs, parts = lax.optimization_barrier([*outs, parts])
-    received = [out if d == 0 else swap(out, "seq", seq, d) for d, out in enumerate(outs)]
+    order = (0, 1, 2, 4, 5, 6, 7, 3)
+    received = [outs[d] if d == 0 else swap(outs[d], "seq", seq, d) for d in order]
     space_out = space_attention(patch_tokens, last, parts, heads)
-    finish_index = jnp.concatenate([mine.astype(jnp.int32)[None], owners])
-    time_out, clip = finish(finish_index, received, frames, positions, width, direct, heads)
-    return space_out, time_out, clip[:, ::HD]
+    finish_index = jnp.stack([mine] + [me ^ d for d in order]).astype(jnp.int32)
+    natural = [i for i, d in enumerate(order) if d not in token_group]
+    time_out, clip = finish(finish_index, received, frames, positions, natural, heads)
+    return space_out, time_out, clip
 
 
 def mixing(scores):
@@ -439,7 +471,7 @@
 
     def body(patch_tokens, projection):
         frames, positions, _ = patch_tokens.shape
-        if seq == 8 and head == 4 and frames == 4 and positions % (16 * seq) == 0:
+        if seq == 8 and head == 4 and frames == 4 and positions % (16 * seq) == 0 and projection.shape[-1] <= 4 * HD:
             return fast_body(seq, head, patch_tokens, projection)
         return plain_body(patch_tokens, projection)
 

time: 93.8 us -> 85.5 us (0.912); the launches traced: 92.3 us -> 85.1 us
  Pallas kernels: 53.4 us -> 50.4 us
  waiting for transfers between devices: 6.61 us -> 4.01 us
    ppermute x17, waiting for transfers between devices: 6.61 us -> 4.01 us  [swap(): return lax.ppermute(value, axis, [(i, i ^ distance) for i in range(size)])]
    pallas_call x3 -> x2, Pallas kernels: 14.8 us -> 12.5 us  [the longest x1 6.67 us: late(): pl.pallas_call(lambda *refs: late_kernel(heads, spots, blocks_to, *refs),...]
    unnamed x8 -> x7, local copies, waits for them, and re-layouts: 2.71 us -> 2.69 us
  transfers between devices with their start and end apart: 17 -> 17, of which waited for: 3 -> 3; matrix products, arithmetic and copies ran while one was open for 0% -> 0% of each run, Pallas kernels for 47% -> 50%
where the time goes in v3:
time: 85.5 us; the launch traced here: 85.1 us
  Pallas kernels  50.4 us (59%)
  starting transfers between devices  25.7 us (30%)
  local copies, waits for them, and re-layouts  4.08 us (5%)
  waiting for transfers between devices  4.01 us (5%)
    ppermute x17, starting transfers between devices, swap(): return lax.ppermute(value, axis, [(i, i ^ distance) for i in range(size)])  25.7 us
    pallas_call x1, Pallas kernels, space_peak(): pl.pallas_call(lambda *refs: space_peak_kernel(heads, *refs), grid=(depth...  14.3 us
    pallas_call x1, Pallas kernels, early(): pl.pallas_call(lambda *refs: early_kernel(count, *refs), grid_spec=pltpu....  13.8 us
    pallas_call x1, Pallas kernels, space_attention(): pl.pallas_call(lambda *refs: space_kernel(heads, *refs), grid=(frames //...  8.26 us
    pallas_call x1, Pallas kernels, late(): pl.pallas_call(lambda *refs: late_kernel(heads, spots, blocks_to, *refs),...  6.67 us
    pallas_call x1, Pallas kernels, project(): pl.pallas_call(project_kernel, grid_spec=pltpu.PrefetchScalarGridSpec(num...  5.81 us
    ppermute x17, waiting for transfers between devices, swap(): return lax.ppermute(value, axis, [(i, i ^ distance) for i in range(size)])  4.01 us
    unnamed x7, local copies, waits for them, and re-layouts  2.69 us
  transfers between devices with their start and end apart: 17, of which 3 were waited for; matrix products, arithmetic and copies ran while one was open for 0% of the time, Pallas kernels for 50%

profile of v3, /device:TPU:0, one launch (start us, length us, event | category | flops | bytes accessed | tf_op | source)
XLA Modules:
  0.0 85.1 jit_solution(11720644037384836248)
XLA Ops:
  0.7 1.3 %constant_dynamic-slice_fusion = (bf16[1,32,3072]{2,1,0:T(8,128)(2,1)S(1)}, bf16[1,32,3072]{2,1,0:T(8,128)(2,1)S(1)}, bf16[1,32,3072]{2,1,0:T(8,128)(2,1)S(1)}, bf16[1,32,3072]{2,1,0:T(8,128)(2,1)S(1)}) fusion(bf16[4,256,3072]{2,1,0:T(8,128)(2,1)} %refs_0_.3, s32[]{:T(128)S(6)} %select_n.18, s32[]{:T(128)S(6)} %select_n.22, s32[]{:T(128)S(6)} %select_n.21, ...), kind=kLoop, calls=%fused_computation.4 | loop fusion | bytes 1572884 | tf_op jit(solution)/shard_map/dynamic_slice | solution.py:411
  1.9 4.0 %collective-permute-start = (bf16[1,32,3072]{2,1,0:T(8,128)(2,1)S(1)}, bf16[1,32,3072]{2,1,0:T(8,128)(2,1)S(1)}, u32[]{:S(2)}, u32[]{:S(2)}) collective-permute-start(bf16[1,32,3072]{2,1,0:T(8,128)(2,1)S(1)} %get-tuple-element.74), channel_id=1, source_target_pairs={{0,12},{4,8},{8,4},{12,0},{16,28},{20,24},{24,20},{28,16},{1,13},{... | collective-permute-start | bytes 589832 | tf_op jit(solution)/shard_map/ppermute | solution.py:398
  6.0 0.4 collective-permute-start.1
  6.4 2.6 %collective-permute-start.2 = (bf16[1,32,3072]{2,1,0:T(8,128)(2,1)S(1)}, bf16[1,32,3072]{2,1,0:T(8,128)(2,1)S(1)}, u32[]{:S(2)}, u32[]{:S(2)}) collective-permute-start(bf16[1,32,3072]{2,1,0:T(8,128)(2,1)S(1)} %get-tuple-element.72), channel_id=1, source_target_pairs={{0,20},{4,16},{8,28},{12,24},{16,4},{20,0},{24,12},{28,8},{1,21},{... | collective-permute-start | bytes 589832 | tf_op jit(solution)/shard_map/ppermute | solution.py:398
  9.0 0.0 collective-permute-start.3
  9.0 0.1 pad_add_fusion.refs_0_
  9.1 13.8 %early.1 = (bf16[3072,1152]{1,0:T(8,128)(2,1)}, bf16[4,32,1152]{2,1,0:T(8,128)(2,1)S(1)}, bf16[4,32,1152]{2,1,0:T(8,128)(2,1)S(1)}, bf16[4,32,1152]{2,1,0:T(8,128)(2,1)S(1)}) custom-call(s32[3]{0:T(128)S(1)} %pad_add_fusion.refs_0_, bf16[4,256,3072]{2,1,0:T(8,128)(2,1)} %refs_0_.3, bf16[4,256,3072]{2,1,0:T(8,128)(2,1)} %refs_0_.3, ...), custom_call_target="tpu_custom_call" | custom-call | flops 5435817984 | bytes 21233664 | tf_op jit(solution)/shard_map/early/pallas_call | solution.py:100
  22.9 0.0 collective-permute-done
  22.9 0.6 collective-permute-done.1
  23.4 0.0 collective-permute-done.2
  23.4 2.6 %collective-permute-done.3 = bf16[1,32,3072]{2,1,0:T(8,128)(2,1)S(1)} collective-permute-done((bf16[1,32,3072]{2,1,0:T(8,128)(2,1)S(1)}, bf16[1,32,3072]{2,1,0:T(8,128)(2,1)S(1)}, u32[]{:S(2)}, u32[]{:S(2)}) %collective-permute-start.3) | collective-permute-done | bytes 196640 | tf_op jit(solution)/shard_map/ppermute | solution.py:398
  26.1 1.6 %collective-permute-start.4 = (bf16[4,32,3072]{2,1,0:T(8,128)(2,1)S(1)}, bf16[4,32,3072]{2,1,0:T(8,128)(2,1)S(1)}, u32[]{:S(2)}, u32[]{:S(2)}) collective-permute-start(bf16[4,32,3072]{2,1,0:T(8,128)(2,1)S(1)} %constant_dynamic-update-slice_fusion.one_ref), channel_id=1, source_target_pairs={{0,2},{1,3},{2,0},{3,1},{4,6},{5,7},{6,4},{7,5},{8,10},{9,11},{10,... | collective-permute-start | bytes 2359304 | tf_op jit(solution)/shard_map/ppermute | solution.py:398
  27.7 4.2 %collective-permute-start.7 = (bf16[4,32,1152]{2,1,0:T(8,128)(2,1)S(1)}, bf16[4,32,1152]{2,1,0:T(8,128)(2,1)S(1)}, u32[]{:S(2)}, u32[]{:S(2)}) collective-permute-start(bf16[4,32,1152]{2,1,0:T(8,128)(2,1)S(1)} %get-tuple-element.47), channel_id=1, source_target_pairs={{0,24},{4,28},{8,16},{12,20},{16,8},{20,12},{24,0},{28,4},{1,25},{... | collective-permute-start | bytes 884744 | tf_op jit(solution)/shard_map/ppermute | solution.py:398
  31.9 1.1 %collective-permute-start.8 = (bf16[4,32,1152]{2,1,0:T(8,128)(2,1)S(1)}, bf16[4,32,1152]{2,1,0:T(8,128)(2,1)S(1)}, u32[]{:S(2)}, u32[]{:S(2)}) collective-permute-start(bf16[4,32,1152]{2,1,0:T(8,128)(2,1)S(1)} %get-tuple-element.48), channel_id=1, source_target_pairs={{0,28},{4,24},{8,20},{12,16},{16,12},{20,8},{24,4},{28,0},{1,29},{... | collective-permute-start | bytes 884744 | tf_op jit(solution)/shard_map/ppermute | solution.py:398
  33.0 0.6 collective-permute-start.9
  33.6 14.3 %space_peak.1 = (bf16[1024,768]{1,0:T(8,128)(2,1)S(1)}, bf16[3072,384]{1,0:T(8,128)(2,1)S(1)}, f32[8,384]{1,0:T(8,128)S(1)}) custom-call(bf16[4,256,3072]{2,1,0:T(8,128)(2,1)} %refs_0_.3, bf16[3072,3,2,384]{3,2,1,0:T(2,128)(2,1)} %bitcast.11), custom_call_target="tpu_custom_call" | custom-call | flops 3000000000 | bytes 8000000 | tf_op jit(solution)/shard_map/space_peak/pallas_call | solution.py:161
  47.9 1.2 %copy-done = bf16[1024,768]{1,0:T(8,128)(2,1)} copy-done((bf16[1024,768]{1,0:T(8,128)(2,1)}, bf16[1024,768]{1,0:T(8,128)(2,1)S(1)}, u32[]{:S(2)}) %copy-start) | copy-done | bytes 1572888
  49.2 0.0 collective-permute-done.4.two_ref
  49.2 0.0 collective-permute-start.5
  49.2 0.5 collective-permute-start.6
  49.7 5.8 %project.1.refs_6_ = bf16[4,96,1152]{2,1,0:T(8,128)(2,1)S(1)} custom-call(s32[1]{0:T(128)} %bitcast.4.index_ref, bf16[4,32,3072]{2,1,0:T(8,128)(2,1)S(1)} %constant_dynamic-update-slice_fusion.one_ref, bf16[4,32,3072]{2,1,0:T(8,128)(2,1)S(1)} %collective-permute-done.4.two_ref, bf16[4,256,3072]{2,1,0:T(8,128)(2,1)} %refs_0_.3, ...), custom_call_target="tpu_custom_call" | custom-call | flops 16000000000 | bytes 40000000 | tf_op jit(solution)/shard_map/project/pallas_call | solution.py:263
  55.5 0.0 collective-permute-done.7.refs_3_
  55.6 6.7 %late.1 = (bf16[400,128]{1,0:T(8,128)(2,1)S(1)}, bf16[400,128]{1,0:T(8,128)(2,1)S(1)}, bf16[400,128]{1,0:T(8,128)(2,1)S(1)}, bf16[400,128]{1,0:T(8,128)(2,1)S(1)...) custom-call(bf16[4,32,3072]{2,1,0:T(8,128)(2,1)S(1)} %collective-per, ...), custom_call_target="tpu_custom_call" | custom-call | flops 16000000000 | bytes 40000000 | tf_op jit(solution)/shard_map/late/pallas_call | solution.py:341
  62.3 1.5 %collective-permute-start.10 = (bf16[400,128]{1,0:T(8,128)(2,1)S(1)}, bf16[400,128]{1,0:T(8,128)(2,1)S(1)}, u32[]{:S(2)}, u32[]{:S(2)}) collective-permute-start(bf16[400,128]{1,0:T(8,128)(2,1)S(1)} %get-tuple-element.62), channel_id=1, source_target_pairs={{0,4},{4,0},{8,12},{12,8},{16,20},{20,16},{24,28},{28,24},{1,5},{5... | collective-permute-start | bytes 307208 | tf_op jit(solution)/shard_map/ppermute | solution.py:398
  63.8 0.1 stack.43.refs_0_
  63.9 4.4 %collective-permute-start.12 = (bf16[400,128]{1,0:T(8,128)(2,1)S(1)}, bf16[400,128]{1,0:T(8,128)(2,1)S(1)}, u32[]{:S(2)}, u32[]{:S(2)}) collective-permute-start(bf16[400,128]{1,0:T(8,128)(2,1)S(1)} %get-tuple-element.64), channel_id=1, source_target_pairs={{0,16},{4,20},{8,24},{12,28},{16,0},{20,4},{24,8},{28,12},{1,17},{... | collective-permute-start | bytes 307208 | tf_op jit(solution)/shard_map/ppermute | solution.py:398
  68.3 2.1 %collective-permute-start.14 = (bf16[400,128]{1,0:T(8,128)(2,1)S(1)}, bf16[400,128]{1,0:T(8,128)(2,1)S(1)}, u32[]{:S(2)}, u32[]{:S(2)}) collective-permute-start(bf16[400,128]{1,0:T(8,128)(2,1)S(1)} %get-tuple-element.66), channel_id=1, source_target_pairs={{0,24},{4,28},{8,16},{12,20},{16,8},{20,12},{24,0},{28,4},{1,25},{... | collective-permute-start | bytes 307208 | tf_op jit(solution)/shard_map/ppermute | solution.py:398
  70.4 2.7 %collective-permute-start.15 = (bf16[400,128]{1,0:T(8,128)(2,1)S(1)}, bf16[400,128]{1,0:T(8,128)(2,1)S(1)}, u32[]{:S(2)}, u32[]{:S(2)}) collective-permute-start(bf16[400,128]{1,0:T(8,128)(2,1)S(1)} %get-tuple-element.67), channel_id=1, source_target_pairs={{0,28},{4,24},{8,20},{12,16},{16,12},{20,8},{24,4},{28,0},{1,29},{... | collective-permute-start | bytes 307208 | tf_op jit(solution)/shard_map/ppermute | solution.py:398
  73.1 1.4 %copy-done.1 = bf16[1024,768]{1,0:T(8,128)(2,1)S(1)} copy-done((bf16[1024,768]{1,0:T(8,128)(2,1)S(1)}, bf16[1024,768]{1,0:T(8,128)(2,1)}, u32[]{:S(2)}) %copy-start.1) | copy-done | bytes 1572888
  74.5 8.3 %space_attention.1 = bf16[4,256,384]{2,1,0:T(8,128)(2,1)} custom-call(bf16[4,256,3072]{2,1,0:T(8,128)(2,1)} %refs_0_.3, bf16[3072,384]{1,0:T(8,128)(2,1)S(1)} %get-tuple-element.37.refs_1_, bf16[1024,768]{1,0:T(8,128)(2,1)S(1)} %copy-done.1), custom_call_target="tpu_custom_call" | custom-call | flops 16000000000 | bytes 40000000 | tf_op jit(solution)/shard_map/space_attention/pallas_call | solution.py:206
  82.8 0.8 collective-permute-done.16.refs_8_
  83.6 1.6 %finish.1 = (bf16[4,256,384]{2,1,0:T(8,128)(2,1)}, f32[2,3]{1,0:T(2,128)}) custom-call(s32[9]{0:T(128)S(1)} %stack.43.refs_0_, bf16[400,128]{1,0:T(8,128)(2,1)S(1)} %get-tuple-element.61.refs_1_, bf16[400,128]{1,0:T(8,128)(2,1)S(1)} %collective-permute-done.10.refs_2_, bf16[400,128]{1,0:T(8,128)(2,1)S(1)} %collective-permute-done.11.refs_3_, ...), custom_call_target="tpu_custom_call" | custom-call | tf_op jit(solution)/shard_map/finish/pallas_call | solution.py:384
  (19 shorter events, 0.1 us)
Async XLA Ops:
  1.9 20.9 %collective-permute-start = (bf16[1,32,3072]{2,1,0:T(8,128)(2,1)S(1)}, bf16[1,32,3072]{2,1,0:T(8,128)(2,1)S(1)}, u32[]{:S(2)}, u32[]{:S(2)}) collective-permute-start(bf16[1,32,3072]{2,1,0:T(8,128)(2,1)S(1)} %get-tuple-element.74), channel_id=1, source_target_pairs={{0,12},{4,8},{8,4},{12,0},{16,28},{20,24},{24,20},{28,16},{1,13},{... | collective-permute-start | bytes 589832 | tf_op jit(solution)/shard_map/ppermute | solution.py:398
  6.0 17.5 %collective-permute-start.1 = (bf16[1,32,3072]{2,1,0:T(8,128)(2,1)S(1)}, bf16[1,32,3072]{2,1,0:T(8,128)(2,1)S(1)}, u32[]{:S(2)}, u32[]{:S(2)}) collective-permute-start(bf16[1,32,3072]{2,1,0:T(8,128)(2,1)S(1)} %get-tuple-element.73), channel_id=1, source_target_pairs={{0,8},{4,12},{8,0},{12,4},{16,24},{20,28},{24,16},{28,20},{1,9},{5... | collective-permute-start | bytes 589832 | tf_op jit(solution)/shard_map/ppermute | solution.py:398
  6.4 17.0 %collective-permute-start.2 = (bf16[1,32,3072]{2,1,0:T(8,128)(2,1)S(1)}, bf16[1,32,3072]{2,1,0:T(8,128)(2,1)S(1)}, u32[]{:S(2)}, u32[]{:S(2)}) collective-permute-start(bf16[1,32,3072]{2,1,0:T(8,128)(2,1)S(1)} %get-tuple-element.72), channel_id=1, source_target_pairs={{0,20},{4,16},{8,28},{12,24},{16,4},{20,0},{24,12},{28,8},{1,21},{... | collective-permute-start | bytes 589832 | tf_op jit(solution)/shard_map/ppermute | solution.py:398
  9.0 17.1 %collective-permute-start.3 = (bf16[1,32,3072]{2,1,0:T(8,128)(2,1)S(1)}, bf16[1,32,3072]{2,1,0:T(8,128)(2,1)S(1)}, u32[]{:S(2)}, u32[]{:S(2)}) collective-permute-start(bf16[1,32,3072]{2,1,0:T(8,128)(2,1)S(1)} %get-tuple-element.71), channel_id=1, source_target_pairs={{0,16},{4,20},{8,24},{12,28},{16,0},{20,4},{24,8},{28,12},{1,17},{... | collective-permute-start | bytes 589832 | tf_op jit(solution)/shard_map/ppermute | solution.py:398
  26.1 23.1 %collective-permute-start.4 = (bf16[4,32,3072]{2,1,0:T(8,128)(2,1)S(1)}, bf16[4,32,3072]{2,1,0:T(8,128)(2,1)S(1)}, u32[]{:S(2)}, u32[]{:S(2)}) collective-permute-start(bf16[4,32,3072]{2,1,0:T(8,128)(2,1)S(1)} %constant_dynamic-update-slice_fusion.one_ref), channel_id=1, source_target_pairs={{0,2},{1,3},{2,0},{3,1},{4,6},{5,7},{6,4},{7,5},{8,10},{9,11},{10,... | collective-permute-start | bytes 2359304 | tf_op jit(solution)/shard_map/ppermute | solution.py:398
  27.7 27.8 %collective-permute-start.7 = (bf16[4,32,1152]{2,1,0:T(8,128)(2,1)S(1)}, bf16[4,32,1152]{2,1,0:T(8,128)(2,1)S(1)}, u32[]{:S(2)}, u32[]{:S(2)}) collective-permute-start(bf16[4,32,1152]{2,1,0:T(8,128)(2,1)S(1)} %get-tuple-element.47), channel_id=1, source_target_pairs={{0,24},{4,28},{8,16},{12,20},{16,8},{20,12},{24,0},{28,4},{1,25},{... | collective-permute-start | bytes 884744 | tf_op jit(solution)/shard_map/ppermute | solution.py:398
  31.9 23.6 %collective-permute-start.8 = (bf16[4,32,1152]{2,1,0:T(8,128)(2,1)S(1)}, bf16[4,32,1152]{2,1,0:T(8,128)(2,1)S(1)}, u32[]{:S(2)}, u32[]{:S(2)}) collective-permute-start(bf16[4,32,1152]{2,1,0:T(8,128)(2,1)S(1)} %get-tuple-element.48), channel_id=1, source_target_pairs={{0,28},{4,24},{8,20},{12,16},{16,12},{20,8},{24,4},{28,0},{1,29},{... | collective-permute-start | bytes 884744 | tf_op jit(solution)/shard_map/ppermute | solution.py:398
  33.0 22.5 %collective-permute-start.9 = (bf16[4,32,1152]{2,1,0:T(8,128)(2,1)S(1)}, bf16[4,32,1152]{2,1,0:T(8,128)(2,1)S(1)}, u32[]{:S(2)}, u32[]{:S(2)}) collective-permute-start(bf16[4,32,1152]{2,1,0:T(8,128)(2,1)S(1)} %get-tuple-element.49), channel_id=1, source_target_pairs={{0,4},{4,0},{8,12},{12,8},{16,20},{20,16},{24,28},{28,24},{1,5},{5... | collective-permute-start | bytes 884744 | tf_op jit(solution)/shard_map/ppermute | solution.py:398
  47.9 1.3 %copy-start = (bf16[1024,768]{1,0:T(8,128)(2,1)}, bf16[1024,768]{1,0:T(8,128)(2,1)S(1)}, u32[]{:S(2)}) copy-start(bf16[1024,768]{1,0:T(8,128)(2,1)S(1)} %get-tuple-element.60.refs_2_) | copy-start | bytes 4718596
  49.2 6.4 %collective-permute-start.5 = (bf16[4,32,3072]{2,1,0:T(8,128)(2,1)S(1)}, bf16[4,32,3072]{2,1,0:T(8,128)(2,1)S(1)}, u32[]{:S(2)}, u32[]{:S(2)}) collective-permute-start(bf16[4,32,3072]{2,1,0:T(8,128)(2,1)S(1)} %constant_dynamic-update-slice_fusion.one_ref), channel_id=1, source_target_pairs={{0,1},{1,0},{2,3},{3,2},{4,5},{5,4},{6,7},{7,6},{8,9},{9,8},{10,11... | collective-permute-start | bytes 2359304 | tf_op jit(solution)/shard_map/ppermute | solution.py:398
  49.2 6.4 %collective-permute-start.6 = (bf16[4,32,3072]{2,1,0:T(8,128)(2,1)S(1)}, bf16[4,32,3072]{2,1,0:T(8,128)(2,1)S(1)}, u32[]{:S(2)}, u32[]{:S(2)}) collective-permute-start(bf16[4,32,3072]{2,1,0:T(8,128)(2,1)S(1)} %collective-permute-done.4.two_ref), channel_id=1, source_target_pairs={{0,1},{1,0},{2,3},{3,2},{4,5},{5,4},{6,7},{7,6},{8,9},{9,8},{10,11... | collective-permute-start | bytes 2359304 | tf_op jit(solution)/shard_map/ppermute | solution.py:398
  62.3 8.1 %collective-permute-start.10 = (bf16[400,128]{1,0:T(8,128)(2,1)S(1)}, bf16[400,128]{1,0:T(8,128)(2,1)S(1)}, u32[]{:S(2)}, u32[]{:S(2)}) collective-permute-start(bf16[400,128]{1,0:T(8,128)(2,1)S(1)} %get-tuple-element.62), channel_id=1, source_target_pairs={{0,4},{4,0},{8,12},{12,8},{16,20},{20,16},{24,28},{28,24},{1,5},{5... | collective-permute-start | bytes 307208 | tf_op jit(solution)/shard_map/ppermute | solution.py:398
  63.8 9.3 %collective-permute-start.11 = (bf16[400,128]{1,0:T(8,128)(2,1)S(1)}, bf16[400,128]{1,0:T(8,128)(2,1)S(1)}, u32[]{:S(2)}, u32[]{:S(2)}) collective-permute-start(bf16[400,128]{1,0:T(8,128)(2,1)S(1)} %get-tuple-element.63), channel_id=1, source_target_pairs={{0,8},{4,12},{8,0},{12,4},{16,24},{20,28},{24,16},{28,20},{1,9},{5... | collective-permute-start | bytes 307208 | tf_op jit(solution)/shard_map/ppermute | solution.py:398
  63.9 18.9 %collective-permute-start.12 = (bf16[400,128]{1,0:T(8,128)(2,1)S(1)}, bf16[400,128]{1,0:T(8,128)(2,1)S(1)}, u32[]{:S(2)}, u32[]{:S(2)}) collective-permute-start(bf16[400,128]{1,0:T(8,128)(2,1)S(1)} %get-tuple-element.64), channel_id=1, source_target_pairs={{0,16},{4,20},{8,24},{12,28},{16,0},{20,4},{24,8},{28,12},{1,17},{... | collective-permute-start | bytes 307208 | tf_op jit(solution)/shard_map/ppermute | solution.py:398
  68.2 14.5 %collective-permute-start.13 = (bf16[400,128]{1,0:T(8,128)(2,1)S(1)}, bf16[400,128]{1,0:T(8,128)(2,1)S(1)}, u32[]{:S(2)}, u32[]{:S(2)}) collective-permute-start(bf16[400,128]{1,0:T(8,128)(2,1)S(1)} %get-tuple-element.65), channel_id=1, source_target_pairs={{0,20},{4,16},{8,28},{12,24},{16,4},{20,0},{24,12},{28,8},{1,21},{... | collective-permute-start | bytes 307208 | tf_op jit(solution)/shard_map/ppermute | solution.py:398
  68.3 14.5 %collective-permute-start.14 = (bf16[400,128]{1,0:T(8,128)(2,1)S(1)}, bf16[400,128]{1,0:T(8,128)(2,1)S(1)}, u32[]{:S(2)}, u32[]{:S(2)}) collective-permute-start(bf16[400,128]{1,0:T(8,128)(2,1)S(1)} %get-tuple-element.66), channel_id=1, source_target_pairs={{0,24},{4,28},{8,16},{12,20},{16,8},{20,12},{24,0},{28,4},{1,25},{... | collective-permute-start | bytes 307208 | tf_op jit(solution)/shard_map/ppermute | solution.py:398
  70.4 12.3 %collective-permute-start.15 = (bf16[400,128]{1,0:T(8,128)(2,1)S(1)}, bf16[400,128]{1,0:T(8,128)(2,1)S(1)}, u32[]{:S(2)}, u32[]{:S(2)}) collective-permute-start(bf16[400,128]{1,0:T(8,128)(2,1)S(1)} %get-tuple-element.67), channel_id=1, source_target_pairs={{0,28},{4,24},{8,20},{12,16},{16,12},{20,8},{24,4},{28,0},{1,29},{... | collective-permute-start | bytes 307208 | tf_op jit(solution)/shard_map/ppermute | solution.py:398
  73.1 10.5 %collective-permute-start.16 = (bf16[400,128]{1,0:T(8,128)(2,1)S(1)}, bf16[400,128]{1,0:T(8,128)(2,1)S(1)}, u32[]{:S(2)}, u32[]{:S(2)}) collective-permute-start(bf16[400,128]{1,0:T(8,128)(2,1)S(1)} %get-tuple-element.68), channel_id=1, source_target_pairs={{0,12},{4,8},{8,4},{12,0},{16,28},{20,24},{24,20},{28,16},{1,13},{... | collective-permute-start | bytes 307208 | tf_op jit(solution)/shard_map/ppermute | solution.py:398
  73.1 1.4 %copy-start.1 = (bf16[1024,768]{1,0:T(8,128)(2,1)S(1)}, bf16[1024,768]{1,0:T(8,128)(2,1)}, u32[]{:S(2)}) copy-start(bf16[1024,768]{1,0:T(8,128)(2,1)} %copy-done) | copy-start | bytes 4718596

commit v4 on v3

v4 whole, which is shorter than its diff:
```python
import math

import jax
import jax.numpy as jnp
from jax import lax
from jax.experimental import pallas as pl
from jax.experimental.pallas import tpu as pltpu
from jax.sharding import PartitionSpec as P

HD = 128
ROLES = 3
clip_limit = 30.0
score_scale = 1.0 / math.sqrt(HD)
exp_scale = score_scale * math.log2(math.e)
VMEM = pl.BlockSpec(memory_space=pltpu.VMEM)
SMALL = pl.CostEstimate(flops=3000000000, bytes_accessed=8000000, transcendentals=0)
LARGE = pl.CostEstimate(flops=16000000000, bytes_accessed=40000000, transcendentals=0)
PARAMS = pltpu.CompilerParams(vmem_limit_bytes=32 * 1024 * 1024)


def in_hbm(value):
    return pltpu.with_memory_space_constraint(value, pltpu.HBM)


def dot_nt(a, b):
    return lax.dot_general(a, b, (((1,), (1,)), ((), ())), preferred_element_type=jnp.float32)


def attend(query_part, key_part, value_part, mask=None):
    raw = dot_nt(query_part, key_part)
    if mask is not None:
        raw = jnp.where(mask, raw, -jnp.inf)
    highest = jnp.max(raw, axis=-1, keepdims=True)
    expon = jnp.exp2((raw - highest) * exp_scale)
    weights = (expon * (1.0 / jnp.sum(expon, axis=-1, keepdims=True))).astype(jnp.bfloat16)
    result = jnp.dot(weights, value_part, preferred_element_type=jnp.float32)
    return result, jnp.max(highest, axis=0, keepdims=True)


def pick_matrix(which, chunk):
    rows = lax.broadcasted_iota(jnp.int32, (ROLES * chunk, ROLES * 2 * chunk), 0)
    cols = lax.broadcasted_iota(jnp.int32, (ROLES * chunk, ROLES * 2 * chunk), 1)
    source = ((rows % chunk) * ROLES + rows // chunk) * 2 + which
    return jnp.where(cols == source, 1.0, 0.0).astype(jnp.bfloat16)


def pick(pick_ref, w_ref, out_refs):
    depth, _, _, width = w_ref.shape
    chunk = pick_ref.shape[0] // ROLES
    span = 2 * ROLES * chunk
    flat = w_ref.reshape(depth * ROLES * 2, width)
    for i in range(depth // chunk):
        found = jnp.dot(pick_ref[...], flat[i * span : (i + 1) * span, :], preferred_element_type=jnp.float32)
        found = found.astype(jnp.bfloat16)
        for r in range(ROLES):
            out_refs[r][i * chunk : (i + 1) * chunk, :] = found[r * chunk : (r + 1) * chunk]


CHUNK = 64


def early_kernel(count, rows, index_ref, tokens_ref, w_ref, out_weights_ref, flag_ref, *refs):
    outs, (held, weights_ref, pick_ref, x_ref, w_sems, out_sems, x_sems) = refs[:count], refs[count:]
    frames, _, depth = tokens_ref.shape
    block = held.shape[1]
    steps = depth // block

    def load(step):
        return pltpu.make_async_copy(w_ref.at[pl.ds(step * block, block)], held.at[step % SLOTS], w_sems.at[step % SLOTS])

    def store(step):
        here = pl.ds(step * block, block)
        return pltpu.make_async_copy(weights_ref.at[here], out_weights_ref.at[here], out_sems.at[step])

    for step in range(SLOTS - 1):
        load(step).start()
    loads = []
    for i in range(count):
        start = pl.multiple_of(index_ref[i] * rows, rows)
        for f in range(frames):
            at = i * frames + f
            loads.append(
                pltpu.make_async_copy(
                    tokens_ref.at[f, pl.ds(start, rows)], x_ref.at[pl.ds(at * rows, rows)], x_sems.at[at]
                )
            )
            loads[-1].start()
    pick_ref[...] = pick_matrix(1, CHUNK)
    for step in range(steps):
        if step + SLOTS - 1 < steps:
            load(step + SLOTS - 1).start()
        load(step).wait()
        here = pl.ds(step * block, block)
        width = held.shape[-1]
        outs_at = [weights_ref.at[here, r * width : (r + 1) * width] for r in range(ROLES)]
        pick(pick_ref, held.at[step % SLOTS], outs_at)
        store(step).start()
    for copy in loads:
        copy.wait()
    total = jnp.dot(x_ref[...], weights_ref[...], preferred_element_type=jnp.float32)
    flag_ref[...] = jnp.zeros_like(flag_ref)
    for i, out in enumerate(outs):
        for pair in range(frames // 2):
            at = (i * frames + 2 * pair) * rows
            for g in range(rows // 8):
                out[g, pair * 16 : pair * 16 + 16, :] = pair_tiles(total, at, at + rows, g)
    for step in range(steps):
        store(step).wait()


def early(index, tokens, paired, rows, count):
    frames, _, depth = tokens.shape
    width = paired.shape[-1]
    cols = ROLES * width
    block = BLOCK
    out = jax.ShapeDtypeStruct((rows // 8, frames * 8, cols), jnp.bfloat16)
    here = count * frames * rows
    return pl.pallas_call(
        lambda *refs: early_kernel(count, rows, *refs),
        in_specs=[pl.BlockSpec(memory_space=pltpu.SMEM)] + [pl.BlockSpec(memory_space=pl.ANY)] * 2,
        out_specs=[pl.BlockSpec(memory_space=pl.ANY)] + [VMEM] * (1 + count),
        out_shape=[pltpu.HBM((depth, cols), jnp.bfloat16), jax.ShapeDtypeStruct((8, HD), jnp.float32)] + [out] * count,
        scratch_shapes=[
            pltpu.VMEM((SLOTS, block, ROLES, 2, width), jnp.bfloat16),
            pltpu.VMEM((depth, cols), jnp.bfloat16),
            pltpu.VMEM((ROLES * CHUNK, 2 * ROLES * CHUNK), jnp.bfloat16),
            pltpu.VMEM((here, depth), jnp.bfloat16),
            pltpu.SemaphoreType.DMA((SLOTS,)),
            pltpu.SemaphoreType.DMA((depth // block,)),
            pltpu.SemaphoreType.DMA((count * frames,)),
        ],
        compiler_params=PARAMS,
        cost_estimate=LARGE,
        name="early",
    )(index, in_hbm(tokens), in_hbm(paired))


BLOCK = 512
SLOTS = 3
SPLITS = 3


def space_peak_kernel(heads, x_hbm, w_hbm, flag_ref, parts_hbm, last_hbm, peak_ref, *scratch):
    held, x_ref, weights_ref, last_ref, parts_ref, pick_ref, w_sems, x_sem, last_sem, parts_sem = scratch
    frames, positions, depth = x_hbm.shape
    steps, block = held.shape[:2]
    width = heads * HD
    loads = [pltpu.make_async_copy(w_hbm.at[pl.ds(i * block, block)], held.at[i], w_sems.at[i]) for i in range(steps)]
    for load in loads:
        load.start()
    load_tokens = pltpu.make_async_copy(x_hbm, x_ref, x_sem.at[0])
    load_tokens.start()
    pick_ref[...] = pick_matrix(0, CHUNK)
    for step in range(steps):
        loads[step].wait()
        here = pl.ds(step * block, block)
        outs = [weights_ref.at[here, r * width : (r + 1) * width] for r in range(2)] + [last_ref.at[here]]
        pick(pick_ref, held.at[step], outs)
    store_last = pltpu.make_async_copy(last_ref, last_hbm, last_sem.at[0])
    store_last.start()
    load_tokens.wait()
    tokens = x_ref[...].reshape(frames * positions, depth)
    parts_ref[...] = jnp.dot(tokens, weights_ref[...], preferred_element_type=jnp.float32).astype(jnp.bfloat16)
    store = pltpu.make_async_copy(parts_ref, parts_hbm, parts_sem.at[0])
    store.start()
    for h in range(heads):
        peak = jnp.full((1, 1), -jnp.inf, jnp.float32)
        for f in range(frames):
            query_part, key_part = (
                parts_ref[f * positions : (f + 1) * positions, r * width + h * HD : r * width + (h + 1) * HD]
                for r in range(2)
            )
            peak = jnp.maximum(peak, jnp.max(dot_nt(query_part, key_part), keepdims=True))
        peak_ref[:, h * HD : (h + 1) * HD] = jnp.broadcast_to(peak * score_scale, (8, HD))
    store.wait()
    store_last.wait()


def space_peak(tokens, paired, flag, heads):
    frames, positions, depth = tokens.shape
    width = heads * HD
    rows = frames * positions
    block = BLOCK
    place = pl.BlockSpec(memory_space=pl.ANY)
    return pl.pallas_call(
        lambda *refs: space_peak_kernel(heads, *refs),
        in_specs=[place] * 3,
        out_specs=[place, place, VMEM],
        out_shape=[
            pltpu.HBM((rows, 2 * width), jnp.bfloat16),
            pltpu.HBM((depth, width), jnp.bfloat16),
            jax.ShapeDtypeStruct((8, width), jnp.float32),
        ],
        scratch_shapes=[
            pltpu.VMEM((depth // block, block, ROLES, 2, width), jnp.bfloat16),
            pltpu.VMEM(tokens.shape, jnp.bfloat16),
            pltpu.VMEM((depth, 2 * width), jnp.bfloat16),
            pltpu.VMEM((depth, width), jnp.bfloat16),
            pltpu.VMEM((rows, 2 * width), jnp.bfloat16),
            pltpu.VMEM((ROLES * CHUNK, 2 * ROLES * CHUNK), jnp.bfloat16),
            pltpu.SemaphoreType.DMA((depth // block,)),
            pltpu.SemaphoreType.DMA((1,)),
            pltpu.SemaphoreType.DMA((1,)),
            pltpu.SemaphoreType.DMA((1,)),
        ],
        compiler_params=pltpu.CompilerParams(vmem_limit_bytes=46 * 1024 * 1024),
        cost_estimate=SMALL,
        name="space_peak",
    )(in_hbm(tokens), in_hbm(paired), flag)


def space_kernel(heads, x_hbm, w_hbm, parts_hbm, out_hbm, x_ref, w_ref, parts_ref, out_ref, total, x_sems, w_sems, parts_sem, out_sems):
    frames, positions, depth = x_hbm.shape
    width = heads * HD
    span = depth // SPLITS
    loads = []
    for split in range(SPLITS):
        here = pl.ds(split * span, span)
        loads.append(
            (
                pltpu.make_async_copy(w_hbm.at[here], w_ref.at[here], w_sems.at[split]),
                pltpu.make_async_copy(x_hbm.at[:, :, here], x_ref.at[:, :, here], x_sems.at[split]),
            )
        )
    loads.append([pltpu.make_async_copy(parts_hbm, parts_ref, parts_sem.at[0])])
    for group in loads:
        for copy in group:
            copy.start()
    for split in range(SPLITS):
        for copy in loads[split]:
            copy.wait()
        at = split * span
        tokens = x_ref[:, :, at : at + span].reshape(frames * positions, span)
        part = jnp.dot(tokens, w_ref[at : at + span, :], preferred_element_type=jnp.float32)
        total[...] = part if split == 0 else total[...] + part
    loads[-1][0].wait()
    stores = []
    for f in range(frames):
        rows = slice(f * positions, (f + 1) * positions)
        for h in range(heads):
            cols = [parts_ref[rows, r * width + h * HD : r * width + (h + 1) * HD] for r in range(2)]
            result, _ = attend(*cols, total[rows, h * HD : (h + 1) * HD].astype(jnp.bfloat16))
            out_ref[f, :, h * HD : (h + 1) * HD] = result.astype(jnp.bfloat16)
        stores.append(pltpu.make_async_copy(out_ref.at[f], out_hbm.at[f], out_sems.at[f]))
        stores[-1].start()
    for store in stores:
        store.wait()


def space_attention(tokens, weights, parts, heads):
    frames, positions, depth = tokens.shape
    width = heads * HD
    rows = frames * positions
    place = pl.BlockSpec(memory_space=pl.ANY)
    return pl.pallas_call(
        lambda *refs: space_kernel(heads, *refs),
        in_specs=[place] * 3,
        out_specs=place,
        out_shape=jax.ShapeDtypeStruct((frames, positions, width), jnp.bfloat16),
        scratch_shapes=[
            pltpu.VMEM(tokens.shape, jnp.bfloat16),
            pltpu.VMEM((depth, width), jnp.bfloat16),
            pltpu.VMEM((rows, 2 * width), jnp.bfloat16),
            pltpu.VMEM((frames, positions, width), jnp.bfloat16),
            pltpu.VMEM((rows, width), jnp.float32),
            pltpu.SemaphoreType.DMA((SPLITS,)),
            pltpu.SemaphoreType.DMA((SPLITS,)),
            pltpu.SemaphoreType.DMA((1,)),
            pltpu.SemaphoreType.DMA((frames,)),
        ],
        compiler_params=PARAMS,
        cost_estimate=LARGE,
        name="space_attention",
    )(in_hbm(tokens), in_hbm(weights), in_hbm(parts))


def pieces(value):
    high = value.astype(jnp.bfloat16).astype(jnp.float32)
    mid = (value - high).astype(jnp.bfloat16).astype(jnp.float32)
    return high, mid, value - high - mid


def pair_tiles(total, one, two, group):
    tile = jnp.concatenate([total[at + group * 8 : at + group * 8 + 8] for at in (one, two)], axis=0)
    return tile.astype(jnp.bfloat16)


def project_kernel(blocks, rows, one_ref, two_ref, w_ref, out_ref):
    tokens = jnp.concatenate([one_ref[...], two_ref[...]], axis=0)
    total = jnp.dot(tokens, w_ref[...], preferred_element_type=jnp.float32)
    for g in range(rows // 8):
        for b in range(blocks):
            out_ref[g, b * 16 : b * 16 + 16, :] = pair_tiles(total, b * rows, (blocks + b) * rows, g)


def project(one, two, weights):
    blocks, rows, depth = one.shape
    return pl.pallas_call(
        lambda *refs: project_kernel(blocks, rows, *refs),
        in_specs=[VMEM] * 3,
        out_specs=VMEM,
        out_shape=jax.ShapeDtypeStruct((rows // 8, blocks * 16, weights.shape[1]), jnp.bfloat16),
        compiler_params=PARAMS,
        cost_estimate=LARGE,
        name="project",
    )(*[x.reshape(-1, depth) for x in (one, two)], pltpu.with_memory_space_constraint(weights, pltpu.VMEM))


def late_kernel(heads, spots, blocks_to, rows, *refs):
    (one_ref, two_ref, w_ref), ins, peak_ref = refs[:3], refs[3 : 3 + len(spots)], refs[3 + len(spots)]
    outs, parts_ref = refs[4 + len(spots) : -1], refs[-1]
    blocks = len(blocks_to)
    tokens = jnp.concatenate([one_ref[...], two_ref[...]], axis=0)
    total = jnp.dot(tokens, w_ref[...], preferred_element_type=jnp.float32)
    for b in range(blocks):
        for g in range(rows // 8):
            parts_ref[g, b * 16 : b * 16 + 16, :] = pair_tiles(total, b * rows, (blocks + b) * rows, g)
    places = [place for spot in spots for place in spot] + [(d, 1) for d in blocks_to]
    attend_time(heads, places, [*ins, parts_ref], peak_ref, outs)


def attend_time(heads, spots, ins, peak_ref, outs):
    groups = ins[0].shape[0]
    width = heads * HD
    size = 16 * len(spots)
    row = lax.broadcasted_iota(jnp.int32, (size, size), 0)
    col = lax.broadcasted_iota(jnp.int32, (size, size), 1)
    mask = ((row ^ col) & 7) == 0
    line = lax.broadcasted_iota(jnp.int32, (16, HD), 0)
    lane = lax.broadcasted_iota(jnp.int32, (16, HD), 1) // TAIL
    tail = jnp.zeros((16, HD), jnp.float32)
    for h in range(heads):
        peak = jnp.full((1, 1), -jnp.inf, jnp.float32)
        for g in range(groups):
            cols = []
            for r in range(ROLES):
                at = r * width + h * HD
                cols.append(jnp.concatenate([x[g, :, at : at + HD] for x in ins], axis=0))
            result, highest = attend(*cols, mask)
            peak = jnp.maximum(peak, highest * score_scale)
            result = result.astype(jnp.bfloat16)
            for i, (out, pair) in enumerate(spots):
                start = (h * groups + g) * 32 + pair * 16
                outs[out][start : start + 16, :] = result[i * 16 : i * 16 + 16]
        both = pieces(peak_ref[0:1, h * HD : (h + 1) * HD]) + pieces(jnp.broadcast_to(peak, (1, HD)))
        for i, value in enumerate(both):
            tail = jnp.where((line == i) & (lane == h), value, tail)
    for out in outs:
        out[heads * groups * 32 :, :] = tail.astype(jnp.bfloat16)


TAIL = 32


def late(one, two, weights, parts, spots, peaks, heads, count, blocks_to):
    blocks, rows, depth = one.shape
    cols = weights.shape[1]
    groups = rows // 8
    shape = (heads * groups * 32 + 16, HD)
    return pl.pallas_call(
        lambda *refs: late_kernel(heads, spots, blocks_to, rows, *refs),
        in_specs=[VMEM] * (4 + len(parts)),
        out_specs=[VMEM] * count,
        out_shape=[jax.ShapeDtypeStruct(shape, jnp.bfloat16)] * count,
        scratch_shapes=[
            pltpu.VMEM((groups, blocks * 16, cols), jnp.bfloat16),
        ],
        compiler_params=PARAMS,
        cost_estimate=LARGE,
        name="late",
    )(
        *[x.reshape(-1, depth) for x in (one, two)],
        pltpu.with_memory_space_constraint(weights, pltpu.VMEM),
        *parts,
        peaks,
    )


def finish_kernel(direct, heads, index_ref, *refs):
    ins, out_ref, clip_ref = refs[:-2], refs[-2], refs[-1]
    groups = (ins[0].shape[0] - 16) // (32 * heads)
    mine = index_ref[0]
    peak = None
    for d, source in enumerate(ins):
        for h in range(heads):
            for two in range(groups // 2):
                for pair in range(2):
                    starts = [(h * groups + 2 * two + k) * 32 + pair * 16 for k in range(2)]
                    a, b = (source[start : start + 16, :].astype(jnp.float32) for start in starts)
                    for k in range(2):
                        tile = jnp.concatenate([a[8 * k : 8 * k + 8], b[8 * k : 8 * k + 8]], axis=0)
                        frame = 2 * pair + k if d in direct else mine ^ (pair + 2 * k)
                        start = pl.multiple_of(index_ref[1 + d] * (groups * 8) + two * 16, 16)
                        out_ref[frame, pl.ds(start, 16), h * HD : (h + 1) * HD] = tile.astype(jnp.bfloat16)
        tail = source[heads * groups * 32 :, :].astype(jnp.float32)
        values = [tail[3 * a : 3 * a + 1] + tail[3 * a + 1 : 3 * a + 2] + tail[3 * a + 2 : 3 * a + 3] for a in range(2)]
        peak = values if peak is None else [jnp.maximum(p, v) for p, v in zip(peak, values)]
    for a in range(2):
        clip = jnp.sqrt(clip_limit / jnp.maximum(peak[a], clip_limit))
        clip_ref[a : a + 1, :] = jnp.concatenate([clip[:, h * TAIL : h * TAIL + 1] for h in range(heads)], axis=1)


def finish(index, received, frames, positions, direct, heads):
    return pl.pallas_call(
        lambda *refs: finish_kernel(direct, heads, *refs),
        in_specs=[pl.BlockSpec(memory_space=pltpu.SMEM)] + [VMEM] * len(received),
        out_specs=[VMEM, VMEM],
        out_shape=[
            jax.ShapeDtypeStruct((frames, positions, heads * HD), jnp.bfloat16),
            jax.ShapeDtypeStruct((2, heads), jnp.float32),
        ],
        compiler_params=PARAMS,
        name="finish",
    )(index, *received)


def swap(value, axis, size, distance):
    return lax.ppermute(value, axis, [(i, i ^ distance) for i in range(size)])


def fast_body(seq, head, patch_tokens, projection):
    frames, positions, depth = patch_tokens.shape
    heads = projection.shape[-1] // HD
    width = heads * HD
    rows = positions // seq
    me, mine = lax.axis_index("seq"), lax.axis_index("head")
    token_group, direct = (3, 2, 5, 4), (6, 7, 1)
    paired = jnp.transpose(projection, (0, 2, 1, 3))

    def piece(frame, owner):
        return lax.dynamic_slice(patch_tokens, (frame, owner * rows, 0), (1, rows, depth))

    got = [swap(piece(mine, me ^ d), "seq", seq, d) for d in token_group]
    index = jnp.stack([me ^ d for d in (*direct, 0)]).astype(jnp.int32)
    weights, flag, *away, own = early(index, patch_tokens, paired, rows, len(direct) + 1)
    away = [swap(part, "seq", seq, d) for d, part in zip(direct, away)]

    *got, flag = lax.optimization_barrier([*got, flag])
    here = jnp.concatenate(got, axis=0)
    there = swap(here, "head", head, 2)
    parts, last, peaks = space_peak(patch_tokens, paired, flag, heads)
    here, there, peaks = lax.optimization_barrier([here, there, peaks])
    here_other = swap(here, "head", head, 1)
    there_other = swap(there, "head", head, 1)
    first = project(here, there, weights)
    spots = [[(d, 0), (d, 1)] for d in (*direct, 0)] + [[(d, 0) for d in token_group]]
    outs = late(here_other, there_other, weights, [*away, own, first], spots, peaks, heads, seq, token_group)
    *outs, parts = lax.optimization_barrier([*outs, parts])
    order = (0, 1, 2, 4, 5, 6, 7, 3)
    received = [outs[d] if d == 0 else swap(outs[d], "seq", seq, d) for d in order]
    space_out = space_attention(patch_tokens, last, parts, heads)
    finish_index = jnp.stack([mine] + [me ^ d for d in order]).astype(jnp.int32)
    natural = [i for i, d in enumerate(order) if d not in token_group]
    time_out, clip = finish(finish_index, received, frames, positions, natural, heads)
    return space_out, time_out, clip


def mixing(scores):
    highest = jnp.max(scores, axis=-1, keepdims=True)
    expon = jnp.exp(scores - highest)
    return (expon / jnp.sum(expon, axis=-1, keepdims=True)).astype(jnp.bfloat16)


def plain_attention(form, query_part, key_part, value_part):
    scores = jnp.einsum(form[0], query_part, key_part, preferred_element_type=jnp.float32) * score_scale
    result = jnp.einsum(form[1], mixing(scores), value_part, preferred_element_type=jnp.float32)
    return result.astype(jnp.bfloat16), jnp.max(scores, axis=(0, 2, 3))


def plain_body(patch_tokens, projection):
    frames, positions, depth = patch_tokens.shape
    heads = projection.shape[-1] // HD
    parts = jnp.dot(
        patch_tokens.reshape(-1, depth), projection.reshape(depth, -1), preferred_element_type=jnp.float32
    )
    parts = parts.astype(jnp.bfloat16).reshape(frames, positions, 2, ROLES, heads, HD)
    space_out, space_high = plain_attention(
        ("fihd,fjhd->fhij", "fhij,fjhd->fihd"), *(parts[:, :, 0, r] for r in range(ROLES))
    )
    moved = [lax.all_to_all(parts[:, :, 1, r], "seq", split_axis=1, concat_axis=0, tiled=True) for r in range(ROLES)]
    time_out, time_high = plain_attention(("fphd,gphd->phfg", "phfg,gphd->fphd"), *moved)
    time_out = lax.all_to_all(time_out, "seq", split_axis=0, concat_axis=1, tiled=True)
    peak = lax.pmax(jnp.stack([space_high, time_high]), "seq")
    clip_factor = jnp.sqrt(clip_limit / jnp.maximum(peak, clip_limit))
    flat = (frames, positions, heads * HD)
    return space_out.reshape(flat), time_out.reshape(flat), clip_factor


def solution(mesh):
    seq, head = mesh.shape["seq"], mesh.shape["head"]

    def body(patch_tokens, projection):
        frames, positions, _ = patch_tokens.shape
        if seq == 8 and head == 4 and frames == 4 and positions % (16 * seq) == 0 and projection.shape[-1] <= 4 * HD:
            return fast_body(seq, head, patch_tokens, projection)
        return plain_body(patch_tokens, projection)

    return jax.shard_map(
        body,
        mesh=mesh,
        in_specs=(P("seq", None, None), P(None, None, None, "head")),
        out_specs=(P("seq", None, "head"), P("seq", None, "head"), P(None, "head")),
        check_vma=False,
    )
```

time: 85.5 us -> 79.4 us (0.929)
  Pallas kernels: 50.4 us -> 44.7 us
  local copies, waits for them, and re-layouts: 4.08 us -> 1.43 us
  starting transfers between devices: 25.7 us -> 28.3 us
    pallas_call x5, Pallas kernels: 48.9 us -> 43.1 us  [the longest x1 14.6 us: space_peak(): pl.pallas_call(lambda *refs: space_peak_kernel(heads, *refs), in_specs=[p...]
    unnamed x7, local copies, waits for them, and re-layouts: 2.69 us -> 0.05 us
    ppermute x17, starting transfers between devices: 25.7 us -> 28.3 us  [swap(): return lax.ppermute(value, axis, [(i, i ^ distance) for i in range(size)])]
  transfers between devices with their start and end apart: 17 -> 17, of which waited for: 3 -> 5; matrix products, arithmetic and copies ran while one was open for 0% -> 0% of each run, Pallas kernels for 50% -> 50%
where the time goes in v4:
time: 79.4 us; the launch traced here: 78.6 us
  Pallas kernels  44.7 us (56%)
  starting transfers between devices  28.3 us (36%)
  waiting for transfers between devices  3.34 us (4%)
  local copies, waits for them, and re-layouts  1.43 us (2%)
  between operations  0.8 us (1%)
    ppermute x17, starting transfers between devices, swap(): return lax.ppermute(value, axis, [(i, i ^ distance) for i in range(size)])  28.3 us
    pallas_call x1, Pallas kernels, space_peak(): pl.pallas_call(lambda *refs: space_peak_kernel(heads, *refs), in_specs=[p...  14.6 us
    pallas_call x1, Pallas kernels, early(): pl.pallas_call(lambda *refs: early_kernel(count, rows, *refs), in_specs=[...  14 us
    pallas_call x1, Pallas kernels, space_attention(): pl.pallas_call(lambda *refs: space_kernel(heads, *refs), in_specs=[place]...  8.14 us
    pallas_call x1, Pallas kernels, late(): pl.pallas_call(lambda *refs: late_kernel(heads, spots, blocks_to, rows, *...  4.1 us
    ppermute x17, waiting for transfers between devices, swap(): return lax.ppermute(value, axis, [(i, i ^ distance) for i in range(size)])  3.34 us
    pallas_call x1, Pallas kernels, project(): pl.pallas_call(lambda *refs: project_kernel(blocks, rows, *refs), in_spec...  2.2 us
  transfers between devices with their start and end apart: 17, of which 5 were waited for; matrix products, arithmetic and copies ran while one was open for 0% of the time, Pallas kernels for 50%

profile of v4, /device:TPU:0, one launch (start us, length us, event | category | flops | bytes accessed | tf_op | source)
XLA Modules:
  0.0 78.6 jit_solution(7659597776154597201)
XLA Ops:
  0.7 1.3 %constant_dynamic-slice_fusion = (bf16[1,32,3072]{2,1,0:T(8,128)(2,1)S(1)}, bf16[1,32,3072]{2,1,0:T(8,128)(2,1)S(1)}, bf16[1,32,3072]{2,1,0:T(8,128)(2,1)S(1)}, bf16[1,32,3072]{2,1,0:T(8,128)(2,1)S(1)}) fusion(bf16[4,256,3072]{2,1,0:T(8,128)(2,1)} %refs_0_.3, s32[]{:T(128)S(6)} %select_n.18, s32[]{:T(128)S(6)} %select_n.22, s32[]{:T(128)S(6)} %select_n.21, ...), kind=kLoop, calls=%fused_computation.4 | loop fusion | bytes 1572884 | tf_op jit(solution)/shard_map/dynamic_slice | solution.py:431
  1.9 4.1 %collective-permute-start.3 = (bf16[1,32,3072]{2,1,0:T(8,128)(2,1)S(1)}, bf16[1,32,3072]{2,1,0:T(8,128)(2,1)S(1)}, u32[]{:S(2)}, u32[]{:S(2)}) collective-permute-start(bf16[1,32,3072]{2,1,0:T(8,128)(2,1)S(1)} %get-tuple-element.75), channel_id=1, source_target_pairs={{0,16},{4,20},{8,24},{12,28},{16,0},{20,4},{24,8},{28,12},{1,17},{... | collective-permute-start | bytes 589832 | tf_op jit(solution)/shard_map/ppermute | solution.py:418
  6.0 1.3 %collective-permute-start.2 = (bf16[1,32,3072]{2,1,0:T(8,128)(2,1)S(1)}, bf16[1,32,3072]{2,1,0:T(8,128)(2,1)S(1)}, u32[]{:S(2)}, u32[]{:S(2)}) collective-permute-start(bf16[1,32,3072]{2,1,0:T(8,128)(2,1)S(1)} %get-tuple-element.76), channel_id=1, source_target_pairs={{0,20},{4,16},{8,28},{12,24},{16,4},{20,0},{24,12},{28,8},{1,21},{... | collective-permute-start | bytes 589832 | tf_op jit(solution)/shard_map/ppermute | solution.py:418
  7.3 1.6 %collective-permute-start.1 = (bf16[1,32,3072]{2,1,0:T(8,128)(2,1)S(1)}, bf16[1,32,3072]{2,1,0:T(8,128)(2,1)S(1)}, u32[]{:S(2)}, u32[]{:S(2)}) collective-permute-start(bf16[1,32,3072]{2,1,0:T(8,128)(2,1)S(1)} %get-tuple-element.77), channel_id=1, source_target_pairs={{0,8},{4,12},{8,0},{12,4},{16,24},{20,28},{24,16},{28,20},{1,9},{5... | collective-permute-start | bytes 589832 | tf_op jit(solution)/shard_map/ppermute | solution.py:418
  8.9 0.2 collective-permute-start
  9.0 0.1 pad_add_fusion.refs_0_
  9.1 14.0 %early.1 = (bf16[3072,1152]{1,0:T(8,128)(2,1)}, f32[8,128]{1,0:T(8,128)S(1)}, bf16[4,32,1152]{2,1,0:T(8,128)(2,1)S(1)}, bf16[4,32,1152]{2,1,0:T(8,128)(2,1)S(1)}...) custom-call(s32[4]{0:T(128)S(1)} %pad_add_fusion.refs_0_, bf16[4,256,3072]{2,1,0:T(8,128)(2,1)} %refs_0_.3, ...), custom_call_target="tpu_custom_call" | custom-call | flops 16000000000 | bytes 40000000 | tf_op jit(solution)/shard_map/early/pallas_call | solution.py:118
  23.2 0.0 collective-permute-done.3
  23.2 1.5 %collective-permute-done.2 = bf16[1,32,3072]{2,1,0:T(8,128)(2,1)S(1)} collective-permute-done((bf16[1,32,3072]{2,1,0:T(8,128)(2,1)S(1)}, bf16[1,32,3072]{2,1,0:T(8,128)(2,1)S(1)}, u32[]{:S(2)}, u32[]{:S(2)}) %collective-permute-start.2) | collective-permute-done | bytes 196640 | tf_op jit(solution)/shard_map/ppermute | solution.py:418
  24.7 0.0 collective-permute-done.1
  24.7 0.2 collective-permute-done
  25.0 1.6 %collective-permute-start.4 = (bf16[4,32,3072]{2,1,0:T(8,128)(2,1)S(1)}, bf16[4,32,3072]{2,1,0:T(8,128)(2,1)S(1)}, u32[]{:S(2)}, u32[]{:S(2)}) collective-permute-start(bf16[4,32,3072]{2,1,0:T(8,128)(2,1)S(1)} %constant_dynamic-update-slice_fusion), channel_id=1, source_target_pairs={{0,2},{1,3},{2,0},{3,1},{4,6},{5,7},{6,4},{7,5},{8,10},{9,11},{10,... | collective-permute-start | bytes 2359304 | tf_op jit(solution)/shard_map/ppermute | solution.py:418
  26.6 4.6 %collective-permute-start.7 = (bf16[4,32,1152]{2,1,0:T(8,128)(2,1)S(1)}, bf16[4,32,1152]{2,1,0:T(8,128)(2,1)S(1)}, u32[]{:S(2)}, u32[]{:S(2)}) collective-permute-start(bf16[4,32,1152]{2,1,0:T(8,128)(2,1)S(1)} %get-tuple-element.50), channel_id=1, source_target_pairs={{0,24},{4,28},{8,16},{12,20},{16,8},{20,12},{24,0},{28,4},{1,25},{... | collective-permute-start | bytes 884744 | tf_op jit(solution)/shard_map/ppermute | solution.py:418
  31.2 0.9 %collective-permute-start.8 = (bf16[4,32,1152]{2,1,0:T(8,128)(2,1)S(1)}, bf16[4,32,1152]{2,1,0:T(8,128)(2,1)S(1)}, u32[]{:S(2)}, u32[]{:S(2)}) collective-permute-start(bf16[4,32,1152]{2,1,0:T(8,128)(2,1)S(1)} %get-tuple-element.51), channel_id=1, source_target_pairs={{0,28},{4,24},{8,20},{12,16},{16,12},{20,8},{24,4},{28,0},{1,29},{... | collective-permute-start | bytes 884744 | tf_op jit(solution)/shard_map/ppermute | solution.py:418
  32.1 0.6 collective-permute-start.9
  32.7 14.6 %space_peak.1 = (bf16[1024,768]{1,0:T(8,128)(2,1)}, bf16[3072,384]{1,0:T(8,128)(2,1)}, f32[8,384]{1,0:T(8,128)S(1)}) custom-call(bf16[4,256,3072]{2,1,0:T(8,128)(2,1)} %refs_0_.3, bf16[3072,3,2,384]{3,2,1,0:T(2,128)(2,1)} %bitcast.21, f32[8,128]{1,0:T(8,128)S(1)} %get-tuple-element.40.refs_2_), custom_call_target="tpu_custom_call" | custom-call | flops 3000000000 | bytes 8000000 | tf_op jit(solution)/shard_map/space_peak/pallas_call | solution.py:185
  47.3 0.1 collective-permute-start.5
  47.4 0.5 collective-permute-start.6
  47.9 2.2 %project.1.refs_7_ = bf16[4,64,1152]{2,1,0:T(8,128)(2,1)S(1)} custom-call(bf16[128,3072]{1,0:T(8,128)(2,1)S(1)} %bitcast.14, bf16[128,3072]{1,0:T(8,128)(2,1)S(1)} %bitcast.15, bf16[3072,1152]{1,0:T(8,128)(2,1)S(1)} %bitcast.19), custom_call_target="tpu_custom_call" | custom-call | flops 16000000000 | bytes 40000000 | tf_op jit(solution)/shard_map/project/pallas_call | solution.py:298
  50.2 0.7 collective-permute-done.6
  50.8 4.1 %late.1 = (bf16[400,128]{1,0:T(8,128)(2,1)S(1)}, bf16[400,128]{1,0:T(8,128)(2,1)S(1)}, bf16[400,128]{1,0:T(8,128)(2,1)S(1)}, bf16[400,128]{1,0:T(8,128)(2,1)S(1)...) custom-call(bf16[128,3072]{1,0:T(8,128)(2,1)S(1)} %bitcast.16, ...), custom_call_target="tpu_custom_call" | custom-call | flops 16000000000 | bytes 40000000 | tf_op jit(solution)/shard_map/late/pallas_call | solution.py:360
  54.9 1.9 %collective-permute-start.10 = (bf16[400,128]{1,0:T(8,128)(2,1)S(1)}, bf16[400,128]{1,0:T(8,128)(2,1)S(1)}, u32[]{:S(2)}, u32[]{:S(2)}) collective-permute-start(bf16[400,128]{1,0:T(8,128)(2,1)S(1)} %get-tuple-element.66), channel_id=1, source_target_pairs={{0,4},{4,0},{8,12},{12,8},{16,20},{20,16},{24,28},{28,24},{1,5},{5... | collective-permute-start | bytes 307208 | tf_op jit(solution)/shard_map/ppermute | solution.py:418
  56.8 3.4 %collective-permute-start.11 = (bf16[400,128]{1,0:T(8,128)(2,1)S(1)}, bf16[400,128]{1,0:T(8,128)(2,1)S(1)}, u32[]{:S(2)}, u32[]{:S(2)}) collective-permute-start(bf16[400,128]{1,0:T(8,128)(2,1)S(1)} %get-tuple-element.67), channel_id=1, source_target_pairs={{0,8},{4,12},{8,0},{12,4},{16,24},{20,28},{24,16},{28,20},{1,9},{5... | collective-permute-start | bytes 307208 | tf_op jit(solution)/shard_map/ppermute | solution.py:418
  60.2 0.1 stack.47.refs_0_
  60.3 1.0 %collective-permute-start.12 = (bf16[400,128]{1,0:T(8,128)(2,1)S(1)}, bf16[400,128]{1,0:T(8,128)(2,1)S(1)}, u32[]{:S(2)}, u32[]{:S(2)}) collective-permute-start(bf16[400,128]{1,0:T(8,128)(2,1)S(1)} %get-tuple-element.68), channel_id=1, source_target_pairs={{0,16},{4,20},{8,24},{12,28},{16,0},{20,4},{24,8},{28,12},{1,17},{... | collective-permute-start | bytes 307208 | tf_op jit(solution)/shard_map/ppermute | solution.py:418
  61.2 2.0 %collective-permute-start.13 = (bf16[400,128]{1,0:T(8,128)(2,1)S(1)}, bf16[400,128]{1,0:T(8,128)(2,1)S(1)}, u32[]{:S(2)}, u32[]{:S(2)}) collective-permute-start(bf16[400,128]{1,0:T(8,128)(2,1)S(1)} %get-tuple-element.69), channel_id=1, source_target_pairs={{0,20},{4,16},{8,28},{12,24},{16,4},{20,0},{24,12},{28,8},{1,21},{... | collective-permute-start | bytes 307208 | tf_op jit(solution)/shard_map/ppermute | solution.py:418
  63.2 1.9 %collective-permute-start.14 = (bf16[400,128]{1,0:T(8,128)(2,1)S(1)}, bf16[400,128]{1,0:T(8,128)(2,1)S(1)}, u32[]{:S(2)}, u32[]{:S(2)}) collective-permute-start(bf16[400,128]{1,0:T(8,128)(2,1)S(1)} %get-tuple-element.70), channel_id=1, source_target_pairs={{0,24},{4,28},{8,16},{12,20},{16,8},{20,12},{24,0},{28,4},{1,25},{... | collective-permute-start | bytes 307208 | tf_op jit(solution)/shard_map/ppermute | solution.py:418
  65.1 2.8 %collective-permute-start.15 = (bf16[400,128]{1,0:T(8,128)(2,1)S(1)}, bf16[400,128]{1,0:T(8,128)(2,1)S(1)}, u32[]{:S(2)}, u32[]{:S(2)}) collective-permute-start(bf16[400,128]{1,0:T(8,128)(2,1)S(1)} %get-tuple-element.71), channel_id=1, source_target_pairs={{0,28},{4,24},{8,20},{12,16},{16,12},{20,8},{24,4},{28,0},{1,29},{... | collective-permute-start | bytes 307208 | tf_op jit(solution)/shard_map/ppermute | solution.py:418
  67.9 8.1 %space_attention.1 = bf16[4,256,384]{2,1,0:T(8,128)(2,1)} custom-call(bf16[4,256,3072]{2,1,0:T(8,128)(2,1)} %refs_0_.3, bf16[3072,384]{1,0:T(8,128)(2,1)} %get-tuple-element.41.refs_1_, bf16[1024,768]{1,0:T(8,128)(2,1)} %get-tuple-element.64.refs_2_), custom_call_target="tpu_custom_call" | custom-call | flops 16000000000 | bytes 40000000 | tf_op jit(solution)/shard_map/space_attention/pallas_call | solution.py:255
  76.1 0.6 collective-permute-done.13.refs_5_
  76.7 0.3 collective-permute-done.16.refs_8_
  77.0 1.6 %finish.1 = (bf16[4,256,384]{2,1,0:T(8,128)(2,1)}, f32[2,3]{1,0:T(2,128)}) custom-call(s32[9]{0:T(128)S(1)} %stack.47.refs_0_, bf16[400,128]{1,0:T(8,128)(2,1)S(1)} %get-tuple-element.65.refs_1_, bf16[400,128]{1,0:T(8,128)(2,1)S(1)} %collective-permute-done.10.refs_2_, bf16[400,128]{1,0:T(8,128)(2,1)S(1)} %collective-permute-done.11.refs_3_, ...), custom_call_target="tpu_custom_call" | custom-call | tf_op jit(solution)/shard_map/finish/pallas_call | solution.py:404
  (20 shorter events, 0.1 us)
Async XLA Ops:
  1.9 21.2 %collective-permute-start.3 = (bf16[1,32,3072]{2,1,0:T(8,128)(2,1)S(1)}, bf16[1,32,3072]{2,1,0:T(8,128)(2,1)S(1)}, u32[]{:S(2)}, u32[]{:S(2)}) collective-permute-start(bf16[1,32,3072]{2,1,0:T(8,128)(2,1)S(1)} %get-tuple-element.75), channel_id=1, source_target_pairs={{0,16},{4,20},{8,24},{12,28},{16,0},{20,4},{24,8},{28,12},{1,17},{... | collective-permute-start | bytes 589832 | tf_op jit(solution)/shard_map/ppermute | solution.py:418
  6.0 18.6 %collective-permute-start.2 = (bf16[1,32,3072]{2,1,0:T(8,128)(2,1)S(1)}, bf16[1,32,3072]{2,1,0:T(8,128)(2,1)S(1)}, u32[]{:S(2)}, u32[]{:S(2)}) collective-permute-start(bf16[1,32,3072]{2,1,0:T(8,128)(2,1)S(1)} %get-tuple-element.76), channel_id=1, source_target_pairs={{0,20},{4,16},{8,28},{12,24},{16,4},{20,0},{24,12},{28,8},{1,21},{... | collective-permute-start | bytes 589832 | tf_op jit(solution)/shard_map/ppermute | solution.py:418
  7.3 17.4 %collective-permute-start.1 = (bf16[1,32,3072]{2,1,0:T(8,128)(2,1)S(1)}, bf16[1,32,3072]{2,1,0:T(8,128)(2,1)S(1)}, u32[]{:S(2)}, u32[]{:S(2)}) collective-permute-start(bf16[1,32,3072]{2,1,0:T(8,128)(2,1)S(1)} %get-tuple-element.77), channel_id=1, source_target_pairs={{0,8},{4,12},{8,0},{12,4},{16,24},{20,28},{24,16},{28,20},{1,9},{5... | collective-permute-start | bytes 589832 | tf_op jit(solution)/shard_map/ppermute | solution.py:418
  8.9 16.0 %collective-permute-start = (bf16[1,32,3072]{2,1,0:T(8,128)(2,1)S(1)}, bf16[1,32,3072]{2,1,0:T(8,128)(2,1)S(1)}, u32[]{:S(2)}, u32[]{:S(2)}) collective-permute-start(bf16[1,32,3072]{2,1,0:T(8,128)(2,1)S(1)} %get-tuple-element.78), channel_id=1, source_target_pairs={{0,12},{4,8},{8,4},{12,0},{16,28},{20,24},{24,20},{28,16},{1,13},{... | collective-permute-start | bytes 589832 | tf_op jit(solution)/shard_map/ppermute | solution.py:418
  25.0 22.3 %collective-permute-start.4 = (bf16[4,32,3072]{2,1,0:T(8,128)(2,1)S(1)}, bf16[4,32,3072]{2,1,0:T(8,128)(2,1)S(1)}, u32[]{:S(2)}, u32[]{:S(2)}) collective-permute-start(bf16[4,32,3072]{2,1,0:T(8,128)(2,1)S(1)} %constant_dynamic-update-slice_fusion), channel_id=1, source_target_pairs={{0,2},{1,3},{2,0},{3,1},{4,6},{5,7},{6,4},{7,5},{8,10},{9,11},{10,... | collective-permute-start | bytes 2359304 | tf_op jit(solution)/shard_map/ppermute | solution.py:418
  26.6 23.5 %collective-permute-start.7 = (bf16[4,32,1152]{2,1,0:T(8,128)(2,1)S(1)}, bf16[4,32,1152]{2,1,0:T(8,128)(2,1)S(1)}, u32[]{:S(2)}, u32[]{:S(2)}) collective-permute-start(bf16[4,32,1152]{2,1,0:T(8,128)(2,1)S(1)} %get-tuple-element.50), channel_id=1, source_target_pairs={{0,24},{4,28},{8,16},{12,20},{16,8},{20,12},{24,0},{28,4},{1,25},{... | collective-permute-start | bytes 884744 | tf_op jit(solution)/shard_map/ppermute | solution.py:418
  31.2 19.0 %collective-permute-start.8 = (bf16[4,32,1152]{2,1,0:T(8,128)(2,1)S(1)}, bf16[4,32,1152]{2,1,0:T(8,128)(2,1)S(1)}, u32[]{:S(2)}, u32[]{:S(2)}) collective-permute-start(bf16[4,32,1152]{2,1,0:T(8,128)(2,1)S(1)} %get-tuple-element.51), channel_id=1, source_target_pairs={{0,28},{4,24},{8,20},{12,16},{16,12},{20,8},{24,4},{28,0},{1,29},{... | collective-permute-start | bytes 884744 | tf_op jit(solution)/shard_map/ppermute | solution.py:418
  32.1 15.8 %slice-start = ((s8[7077888]{0:T(1024)(128)(4,1)}), s8[4194304]{0:T(1024)(128)(4,1)S(1)}, s32[]{:S(2)}) async-start(s8[7077888]{0:T(1024)(128)(4,1)} %bitcast.18), calls=%async_computation | async-start | bytes 8388608
  32.1 15.8 %slice-start.1 = ((s8[7077888]{0:T(1024)(128)(4,1)}), s8[2883584]{0:T(1024)(128)(4,1)S(1)}, s32[]{:S(2)}) async-start(s8[7077888]{0:T(1024)(128)(4,1)} %bitcast.18), calls=%async_computation.1 | async-start | bytes 5767168
  32.1 18.0 %collective-permute-start.9 = (bf16[4,32,1152]{2,1,0:T(8,128)(2,1)S(1)}, bf16[4,32,1152]{2,1,0:T(8,128)(2,1)S(1)}, u32[]{:S(2)}, u32[]{:S(2)}) collective-permute-start(bf16[4,32,1152]{2,1,0:T(8,128)(2,1)S(1)} %get-tuple-element.52), channel_id=1, source_target_pairs={{0,4},{4,0},{8,12},{12,8},{16,20},{20,16},{24,28},{28,24},{1,5},{5... | collective-permute-start | bytes 884744 | tf_op jit(solution)/shard_map/ppermute | solution.py:418
  47.3 2.8 %collective-permute-start.5 = (bf16[4,32,3072]{2,1,0:T(8,128)(2,1)S(1)}, bf16[4,32,3072]{2,1,0:T(8,128)(2,1)S(1)}, u32[]{:S(2)}, u32[]{:S(2)}) collective-permute-start(bf16[4,32,3072]{2,1,0:T(8,128)(2,1)S(1)} %constant_dynamic-update-slice_fusion), channel_id=1, source_target_pairs={{0,1},{1,0},{2,3},{3,2},{4,5},{5,4},{6,7},{7,6},{8,9},{9,8},{10,11... | collective-permute-start | bytes 2359304 | tf_op jit(solution)/shard_map/ppermute | solution.py:418
  47.4 3.4 %collective-permute-start.6 = (bf16[4,32,3072]{2,1,0:T(8,128)(2,1)S(1)}, bf16[4,32,3072]{2,1,0:T(8,128)(2,1)S(1)}, u32[]{:S(2)}, u32[]{:S(2)}) collective-permute-start(bf16[4,32,3072]{2,1,0:T(8,128)(2,1)S(1)} %collective-permute-done.4), channel_id=1, source_target_pairs={{0,1},{1,0},{2,3},{3,2},{4,5},{5,4},{6,7},{7,6},{8,9},{9,8},{10,11... | collective-permute-start | bytes 2359304 | tf_op jit(solution)/shard_map/ppermute | solution.py:418
  54.9 10.2 %collective-permute-start.10 = (bf16[400,128]{1,0:T(8,128)(2,1)S(1)}, bf16[400,128]{1,0:T(8,128)(2,1)S(1)}, u32[]{:S(2)}, u32[]{:S(2)}) collective-permute-start(bf16[400,128]{1,0:T(8,128)(2,1)S(1)} %get-tuple-element.66), channel_id=1, source_target_pairs={{0,4},{4,0},{8,12},{12,8},{16,20},{20,16},{24,28},{28,24},{1,5},{5... | collective-permute-start | bytes 307208 | tf_op jit(solution)/shard_map/ppermute | solution.py:418
  56.8 11.1 %collective-permute-start.11 = (bf16[400,128]{1,0:T(8,128)(2,1)S(1)}, bf16[400,128]{1,0:T(8,128)(2,1)S(1)}, u32[]{:S(2)}, u32[]{:S(2)}) collective-permute-start(bf16[400,128]{1,0:T(8,128)(2,1)S(1)} %get-tuple-element.67), channel_id=1, source_target_pairs={{0,8},{4,12},{8,0},{12,4},{16,24},{20,28},{24,16},{28,20},{1,9},{5... | collective-permute-start | bytes 307208 | tf_op jit(solution)/shard_map/ppermute | solution.py:418
  60.3 15.8 %collective-permute-start.12 = (bf16[400,128]{1,0:T(8,128)(2,1)S(1)}, bf16[400,128]{1,0:T(8,128)(2,1)S(1)}, u32[]{:S(2)}, u32[]{:S(2)}) collective-permute-start(bf16[400,128]{1,0:T(8,128)(2,1)S(1)} %get-tuple-element.68), channel_id=1, source_target_pairs={{0,16},{4,20},{8,24},{12,28},{16,0},{20,4},{24,8},{28,12},{1,17},{... | collective-permute-start | bytes 307208 | tf_op jit(solution)/shard_map/ppermute | solution.py:418
  61.2 15.5 %collective-permute-start.13 = (bf16[400,128]{1,0:T(8,128)(2,1)S(1)}, bf16[400,128]{1,0:T(8,128)(2,1)S(1)}, u32[]{:S(2)}, u32[]{:S(2)}) collective-permute-start(bf16[400,128]{1,0:T(8,128)(2,1)S(1)} %get-tuple-element.69), channel_id=1, source_target_pairs={{0,20},{4,16},{8,28},{12,24},{16,4},{20,0},{24,12},{28,8},{1,21},{... | collective-permute-start | bytes 307208 | tf_op jit(solution)/shard_map/ppermute | solution.py:418
  63.2 13.5 %collective-permute-start.14 = (bf16[400,128]{1,0:T(8,128)(2,1)S(1)}, bf16[400,128]{1,0:T(8,128)(2,1)S(1)}, u32[]{:S(2)}, u32[]{:S(2)}) collective-permute-start(bf16[400,128]{1,0:T(8,128)(2,1)S(1)} %get-tuple-element.70), channel_id=1, source_target_pairs={{0,24},{4,28},{8,16},{12,20},{16,8},{20,12},{24,0},{28,4},{1,25},{... | collective-permute-start | bytes 307208 | tf_op jit(solution)/shard_map/ppermute | solution.py:418
  65.1 11.6 %collective-permute-start.15 = (bf16[400,128]{1,0:T(8,128)(2,1)S(1)}, bf16[400,128]{1,0:T(8,128)(2,1)S(1)}, u32[]{:S(2)}, u32[]{:S(2)}) collective-permute-start(bf16[400,128]{1,0:T(8,128)(2,1)S(1)} %get-tuple-element.71), channel_id=1, source_target_pairs={{0,28},{4,24},{8,20},{12,16},{16,12},{20,8},{24,4},{28,0},{1,29},{... | collective-permute-start | bytes 307208 | tf_op jit(solution)/shard_map/ppermute | solution.py:418
  67.9 9.1 %collective-permute-start.16 = (bf16[400,128]{1,0:T(8,128)(2,1)S(1)}, bf16[400,128]{1,0:T(8,128)(2,1)S(1)}, u32[]{:S(2)}, u32[]{:S(2)}) collective-permute-start(bf16[400,128]{1,0:T(8,128)(2,1)S(1)} %get-tuple-element.72), channel_id=1, source_target_pairs={{0,12},{4,8},{8,4},{12,0},{16,28},{20,24},{24,20},{28,16},{1,13},{... | collective-permute-start | bytes 307208 | tf_op jit(solution)/shard_map/ppermute | solution.py:418

commit v5 on v4

--- a/solution.py
+++ b/solution.py
@@ -209,19 +209,14 @@
     )(in_hbm(tokens), in_hbm(paired), flag)
 
 
-def space_kernel(heads, x_hbm, w_hbm, parts_hbm, out_hbm, x_ref, w_ref, parts_ref, out_ref, total, x_sems, w_sems, parts_sem, out_sems):
+def space_kernel(heads, x_hbm, w_ref, parts_hbm, out_hbm, x_ref, parts_ref, out_ref, total, x_sems, parts_sem, out_sems):
     frames, positions, depth = x_hbm.shape
     width = heads * HD
     span = depth // SPLITS
     loads = []
     for split in range(SPLITS):
         here = pl.ds(split * span, span)
-        loads.append(
-            (
-                pltpu.make_async_copy(w_hbm.at[here], w_ref.at[here], w_sems.at[split]),
-                pltpu.make_async_copy(x_hbm.at[:, :, here], x_ref.at[:, :, here], x_sems.at[split]),
-            )
-        )
+        loads.append([pltpu.make_async_copy(x_hbm.at[:, :, here], x_ref.at[:, :, here], x_sems.at[split])])
     loads.append([pltpu.make_async_copy(parts_hbm, parts_ref, parts_sem.at[0])])
     for group in loads:
         for copy in group:
@@ -254,16 +249,14 @@
     place = pl.BlockSpec(memory_space=pl.ANY)
     return pl.pallas_call(
         lambda *refs: space_kernel(heads, *refs),
-        in_specs=[place] * 3,
+        in_specs=[place, VMEM, place],
         out_specs=place,
         out_shape=jax.ShapeDtypeStruct((frames, positions, width), jnp.bfloat16),
         scratch_shapes=[
             pltpu.VMEM(tokens.shape, jnp.bfloat16),
-            pltpu.VMEM((depth, width), jnp.bfloat16),
             pltpu.VMEM((rows, 2 * width), jnp.bfloat16),
             pltpu.VMEM((frames, positions, width), jnp.bfloat16),
             pltpu.VMEM((rows, width), jnp.float32),
-            pltpu.SemaphoreType.DMA((SPLITS,)),
             pltpu.SemaphoreType.DMA((SPLITS,)),
             pltpu.SemaphoreType.DMA((1,)),
             pltpu.SemaphoreType.DMA((frames,)),
@@ -271,7 +264,7 @@
         compiler_params=PARAMS,
         cost_estimate=LARGE,
         name="space_attention",
-    )(in_hbm(tokens), in_hbm(weights), in_hbm(parts))
+    )(in_hbm(tokens), pltpu.with_memory_space_constraint(weights, pltpu.VMEM), in_hbm(parts))
 
 
 def pieces(value):
@@ -309,6 +302,8 @@
 def late_kernel(heads, spots, blocks_to, rows, *refs):
     (one_ref, two_ref, w_ref), ins, peak_ref = refs[:3], refs[3 : 3 + len(spots)], refs[3 + len(spots)]
     outs, parts_ref = refs[4 + len(spots) : -1], refs[-1]
+    half = outs[0].shape[0]
+    outs = [*outs[:2], outs[2].at[pl.ds(0, half)], outs[2].at[pl.ds(half, half)], *outs[3:]]
     blocks = len(blocks_to)
     tokens = jnp.concatenate([one_ref[...], two_ref[...]], axis=0)
     total = jnp.dot(tokens, w_ref[...], preferred_element_type=jnp.float32)
@@ -331,6 +326,7 @@
     tail = jnp.zeros((16, HD), jnp.float32)
     for h in range(heads):
         peak = jnp.full((1, 1), -jnp.inf, jnp.float32)
+        results = []
         for g in range(groups):
             cols = []
             for r in range(ROLES):
@@ -338,10 +334,14 @@
                 cols.append(jnp.concatenate([x[g, :, at : at + HD] for x in ins], axis=0))
             result, highest = attend(*cols, mask)
             peak = jnp.maximum(peak, highest * score_scale)
-            result = result.astype(jnp.bfloat16)
-            for i, (out, pair) in enumerate(spots):
-                start = (h * groups + g) * 32 + pair * 16
-                outs[out][start : start + 16, :] = result[i * 16 : i * 16 + 16]
+            results.append(result)
+        for i, (out, pair) in enumerate(spots):
+            for two in range(0, groups, 2):
+                for k in range(2):
+                    at = i * 16 + k * 8
+                    tile = jnp.concatenate([results[two + j][at : at + 8] for j in range(2)], axis=0)
+                    start = ((h * 4 + 2 * pair + k) * groups + two) * 8
+                    outs[out][start : start + 16, :] = tile.astype(jnp.bfloat16)
         both = pieces(peak_ref[0:1, h * HD : (h + 1) * HD]) + pieces(jnp.broadcast_to(peak, (1, HD)))
         for i, value in enumerate(both):
             tail = jnp.where((line == i) & (lane == h), value, tail)
@@ -360,8 +360,10 @@
     return pl.pallas_call(
         lambda *refs: late_kernel(heads, spots, blocks_to, rows, *refs),
         in_specs=[VMEM] * (4 + len(parts)),
-        out_specs=[VMEM] * count,
-        out_shape=[jax.ShapeDtypeStruct(shape, jnp.bfloat16)] * count,
+        out_specs=[VMEM] * (count - 1),
+        out_shape=[jax.ShapeDtypeStruct(shape, jnp.bfloat16)] * 2
+        + [jax.ShapeDtypeStruct((2 * shape[0], HD), jnp.bfloat16)]
+        + [jax.ShapeDtypeStruct(shape, jnp.bfloat16)] * (count - 4),
         scratch_shapes=[
             pltpu.VMEM((groups, blocks * 16, cols), jnp.bfloat16),
         ],
@@ -378,21 +380,21 @@
 
 def finish_kernel(direct, heads, index_ref, *refs):
     ins, out_ref, clip_ref = refs[:-2], refs[-2], refs[-1]
-    groups = (ins[0].shape[0] - 16) // (32 * heads)
+    half = ins[0].shape[0]
+    near = [ins[0], ins[1].at[pl.ds(0, half)], ins[2].at[pl.ds(0, half)], ins[2].at[pl.ds(half, half)]]
+    ins = [*near, *ins[3:]]
+    rows = (half - 16) // (4 * heads)
     mine = index_ref[0]
     peak = None
     for d, source in enumerate(ins):
+        start = pl.multiple_of(index_ref[1 + d] * rows, rows)
         for h in range(heads):
-            for two in range(groups // 2):
-                for pair in range(2):
-                    starts = [(h * groups + 2 * two + k) * 32 + pair * 16 for k in range(2)]
-                    a, b = (source[start : start + 16, :].astype(jnp.float32) for start in starts)
-                    for k in range(2):
-                        tile = jnp.concatenate([a[8 * k : 8 * k + 8], b[8 * k : 8 * k + 8]], axis=0)
-                        frame = 2 * pair + k if d in direct else mine ^ (pair + 2 * k)
-                        start = pl.multiple_of(index_ref[1 + d] * (groups * 8) + two * 16, 16)
-                        out_ref[frame, pl.ds(start, 16), h * HD : (h + 1) * HD] = tile.astype(jnp.bfloat16)
-        tail = source[heads * groups * 32 :, :].astype(jnp.float32)
+            for pair in range(2):
+                for k in range(2):
+                    frame = 2 * pair + k if d in direct else mine ^ (pair + 2 * k)
+                    at = (h * 4 + 2 * pair + k) * rows
+                    out_ref[frame, pl.ds(start, rows), h * HD : (h + 1) * HD] = source[at : at + rows, :]
+        tail = source[half - 16 :, :].astype(jnp.float32)
         values = [tail[3 * a : 3 * a + 1] + tail[3 * a + 1 : 3 * a + 2] + tail[3 * a + 2 : 3 * a + 3] for a in range(2)]
         peak = values if peak is None else [jnp.maximum(p, v) for p, v in zip(peak, values)]
     for a in range(2):
@@ -446,8 +448,13 @@
     spots = [[(d, 0), (d, 1)] for d in (*direct, 0)] + [[(d, 0) for d in token_group]]
     outs = late(here_other, there_other, weights, [*away, own, first], spots, peaks, heads, seq, token_group)
     *outs, parts = lax.optimization_barrier([*outs, parts])
-    order = (0, 1, 2, 4, 5, 6, 7, 3)
-    received = [outs[d] if d == 0 else swap(outs[d], "seq", seq, d) for d in order]
+    mine_out, x_out, z_out, *far_outs = outs
+    half = mine_out.shape[0]
+    z_pair = swap(z_out, "seq", seq, 2)
+    far_pairs = [swap(out, "seq", seq, d) for d, out in zip((4, 5, 6, 7), far_outs)]
+    x_pair = swap(jnp.concatenate([x_out, z_pair[half:]], axis=0), "seq", seq, 1)
+    received = [mine_out, z_pair, x_pair, *far_pairs]
+    order = (0, 2, 1, 3, 4, 5, 6, 7)
     space_out = space_attention(patch_tokens, last, parts, heads)
     finish_index = jnp.stack([mine] + [me ^ d for d in order]).astype(jnp.int32)
     natural = [i for i, d in enumerate(order) if d not in token_group]

time: 79.4 us -> 79 us (level)
    ppermute x17 -> x16, starting transfers between devices: 28.3 us -> 28.3 us  [swap(): return lax.ppermute(value, axis, [(i, i ^ distance) for i in range(size)])]
    ppermute x17 -> x16, waiting for transfers between devices: 3.34 us -> 3.3 us  [swap(): return lax.ppermute(value, axis, [(i, i ^ distance) for i in range(size)])]
  transfers between devices with their start and end apart: 17 -> 16, of which waited for: 5 -> 4; matrix products, arithmetic and copies ran while one was open for 0% -> 0% of each run, Pallas kernels for 50% -> 49%
where the time goes in v5:
time: 79 us; the launch traced here: 78.4 us
  Pallas kernels  44.4 us (56%)
  starting transfers between devices  28.3 us (36%)
  waiting for transfers between devices  3.3 us (4%)
  local copies, waits for them, and re-layouts  1.45 us (2%)
  between operations  0.82 us (1%)
    ppermute x16, starting transfers between devices, swap(): return lax.ppermute(value, axis, [(i, i ^ distance) for i in range(size)])  28.3 us
    pallas_call x1, Pallas kernels, space_peak(): pl.pallas_call(lambda *refs: space_peak_kernel(heads, *refs), in_specs=[p...  14.6 us
    pallas_call x1, Pallas kernels, early(): pl.pallas_call(lambda *refs: early_kernel(count, rows, *refs), in_specs=[...  14 us
    pallas_call x1, Pallas kernels, space_attention(): pl.pallas_call(lambda *refs: space_kernel(heads, *refs), in_specs=[place,...  7.86 us
    pallas_call x1, Pallas kernels, late(): pl.pallas_call(lambda *refs: late_kernel(heads, spots, blocks_to, rows, *...  4.1 us
    ppermute x16, waiting for transfers between devices, swap(): return lax.ppermute(value, axis, [(i, i ^ distance) for i in range(size)])  3.3 us
    pallas_call x1, Pallas kernels, project(): pl.pallas_call(lambda *refs: project_kernel(blocks, rows, *refs), in_spec...  2.2 us
  transfers between devices with their start and end apart: 16, of which 4 were waited for; matrix products, arithmetic and copies ran while one was open for 0% of the time, Pallas kernels for 49%

profile of v5, /device:TPU:0, one launch (start us, length us, event | category | flops | bytes accessed | tf_op | source)
XLA Modules:
  0.0 78.4 jit_solution(2052708531473090640)
XLA Ops:
  0.7 1.3 %constant_dynamic-slice_fusion = (bf16[1,32,3072]{2,1,0:T(8,128)(2,1)S(1)}, bf16[1,32,3072]{2,1,0:T(8,128)(2,1)S(1)}, bf16[1,32,3072]{2,1,0:T(8,128)(2,1)S(1)}, bf16[1,32,3072]{2,1,0:T(8,128)(2,1)S(1)}) fusion(bf16[4,256,3072]{2,1,0:T(8,128)(2,1)} %refs_0_.3, s32[]{:T(128)S(6)} %select_n.18, s32[]{:T(128)S(6)} %select_n.22, s32[]{:T(128)S(6)} %select_n.21, ...), kind=kLoop, calls=%fused_computation.5 | loop fusion | bytes 1572884 | tf_op jit(solution)/shard_map/dynamic_slice | solution.py:433
  1.9 4.1 %collective-permute-start.3 = (bf16[1,32,3072]{2,1,0:T(8,128)(2,1)S(1)}, bf16[1,32,3072]{2,1,0:T(8,128)(2,1)S(1)}, u32[]{:S(2)}, u32[]{:S(2)}) collective-permute-start(bf16[1,32,3072]{2,1,0:T(8,128)(2,1)S(1)} %get-tuple-element.71), channel_id=1, source_target_pairs={{0,16},{4,20},{8,24},{12,28},{16,0},{20,4},{24,8},{28,12},{1,17},{... | collective-permute-start | bytes 589832 | tf_op jit(solution)/shard_map/ppermute | solution.py:420
  6.0 1.3 %collective-permute-start.2 = (bf16[1,32,3072]{2,1,0:T(8,128)(2,1)S(1)}, bf16[1,32,3072]{2,1,0:T(8,128)(2,1)S(1)}, u32[]{:S(2)}, u32[]{:S(2)}) collective-permute-start(bf16[1,32,3072]{2,1,0:T(8,128)(2,1)S(1)} %get-tuple-element.72), channel_id=1, source_target_pairs={{0,20},{4,16},{8,28},{12,24},{16,4},{20,0},{24,12},{28,8},{1,21},{... | collective-permute-start | bytes 589832 | tf_op jit(solution)/shard_map/ppermute | solution.py:420
  7.3 1.6 %collective-permute-start.1 = (bf16[1,32,3072]{2,1,0:T(8,128)(2,1)S(1)}, bf16[1,32,3072]{2,1,0:T(8,128)(2,1)S(1)}, u32[]{:S(2)}, u32[]{:S(2)}) collective-permute-start(bf16[1,32,3072]{2,1,0:T(8,128)(2,1)S(1)} %get-tuple-element.73), channel_id=1, source_target_pairs={{0,8},{4,12},{8,0},{12,4},{16,24},{20,28},{24,16},{28,20},{1,9},{5... | collective-permute-start | bytes 589832 | tf_op jit(solution)/shard_map/ppermute | solution.py:420
  8.9 0.2 collective-permute-start
  9.0 0.1 pad_add_fusion.refs_0_
  9.1 14.0 %early.1 = (bf16[3072,1152]{1,0:T(8,128)(2,1)}, f32[8,128]{1,0:T(8,128)S(1)}, bf16[4,32,1152]{2,1,0:T(8,128)(2,1)S(1)}, bf16[4,32,1152]{2,1,0:T(8,128)(2,1)S(1)}...) custom-call(s32[4]{0:T(128)S(1)} %pad_add_fusion.refs_0_, bf16[4,256,3072]{2,1,0:T(8,128)(2,1)} %refs_0_.3, ...), custom_call_target="tpu_custom_call" | custom-call | flops 16000000000 | bytes 40000000 | tf_op jit(solution)/shard_map/early/pallas_call | solution.py:118
  23.2 0.0 collective-permute-done.3
  23.2 1.5 %collective-permute-done.2 = bf16[1,32,3072]{2,1,0:T(8,128)(2,1)S(1)} collective-permute-done((bf16[1,32,3072]{2,1,0:T(8,128)(2,1)S(1)}, bf16[1,32,3072]{2,1,0:T(8,128)(2,1)S(1)}, u32[]{:S(2)}, u32[]{:S(2)}) %collective-permute-start.2) | collective-permute-done | bytes 196640 | tf_op jit(solution)/shard_map/ppermute | solution.py:420
  24.7 0.0 collective-permute-done.1
  24.7 0.2 collective-permute-done
  25.0 1.6 %collective-permute-start.4 = (bf16[4,32,3072]{2,1,0:T(8,128)(2,1)S(1)}, bf16[4,32,3072]{2,1,0:T(8,128)(2,1)S(1)}, u32[]{:S(2)}, u32[]{:S(2)}) collective-permute-start(bf16[4,32,3072]{2,1,0:T(8,128)(2,1)S(1)} %constant_dynamic-update-slice_fusion), channel_id=1, source_target_pairs={{0,2},{1,3},{2,0},{3,1},{4,6},{5,7},{6,4},{7,5},{8,10},{9,11},{10,... | collective-permute-start | bytes 2359304 | tf_op jit(solution)/shard_map/ppermute | solution.py:420
  26.6 4.6 %collective-permute-start.7 = (bf16[4,32,1152]{2,1,0:T(8,128)(2,1)S(1)}, bf16[4,32,1152]{2,1,0:T(8,128)(2,1)S(1)}, u32[]{:S(2)}, u32[]{:S(2)}) collective-permute-start(bf16[4,32,1152]{2,1,0:T(8,128)(2,1)S(1)} %get-tuple-element.48), channel_id=1, source_target_pairs={{0,24},{4,28},{8,16},{12,20},{16,8},{20,12},{24,0},{28,4},{1,25},{... | collective-permute-start | bytes 884744 | tf_op jit(solution)/shard_map/ppermute | solution.py:420
  31.2 0.9 %collective-permute-start.8 = (bf16[4,32,1152]{2,1,0:T(8,128)(2,1)S(1)}, bf16[4,32,1152]{2,1,0:T(8,128)(2,1)S(1)}, u32[]{:S(2)}, u32[]{:S(2)}) collective-permute-start(bf16[4,32,1152]{2,1,0:T(8,128)(2,1)S(1)} %get-tuple-element.49), channel_id=1, source_target_pairs={{0,28},{4,24},{8,20},{12,16},{16,12},{20,8},{24,4},{28,0},{1,29},{... | collective-permute-start | bytes 884744 | tf_op jit(solution)/shard_map/ppermute | solution.py:420
  32.1 0.6 collective-permute-start.9
  32.7 14.6 %space_peak.1 = (bf16[1024,768]{1,0:T(8,128)(2,1)}, bf16[3072,384]{1,0:T(8,128)(2,1)}, f32[8,384]{1,0:T(8,128)S(1)}) custom-call(bf16[4,256,3072]{2,1,0:T(8,128)(2,1)} %refs_0_.3, bf16[3072,3,2,384]{3,2,1,0:T(2,128)(2,1)} %bitcast.21, f32[8,128]{1,0:T(8,128)S(1)} %get-tuple-element.38.refs_2_), custom_call_target="tpu_custom_call" | custom-call | flops 3000000000 | bytes 8000000 | tf_op jit(solution)/shard_map/space_peak/pallas_call | solution.py:185
  47.3 0.0 collective-permute-done.4
  47.3 0.1 collective-permute-start.5
  47.4 0.5 collective-permute-start.6
  47.9 2.2 %project.1.refs_7_ = bf16[4,64,1152]{2,1,0:T(8,128)(2,1)S(1)} custom-call(bf16[128,3072]{1,0:T(8,128)(2,1)S(1)} %bitcast.14, bf16[128,3072]{1,0:T(8,128)(2,1)S(1)} %bitcast.15, bf16[3072,1152]{1,0:T(8,128)(2,1)S(1)} %bitcast.19), custom_call_target="tpu_custom_call" | custom-call | flops 16000000000 | bytes 40000000 | tf_op jit(solution)/shard_map/project/pallas_call | solution.py:291
  50.2 0.7 collective-permute-done.6
  50.8 4.1 %late.1 = (bf16[400,128]{1,0:T(8,128)(2,1)S(1)}, bf16[400,128]{1,0:T(8,128)(2,1)S(1)}, bf16[800,128]{1,0:T(8,128)(2,1)S(1)}, bf16[400,128]{1,0:T(8,128)(2,1)S(1)...) custom-call(bf16[128,3072]{1,0:T(8,128)(2,1)S(1)} %bitcast.16, ...), custom_call_target="tpu_custom_call" | custom-call | flops 16000000000 | bytes 40000000 | tf_op jit(solution)/shard_map/late/pallas_call | solution.py:360
  54.9 3.9 %collective-permute-start.10 = (bf16[800,128]{1,0:T(8,128)(2,1)S(1)}, bf16[800,128]{1,0:T(8,128)(2,1)S(1)}, u32[]{:S(2)}, u32[]{:S(2)}) collective-permute-start(bf16[800,128]{1,0:T(8,128)(2,1)S(1)} %get-tuple-element.63), channel_id=1, source_target_pairs={{0,8},{4,12},{8,0},{12,4},{16,24},{20,28},{24,16},{28,20},{1,9},{5... | collective-permute-start | bytes 614408 | tf_op jit(solution)/shard_map/ppermute | solution.py:420
  58.8 0.1 stack.47.refs_0_
  58.9 0.6 collective-permute-start.12
  59.4 3.2 %collective-permute-start.13 = (bf16[400,128]{1,0:T(8,128)(2,1)S(1)}, bf16[400,128]{1,0:T(8,128)(2,1)S(1)}, u32[]{:S(2)}, u32[]{:S(2)}) collective-permute-start(bf16[400,128]{1,0:T(8,128)(2,1)S(1)} %get-tuple-element.66), channel_id=1, source_target_pairs={{0,20},{4,16},{8,28},{12,24},{16,4},{20,0},{24,12},{28,8},{1,21},{... | collective-permute-start | bytes 307208 | tf_op jit(solution)/shard_map/ppermute | solution.py:420
  62.6 2.0 %collective-permute-start.14 = (bf16[400,128]{1,0:T(8,128)(2,1)S(1)}, bf16[400,128]{1,0:T(8,128)(2,1)S(1)}, u32[]{:S(2)}, u32[]{:S(2)}) collective-permute-start(bf16[400,128]{1,0:T(8,128)(2,1)S(1)} %get-tuple-element.67), channel_id=1, source_target_pairs={{0,24},{4,28},{8,16},{12,20},{16,8},{20,12},{24,0},{28,4},{1,25},{... | collective-permute-start | bytes 307208 | tf_op jit(solution)/shard_map/ppermute | solution.py:420
  64.7 1.8 %collective-permute-start.15 = (bf16[400,128]{1,0:T(8,128)(2,1)S(1)}, bf16[400,128]{1,0:T(8,128)(2,1)S(1)}, u32[]{:S(2)}, u32[]{:S(2)}) collective-permute-start(bf16[400,128]{1,0:T(8,128)(2,1)S(1)} %get-tuple-element.68), channel_id=1, source_target_pairs={{0,28},{4,24},{8,20},{12,16},{16,12},{20,8},{24,4},{28,0},{1,29},{... | collective-permute-start | bytes 307208 | tf_op jit(solution)/shard_map/ppermute | solution.py:420
  66.6 1.5 %collective-permute-start.11 = (bf16[800,128]{1,0:T(8,128)(2,1)S(1)}, bf16[800,128]{1,0:T(8,128)(2,1)S(1)}, u32[]{:S(2)}, u32[]{:S(2)}) collective-permute-start(bf16[800,128]{1,0:T(8,128)(2,1)S(1)} %pad_maximum_fusion), channel_id=1, source_target_pairs={{0,4},{4,0},{8,12},{12,8},{16,20},{20,16},{24,28},{28,24},{1,5},{5... | collective-permute-start | bytes 614408 | tf_op jit(solution)/shard_map/ppermute | solution.py:420
  68.0 7.9 %space_attention.1 = bf16[4,256,384]{2,1,0:T(8,128)(2,1)} custom-call(bf16[4,256,3072]{2,1,0:T(8,128)(2,1)} %refs_0_.3, bf16[3072,384]{1,0:T(8,128)(2,1)S(1)} %copy-done, bf16[1024,768]{1,0:T(8,128)(2,1)} %get-tuple-element.61.refs_2_), custom_call_target="tpu_custom_call" | custom-call | flops 16000000000 | bytes 40000000 | tf_op jit(solution)/shard_map/space_attention/pallas_call | solution.py:250
  75.9 0.9 %collective-permute-done.13.refs_5_ = bf16[400,128]{1,0:T(8,128)(2,1)S(1)} collective-permute-done((bf16[400,128]{1,0:T(8,128)(2,1)S(1)}, bf16[400,128]{1,0:T(8,128)(2,1)S(1)}, u32[]{:S(2)}, u32[]{:S(2)}) %collective-permute-start.13) | collective-permute-done | bytes 102432 | tf_op jit(solution)/shard_map/ppermute | solution.py:420
  76.8 1.6 %finish.1 = (bf16[4,256,384]{2,1,0:T(8,128)(2,1)}, f32[2,3]{1,0:T(2,128)}) custom-call(s32[9]{0:T(128)S(1)} %stack.47.refs_0_, bf16[400,128]{1,0:T(8,128)(2,1)S(1)} %get-tuple-element.62.refs_1_, bf16[800,128]{1,0:T(8,128)(2,1)S(1)} %collective-permute-done.10.refs_2_, bf16[800,128]{1,0:T(8,128)(2,1)S(1)} %collective-permute-done.11.refs_3_, ...), custom_call_target="tpu_custom_call" | custom-call | tf_op jit(solution)/shard_map/finish/pallas_call | solution.py:406
  (22 shorter events, 0.1 us)
Async XLA Ops:
  1.9 21.2 %collective-permute-start.3 = (bf16[1,32,3072]{2,1,0:T(8,128)(2,1)S(1)}, bf16[1,32,3072]{2,1,0:T(8,128)(2,1)S(1)}, u32[]{:S(2)}, u32[]{:S(2)}) collective-permute-start(bf16[1,32,3072]{2,1,0:T(8,128)(2,1)S(1)} %get-tuple-element.71), channel_id=1, source_target_pairs={{0,16},{4,20},{8,24},{12,28},{16,0},{20,4},{24,8},{28,12},{1,17},{... | collective-permute-start | bytes 589832 | tf_op jit(solution)/shard_map/ppermute | solution.py:420
  6.0 18.6 %collective-permute-start.2 = (bf16[1,32,3072]{2,1,0:T(8,128)(2,1)S(1)}, bf16[1,32,3072]{2,1,0:T(8,128)(2,1)S(1)}, u32[]{:S(2)}, u32[]{:S(2)}) collective-permute-start(bf16[1,32,3072]{2,1,0:T(8,128)(2,1)S(1)} %get-tuple-element.72), channel_id=1, source_target_pairs={{0,20},{4,16},{8,28},{12,24},{16,4},{20,0},{24,12},{28,8},{1,21},{... | collective-permute-start | bytes 589832 | tf_op jit(solution)/shard_map/ppermute | solution.py:420
  7.3 17.4 %collective-permute-start.1 = (bf16[1,32,3072]{2,1,0:T(8,128)(2,1)S(1)}, bf16[1,32,3072]{2,1,0:T(8,128)(2,1)S(1)}, u32[]{:S(2)}, u32[]{:S(2)}) collective-permute-start(bf16[1,32,3072]{2,1,0:T(8,128)(2,1)S(1)} %get-tuple-element.73), channel_id=1, source_target_pairs={{0,8},{4,12},{8,0},{12,4},{16,24},{20,28},{24,16},{28,20},{1,9},{5... | collective-permute-start | bytes 589832 | tf_op jit(solution)/shard_map/ppermute | solution.py:420
  8.9 16.0 %collective-permute-start = (bf16[1,32,3072]{2,1,0:T(8,128)(2,1)S(1)}, bf16[1,32,3072]{2,1,0:T(8,128)(2,1)S(1)}, u32[]{:S(2)}, u32[]{:S(2)}) collective-permute-start(bf16[1,32,3072]{2,1,0:T(8,128)(2,1)S(1)} %get-tuple-element.74), channel_id=1, source_target_pairs={{0,12},{4,8},{8,4},{12,0},{16,28},{20,24},{24,20},{28,16},{1,13},{... | collective-permute-start | bytes 589832 | tf_op jit(solution)/shard_map/ppermute | solution.py:420
  25.0 22.3 %collective-permute-start.4 = (bf16[4,32,3072]{2,1,0:T(8,128)(2,1)S(1)}, bf16[4,32,3072]{2,1,0:T(8,128)(2,1)S(1)}, u32[]{:S(2)}, u32[]{:S(2)}) collective-permute-start(bf16[4,32,3072]{2,1,0:T(8,128)(2,1)S(1)} %constant_dynamic-update-slice_fusion), channel_id=1, source_target_pairs={{0,2},{1,3},{2,0},{3,1},{4,6},{5,7},{6,4},{7,5},{8,10},{9,11},{10,... | collective-permute-start | bytes 2359304 | tf_op jit(solution)/shard_map/ppermute | solution.py:420
  26.6 23.5 %collective-permute-start.7 = (bf16[4,32,1152]{2,1,0:T(8,128)(2,1)S(1)}, bf16[4,32,1152]{2,1,0:T(8,128)(2,1)S(1)}, u32[]{:S(2)}, u32[]{:S(2)}) collective-permute-start(bf16[4,32,1152]{2,1,0:T(8,128)(2,1)S(1)} %get-tuple-element.48), channel_id=1, source_target_pairs={{0,24},{4,28},{8,16},{12,20},{16,8},{20,12},{24,0},{28,4},{1,25},{... | collective-permute-start | bytes 884744 | tf_op jit(solution)/shard_map/ppermute | solution.py:420
  31.2 19.0 %collective-permute-start.8 = (bf16[4,32,1152]{2,1,0:T(8,128)(2,1)S(1)}, bf16[4,32,1152]{2,1,0:T(8,128)(2,1)S(1)}, u32[]{:S(2)}, u32[]{:S(2)}) collective-permute-start(bf16[4,32,1152]{2,1,0:T(8,128)(2,1)S(1)} %get-tuple-element.49), channel_id=1, source_target_pairs={{0,28},{4,24},{8,20},{12,16},{16,12},{20,8},{24,4},{28,0},{1,29},{... | collective-permute-start | bytes 884744 | tf_op jit(solution)/shard_map/ppermute | solution.py:420
  32.1 15.8 %slice-start = ((s8[7077888]{0:T(1024)(128)(4,1)}), s8[4194304]{0:T(1024)(128)(4,1)S(1)}, s32[]{:S(2)}) async-start(s8[7077888]{0:T(1024)(128)(4,1)} %bitcast.18), calls=%async_computation | async-start | bytes 8388608
  32.1 15.8 %slice-start.1 = ((s8[7077888]{0:T(1024)(128)(4,1)}), s8[2883584]{0:T(1024)(128)(4,1)S(1)}, s32[]{:S(2)}) async-start(s8[7077888]{0:T(1024)(128)(4,1)} %bitcast.18), calls=%async_computation.1 | async-start | bytes 5767168
  32.1 18.0 %collective-permute-start.9 = (bf16[4,32,1152]{2,1,0:T(8,128)(2,1)S(1)}, bf16[4,32,1152]{2,1,0:T(8,128)(2,1)S(1)}, u32[]{:S(2)}, u32[]{:S(2)}) collective-permute-start(bf16[4,32,1152]{2,1,0:T(8,128)(2,1)S(1)} %get-tuple-element.50), channel_id=1, source_target_pairs={{0,4},{4,0},{8,12},{12,8},{16,20},{20,16},{24,28},{28,24},{1,5},{5... | collective-permute-start | bytes 884744 | tf_op jit(solution)/shard_map/ppermute | solution.py:420
  47.3 2.8 %collective-permute-start.5 = (bf16[4,32,3072]{2,1,0:T(8,128)(2,1)S(1)}, bf16[4,32,3072]{2,1,0:T(8,128)(2,1)S(1)}, u32[]{:S(2)}, u32[]{:S(2)}) collective-permute-start(bf16[4,32,3072]{2,1,0:T(8,128)(2,1)S(1)} %constant_dynamic-update-slice_fusion), channel_id=1, source_target_pairs={{0,1},{1,0},{2,3},{3,2},{4,5},{5,4},{6,7},{7,6},{8,9},{9,8},{10,11... | collective-permute-start | bytes 2359304 | tf_op jit(solution)/shard_map/ppermute | solution.py:420
  47.4 3.4 %collective-permute-start.6 = (bf16[4,32,3072]{2,1,0:T(8,128)(2,1)S(1)}, bf16[4,32,3072]{2,1,0:T(8,128)(2,1)S(1)}, u32[]{:S(2)}, u32[]{:S(2)}) collective-permute-start(bf16[4,32,3072]{2,1,0:T(8,128)(2,1)S(1)} %collective-permute-done.4), channel_id=1, source_target_pairs={{0,1},{1,0},{2,3},{3,2},{4,5},{5,4},{6,7},{7,6},{8,9},{9,8},{10,11... | collective-permute-start | bytes 2359304 | tf_op jit(solution)/shard_map/ppermute | solution.py:420
  50.8 17.2 %copy-start = (bf16[3072,384]{1,0:T(8,128)(2,1)S(1)}, bf16[3072,384]{1,0:T(8,128)(2,1)}, u32[]{:S(2)}) copy-start(bf16[3072,384]{1,0:T(8,128)(2,1)} %get-tuple-element.39.refs_1_) | copy-start | bytes 7077892
  54.9 11.6 %collective-permute-start.10 = (bf16[800,128]{1,0:T(8,128)(2,1)S(1)}, bf16[800,128]{1,0:T(8,128)(2,1)S(1)}, u32[]{:S(2)}, u32[]{:S(2)}) collective-permute-start(bf16[800,128]{1,0:T(8,128)(2,1)S(1)} %get-tuple-element.63), channel_id=1, source_target_pairs={{0,8},{4,12},{8,0},{12,4},{16,24},{20,28},{24,16},{28,20},{1,9},{5... | collective-permute-start | bytes 614408 | tf_op jit(solution)/shard_map/ppermute | solution.py:420
  58.9 17.0 %collective-permute-start.12 = (bf16[400,128]{1,0:T(8,128)(2,1)S(1)}, bf16[400,128]{1,0:T(8,128)(2,1)S(1)}, u32[]{:S(2)}, u32[]{:S(2)}) collective-permute-start(bf16[400,128]{1,0:T(8,128)(2,1)S(1)} %get-tuple-element.65), channel_id=1, source_target_pairs={{0,16},{4,20},{8,24},{12,28},{16,0},{20,4},{24,8},{28,12},{1,17},{... | collective-permute-start | bytes 307208 | tf_op jit(solution)/shard_map/ppermute | solution.py:420
  59.4 17.4 %collective-permute-start.13 = (bf16[400,128]{1,0:T(8,128)(2,1)S(1)}, bf16[400,128]{1,0:T(8,128)(2,1)S(1)}, u32[]{:S(2)}, u32[]{:S(2)}) collective-permute-start(bf16[400,128]{1,0:T(8,128)(2,1)S(1)} %get-tuple-element.66), channel_id=1, source_target_pairs={{0,20},{4,16},{8,28},{12,24},{16,4},{20,0},{24,12},{28,8},{1,21},{... | collective-permute-start | bytes 307208 | tf_op jit(solution)/shard_map/ppermute | solution.py:420
  62.6 14.2 %collective-permute-start.14 = (bf16[400,128]{1,0:T(8,128)(2,1)S(1)}, bf16[400,128]{1,0:T(8,128)(2,1)S(1)}, u32[]{:S(2)}, u32[]{:S(2)}) collective-permute-start(bf16[400,128]{1,0:T(8,128)(2,1)S(1)} %get-tuple-element.67), channel_id=1, source_target_pairs={{0,24},{4,28},{8,16},{12,20},{16,8},{20,12},{24,0},{28,4},{1,25},{... | collective-permute-start | bytes 307208 | tf_op jit(solution)/shard_map/ppermute | solution.py:420
  64.7 12.1 %collective-permute-start.15 = (bf16[400,128]{1,0:T(8,128)(2,1)S(1)}, bf16[400,128]{1,0:T(8,128)(2,1)S(1)}, u32[]{:S(2)}, u32[]{:S(2)}) collective-permute-start(bf16[400,128]{1,0:T(8,128)(2,1)S(1)} %get-tuple-element.68), channel_id=1, source_target_pairs={{0,28},{4,24},{8,20},{12,16},{16,12},{20,8},{24,4},{28,0},{1,29},{... | collective-permute-start | bytes 307208 | tf_op jit(solution)/shard_map/ppermute | solution.py:420
  66.6 10.3 %collective-permute-start.11 = (bf16[800,128]{1,0:T(8,128)(2,1)S(1)}, bf16[800,128]{1,0:T(8,128)(2,1)S(1)}, u32[]{:S(2)}, u32[]{:S(2)}) collective-permute-start(bf16[800,128]{1,0:T(8,128)(2,1)S(1)} %pad_maximum_fusion), channel_id=1, source_target_pairs={{0,4},{4,0},{8,12},{12,8},{16,20},{20,16},{24,28},{28,24},{1,5},{5... | collective-permute-start | bytes 614408 | tf_op jit(solution)/shard_map/ppermute | solution.py:420

commit v6 on v5

--- a/solution.py
+++ b/solution.py
@@ -426,7 +426,7 @@
     width = heads * HD
     rows = positions // seq
     me, mine = lax.axis_index("seq"), lax.axis_index("head")
-    token_group, direct = (3, 2, 5, 4), (6, 7, 1)
+    token_group, direct = (3, 2, 5, 4), (1, 6, 7)
     paired = jnp.transpose(projection, (0, 2, 1, 3))
 
     def piece(frame, owner):

time: 79 us -> 78.3 us (level)
  no operation moved by 1% of the time
where the time goes in v6:
time: 78.3 us; the launch traced here: 78 us
  Pallas kernels  44.3 us (57%)
  starting transfers between devices  28.8 us (37%)
  waiting for transfers between devices  2.55 us (3%)
  local copies, waits for them, and re-layouts  1.45 us (2%)
  between operations  0.82 us (1%)
    ppermute x16, starting transfers between devices, swap(): return lax.ppermute(value, axis, [(i, i ^ distance) for i in range(size)])  28.8 us
    pallas_call x1, Pallas kernels, space_peak(): pl.pallas_call(lambda *refs: space_peak_kernel(heads, *refs), in_specs=[p...  14.5 us
    pallas_call x1, Pallas kernels, early(): pl.pallas_call(lambda *refs: early_kernel(count, rows, *refs), in_specs=[...  14 us
    pallas_call x1, Pallas kernels, space_attention(): pl.pallas_call(lambda *refs: space_kernel(heads, *refs), in_specs=[place,...  7.86 us
    pallas_call x1, Pallas kernels, late(): pl.pallas_call(lambda *refs: late_kernel(heads, spots, blocks_to, rows, *...  4.1 us
    ppermute x16, waiting for transfers between devices, swap(): return lax.ppermute(value, axis, [(i, i ^ distance) for i in range(size)])  2.55 us
    pallas_call x1, Pallas kernels, project(): pl.pallas_call(lambda *refs: project_kernel(blocks, rows, *refs), in_spec...  2.2 us
    pallas_call x1, Pallas kernels, finish(): pl.pallas_call(lambda *refs: finish_kernel(direct, heads, *refs), in_spec...  1.57 us
  transfers between devices with their start and end apart: 16, of which 4 were waited for; matrix products, arithmetic and copies ran while one was open for 0% of the time, Pallas kernels for 49%

profile of v6, /device:TPU:0, one launch (start us, length us, event | category | flops | bytes accessed | tf_op | source)
XLA Modules:
  0.0 78.0 jit_solution(13193084788818866921)
XLA Ops:
  0.7 1.3 %constant_dynamic-slice_fusion = (bf16[1,32,3072]{2,1,0:T(8,128)(2,1)S(1)}, bf16[1,32,3072]{2,1,0:T(8,128)(2,1)S(1)}, bf16[1,32,3072]{2,1,0:T(8,128)(2,1)S(1)}, bf16[1,32,3072]{2,1,0:T(8,128)(2,1)S(1)}) fusion(bf16[4,256,3072]{2,1,0:T(8,128)(2,1)} %refs_0_.3, s32[]{:T(128)S(6)} %select_n.18, s32[]{:T(128)S(6)} %select_n.22, s32[]{:T(128)S(6)} %select_n.21, ...), kind=kLoop, calls=%fused_computation.5 | loop fusion | bytes 1572884 | tf_op jit(solution)/shard_map/dynamic_slice | solution.py:433
  1.9 4.1 %collective-permute-start.3 = (bf16[1,32,3072]{2,1,0:T(8,128)(2,1)S(1)}, bf16[1,32,3072]{2,1,0:T(8,128)(2,1)S(1)}, u32[]{:S(2)}, u32[]{:S(2)}) collective-permute-start(bf16[1,32,3072]{2,1,0:T(8,128)(2,1)S(1)} %get-tuple-element.71), channel_id=1, source_target_pairs={{0,16},{4,20},{8,24},{12,28},{16,0},{20,4},{24,8},{28,12},{1,17},{... | collective-permute-start | bytes 589832 | tf_op jit(solution)/shard_map/ppermute | solution.py:420
  6.0 1.3 %collective-permute-start.2 = (bf16[1,32,3072]{2,1,0:T(8,128)(2,1)S(1)}, bf16[1,32,3072]{2,1,0:T(8,128)(2,1)S(1)}, u32[]{:S(2)}, u32[]{:S(2)}) collective-permute-start(bf16[1,32,3072]{2,1,0:T(8,128)(2,1)S(1)} %get-tuple-element.72), channel_id=1, source_target_pairs={{0,20},{4,16},{8,28},{12,24},{16,4},{20,0},{24,12},{28,8},{1,21},{... | collective-permute-start | bytes 589832 | tf_op jit(solution)/shard_map/ppermute | solution.py:420
  7.3 1.6 %collective-permute-start.1 = (bf16[1,32,3072]{2,1,0:T(8,128)(2,1)S(1)}, bf16[1,32,3072]{2,1,0:T(8,128)(2,1)S(1)}, u32[]{:S(2)}, u32[]{:S(2)}) collective-permute-start(bf16[1,32,3072]{2,1,0:T(8,128)(2,1)S(1)} %get-tuple-element.73), channel_id=1, source_target_pairs={{0,8},{4,12},{8,0},{12,4},{16,24},{20,28},{24,16},{28,20},{1,9},{5... | collective-permute-start | bytes 589832 | tf_op jit(solution)/shard_map/ppermute | solution.py:420
  8.9 0.2 collective-permute-start
  9.0 0.1 pad_add_fusion.refs_0_
  9.1 14.0 %early.1 = (bf16[3072,1152]{1,0:T(8,128)(2,1)}, f32[8,128]{1,0:T(8,128)S(1)}, bf16[4,32,1152]{2,1,0:T(8,128)(2,1)S(1)}, bf16[4,32,1152]{2,1,0:T(8,128)(2,1)S(1)}...) custom-call(s32[4]{0:T(128)S(1)} %pad_add_fusion.refs_0_, bf16[4,256,3072]{2,1,0:T(8,128)(2,1)} %refs_0_.3, ...), custom_call_target="tpu_custom_call" | custom-call | flops 16000000000 | bytes 40000000 | tf_op jit(solution)/shard_map/early/pallas_call | solution.py:118
  23.2 0.0 collective-permute-done.3
  23.2 1.5 %collective-permute-done.2 = bf16[1,32,3072]{2,1,0:T(8,128)(2,1)S(1)} collective-permute-done((bf16[1,32,3072]{2,1,0:T(8,128)(2,1)S(1)}, bf16[1,32,3072]{2,1,0:T(8,128)(2,1)S(1)}, u32[]{:S(2)}, u32[]{:S(2)}) %collective-permute-start.2) | collective-permute-done | bytes 196640 | tf_op jit(solution)/shard_map/ppermute | solution.py:420
  24.7 0.0 collective-permute-done.1
  24.7 0.2 collective-permute-done
  25.0 1.6 %collective-permute-start.4 = (bf16[4,32,3072]{2,1,0:T(8,128)(2,1)S(1)}, bf16[4,32,3072]{2,1,0:T(8,128)(2,1)S(1)}, u32[]{:S(2)}, u32[]{:S(2)}) collective-permute-start(bf16[4,32,3072]{2,1,0:T(8,128)(2,1)S(1)} %constant_dynamic-update-slice_fusion), channel_id=1, source_target_pairs={{0,2},{1,3},{2,0},{3,1},{4,6},{5,7},{6,4},{7,5},{8,10},{9,11},{10,... | collective-permute-start | bytes 2359304 | tf_op jit(solution)/shard_map/ppermute | solution.py:420
  26.6 1.5 %collective-permute-start.7 = (bf16[4,32,1152]{2,1,0:T(8,128)(2,1)S(1)}, bf16[4,32,1152]{2,1,0:T(8,128)(2,1)S(1)}, u32[]{:S(2)}, u32[]{:S(2)}) collective-permute-start(bf16[4,32,1152]{2,1,0:T(8,128)(2,1)S(1)} %get-tuple-element.48), channel_id=1, source_target_pairs={{0,4},{4,0},{8,12},{12,8},{16,20},{20,16},{24,28},{28,24},{1,5},{5... | collective-permute-start | bytes 884744 | tf_op jit(solution)/shard_map/ppermute | solution.py:420
  28.1 4.6 %collective-permute-start.8 = (bf16[4,32,1152]{2,1,0:T(8,128)(2,1)S(1)}, bf16[4,32,1152]{2,1,0:T(8,128)(2,1)S(1)}, u32[]{:S(2)}, u32[]{:S(2)}) collective-permute-start(bf16[4,32,1152]{2,1,0:T(8,128)(2,1)S(1)} %get-tuple-element.49), channel_id=1, source_target_pairs={{0,24},{4,28},{8,16},{12,20},{16,8},{20,12},{24,0},{28,4},{1,25},{... | collective-permute-start | bytes 884744 | tf_op jit(solution)/shard_map/ppermute | solution.py:420
  32.7 14.5 %space_peak.1 = (bf16[1024,768]{1,0:T(8,128)(2,1)}, bf16[3072,384]{1,0:T(8,128)(2,1)}, f32[8,384]{1,0:T(8,128)S(1)}) custom-call(bf16[4,256,3072]{2,1,0:T(8,128)(2,1)} %refs_0_.3, bf16[3072,3,2,384]{3,2,1,0:T(2,128)(2,1)} %bitcast.21, f32[8,128]{1,0:T(8,128)S(1)} %get-tuple-element.38.refs_2_), custom_call_target="tpu_custom_call" | custom-call | flops 3000000000 | bytes 8000000 | tf_op jit(solution)/shard_map/space_peak/pallas_call | solution.py:185
  47.2 0.1 collective-permute-start.5
  47.3 0.5 collective-permute-start.6
  47.8 2.2 %project.1.refs_7_ = bf16[4,64,1152]{2,1,0:T(8,128)(2,1)S(1)} custom-call(bf16[128,3072]{1,0:T(8,128)(2,1)S(1)} %bitcast.14, bf16[128,3072]{1,0:T(8,128)(2,1)S(1)} %bitcast.15, bf16[3072,1152]{1,0:T(8,128)(2,1)S(1)} %bitcast.19), custom_call_target="tpu_custom_call" | custom-call | flops 16000000000 | bytes 40000000 | tf_op jit(solution)/shard_map/project/pallas_call | solution.py:291
  50.0 0.0 collective-permute-done.8.refs_4_
  50.0 0.0 collective-permute-done.9.refs_5_
  50.0 0.7 collective-permute-done.6
  50.7 4.1 %late.1 = (bf16[400,128]{1,0:T(8,128)(2,1)S(1)}, bf16[400,128]{1,0:T(8,128)(2,1)S(1)}, bf16[800,128]{1,0:T(8,128)(2,1)S(1)}, bf16[400,128]{1,0:T(8,128)(2,1)S(1)...) custom-call(bf16[128,3072]{1,0:T(8,128)(2,1)S(1)} %bitcast.16, ...), custom_call_target="tpu_custom_call" | custom-call | flops 16000000000 | bytes 40000000 | tf_op jit(solution)/shard_map/late/pallas_call | solution.py:360
  54.8 5.1 %collective-permute-start.10 = (bf16[800,128]{1,0:T(8,128)(2,1)S(1)}, bf16[800,128]{1,0:T(8,128)(2,1)S(1)}, u32[]{:S(2)}, u32[]{:S(2)}) collective-permute-start(bf16[800,128]{1,0:T(8,128)(2,1)S(1)} %get-tuple-element.63), channel_id=1, source_target_pairs={{0,8},{4,12},{8,0},{12,4},{16,24},{20,28},{24,16},{28,20},{1,9},{5... | collective-permute-start | bytes 614408 | tf_op jit(solution)/shard_map/ppermute | solution.py:420
  59.9 0.1 stack.47.refs_0_
  60.0 0.6 collective-permute-start.12
  60.6 2.4 %collective-permute-start.13 = (bf16[400,128]{1,0:T(8,128)(2,1)S(1)}, bf16[400,128]{1,0:T(8,128)(2,1)S(1)}, u32[]{:S(2)}, u32[]{:S(2)}) collective-permute-start(bf16[400,128]{1,0:T(8,128)(2,1)S(1)} %get-tuple-element.66), channel_id=1, source_target_pairs={{0,20},{4,16},{8,28},{12,24},{16,4},{20,0},{24,12},{28,8},{1,21},{... | collective-permute-start | bytes 307208 | tf_op jit(solution)/shard_map/ppermute | solution.py:420
  63.0 1.9 %collective-permute-start.14 = (bf16[400,128]{1,0:T(8,128)(2,1)S(1)}, bf16[400,128]{1,0:T(8,128)(2,1)S(1)}, u32[]{:S(2)}, u32[]{:S(2)}) collective-permute-start(bf16[400,128]{1,0:T(8,128)(2,1)S(1)} %get-tuple-element.67), channel_id=1, source_target_pairs={{0,24},{4,28},{8,16},{12,20},{16,8},{20,12},{24,0},{28,4},{1,25},{... | collective-permute-start | bytes 307208 | tf_op jit(solution)/shard_map/ppermute | solution.py:420
  64.8 2.8 %collective-permute-start.15 = (bf16[400,128]{1,0:T(8,128)(2,1)S(1)}, bf16[400,128]{1,0:T(8,128)(2,1)S(1)}, u32[]{:S(2)}, u32[]{:S(2)}) collective-permute-start(bf16[400,128]{1,0:T(8,128)(2,1)S(1)} %get-tuple-element.68), channel_id=1, source_target_pairs={{0,28},{4,24},{8,20},{12,16},{16,12},{20,8},{24,4},{28,0},{1,29},{... | collective-permute-start | bytes 307208 | tf_op jit(solution)/shard_map/ppermute | solution.py:420
  67.7 0.7 collective-permute-start.11
  68.4 7.9 %space_attention.1 = bf16[4,256,384]{2,1,0:T(8,128)(2,1)} custom-call(bf16[4,256,3072]{2,1,0:T(8,128)(2,1)} %refs_0_.3, bf16[3072,384]{1,0:T(8,128)(2,1)S(1)} %copy-done, bf16[1024,768]{1,0:T(8,128)(2,1)} %get-tuple-element.61.refs_2_), custom_call_target="tpu_custom_call" | custom-call | flops 16000000000 | bytes 40000000 | tf_op jit(solution)/shard_map/space_attention/pallas_call | solution.py:250
  76.2 0.1 collective-permute-done.13.refs_5_
  76.4 1.6 %finish.1 = (bf16[4,256,384]{2,1,0:T(8,128)(2,1)}, f32[2,3]{1,0:T(2,128)}) custom-call(s32[9]{0:T(128)S(1)} %stack.47.refs_0_, bf16[400,128]{1,0:T(8,128)(2,1)S(1)} %get-tuple-element.62.refs_1_, bf16[800,128]{1,0:T(8,128)(2,1)S(1)} %collective-permute-done.10.refs_2_, bf16[800,128]{1,0:T(8,128)(2,1)S(1)} %collective-permute-done.11.refs_3_, ...), custom_call_target="tpu_custom_call" | custom-call | tf_op jit(solution)/shard_map/finish/pallas_call | solution.py:406
  (22 shorter events, 0.1 us)
Async XLA Ops:
  1.9 21.2 %collective-permute-start.3 = (bf16[1,32,3072]{2,1,0:T(8,128)(2,1)S(1)}, bf16[1,32,3072]{2,1,0:T(8,128)(2,1)S(1)}, u32[]{:S(2)}, u32[]{:S(2)}) collective-permute-start(bf16[1,32,3072]{2,1,0:T(8,128)(2,1)S(1)} %get-tuple-element.71), channel_id=1, source_target_pairs={{0,16},{4,20},{8,24},{12,28},{16,0},{20,4},{24,8},{28,12},{1,17},{... | collective-permute-start | bytes 589832 | tf_op jit(solution)/shard_map/ppermute | solution.py:420
  6.0 18.6 %collective-permute-start.2 = (bf16[1,32,3072]{2,1,0:T(8,128)(2,1)S(1)}, bf16[1,32,3072]{2,1,0:T(8,128)(2,1)S(1)}, u32[]{:S(2)}, u32[]{:S(2)}) collective-permute-start(bf16[1,32,3072]{2,1,0:T(8,128)(2,1)S(1)} %get-tuple-element.72), channel_id=1, source_target_pairs={{0,20},{4,16},{8,28},{12,24},{16,4},{20,0},{24,12},{28,8},{1,21},{... | collective-permute-start | bytes 589832 | tf_op jit(solution)/shard_map/ppermute | solution.py:420
  7.3 17.4 %collective-permute-start.1 = (bf16[1,32,3072]{2,1,0:T(8,128)(2,1)S(1)}, bf16[1,32,3072]{2,1,0:T(8,128)(2,1)S(1)}, u32[]{:S(2)}, u32[]{:S(2)}) collective-permute-start(bf16[1,32,3072]{2,1,0:T(8,128)(2,1)S(1)} %get-tuple-element.73), channel_id=1, source_target_pairs={{0,8},{4,12},{8,0},{12,4},{16,24},{20,28},{24,16},{28,20},{1,9},{5... | collective-permute-start | bytes 589832 | tf_op jit(solution)/shard_map/ppermute | solution.py:420
  8.9 16.0 %collective-permute-start = (bf16[1,32,3072]{2,1,0:T(8,128)(2,1)S(1)}, bf16[1,32,3072]{2,1,0:T(8,128)(2,1)S(1)}, u32[]{:S(2)}, u32[]{:S(2)}) collective-permute-start(bf16[1,32,3072]{2,1,0:T(8,128)(2,1)S(1)} %get-tuple-element.74), channel_id=1, source_target_pairs={{0,12},{4,8},{8,4},{12,0},{16,28},{20,24},{24,20},{28,16},{1,13},{... | collective-permute-start | bytes 589832 | tf_op jit(solution)/shard_map/ppermute | solution.py:420
  25.0 22.2 %collective-permute-start.4 = (bf16[4,32,3072]{2,1,0:T(8,128)(2,1)S(1)}, bf16[4,32,3072]{2,1,0:T(8,128)(2,1)S(1)}, u32[]{:S(2)}, u32[]{:S(2)}) collective-permute-start(bf16[4,32,3072]{2,1,0:T(8,128)(2,1)S(1)} %constant_dynamic-update-slice_fusion), channel_id=1, source_target_pairs={{0,2},{1,3},{2,0},{3,1},{4,6},{5,7},{6,4},{7,5},{8,10},{9,11},{10,... | collective-permute-start | bytes 2359304 | tf_op jit(solution)/shard_map/ppermute | solution.py:420
  26.6 23.4 %collective-permute-start.7 = (bf16[4,32,1152]{2,1,0:T(8,128)(2,1)S(1)}, bf16[4,32,1152]{2,1,0:T(8,128)(2,1)S(1)}, u32[]{:S(2)}, u32[]{:S(2)}) collective-permute-start(bf16[4,32,1152]{2,1,0:T(8,128)(2,1)S(1)} %get-tuple-element.48), channel_id=1, source_target_pairs={{0,4},{4,0},{8,12},{12,8},{16,20},{20,16},{24,28},{28,24},{1,5},{5... | collective-permute-start | bytes 884744 | tf_op jit(solution)/shard_map/ppermute | solution.py:420
  28.1 21.9 %collective-permute-start.8 = (bf16[4,32,1152]{2,1,0:T(8,128)(2,1)S(1)}, bf16[4,32,1152]{2,1,0:T(8,128)(2,1)S(1)}, u32[]{:S(2)}, u32[]{:S(2)}) collective-permute-start(bf16[4,32,1152]{2,1,0:T(8,128)(2,1)S(1)} %get-tuple-element.49), channel_id=1, source_target_pairs={{0,24},{4,28},{8,16},{12,20},{16,8},{20,12},{24,0},{28,4},{1,25},{... | collective-permute-start | bytes 884744 | tf_op jit(solution)/shard_map/ppermute | solution.py:420
  32.7 15.1 %slice-start = ((s8[7077888]{0:T(1024)(128)(4,1)}), s8[4194304]{0:T(1024)(128)(4,1)S(1)}, s32[]{:S(2)}) async-start(s8[7077888]{0:T(1024)(128)(4,1)} %bitcast.18), calls=%async_computation | async-start | bytes 8388608
  32.7 15.1 %slice-start.1 = ((s8[7077888]{0:T(1024)(128)(4,1)}), s8[2883584]{0:T(1024)(128)(4,1)S(1)}, s32[]{:S(2)}) async-start(s8[7077888]{0:T(1024)(128)(4,1)} %bitcast.18), calls=%async_computation.1 | async-start | bytes 5767168
  32.7 17.3 %collective-permute-start.9 = (bf16[4,32,1152]{2,1,0:T(8,128)(2,1)S(1)}, bf16[4,32,1152]{2,1,0:T(8,128)(2,1)S(1)}, u32[]{:S(2)}, u32[]{:S(2)}) collective-permute-start(bf16[4,32,1152]{2,1,0:T(8,128)(2,1)S(1)} %get-tuple-element.50), channel_id=1, source_target_pairs={{0,28},{4,24},{8,20},{12,16},{16,12},{20,8},{24,4},{28,0},{1,29},{... | collective-permute-start | bytes 884744 | tf_op jit(solution)/shard_map/ppermute | solution.py:420
  47.2 2.8 %collective-permute-start.5 = (bf16[4,32,3072]{2,1,0:T(8,128)(2,1)S(1)}, bf16[4,32,3072]{2,1,0:T(8,128)(2,1)S(1)}, u32[]{:S(2)}, u32[]{:S(2)}) collective-permute-start(bf16[4,32,3072]{2,1,0:T(8,128)(2,1)S(1)} %constant_dynamic-update-slice_fusion), channel_id=1, source_target_pairs={{0,1},{1,0},{2,3},{3,2},{4,5},{5,4},{6,7},{7,6},{8,9},{9,8},{10,11... | collective-permute-start | bytes 2359304 | tf_op jit(solution)/shard_map/ppermute | solution.py:420
  47.3 3.4 %collective-permute-start.6 = (bf16[4,32,3072]{2,1,0:T(8,128)(2,1)S(1)}, bf16[4,32,3072]{2,1,0:T(8,128)(2,1)S(1)}, u32[]{:S(2)}, u32[]{:S(2)}) collective-permute-start(bf16[4,32,3072]{2,1,0:T(8,128)(2,1)S(1)} %collective-permute-done.4), channel_id=1, source_target_pairs={{0,1},{1,0},{2,3},{3,2},{4,5},{5,4},{6,7},{7,6},{8,9},{9,8},{10,11... | collective-permute-start | bytes 2359304 | tf_op jit(solution)/shard_map/ppermute | solution.py:420
  50.7 17.7 %copy-start = (bf16[3072,384]{1,0:T(8,128)(2,1)S(1)}, bf16[3072,384]{1,0:T(8,128)(2,1)}, u32[]{:S(2)}) copy-start(bf16[3072,384]{1,0:T(8,128)(2,1)} %get-tuple-element.39.refs_1_) | copy-start | bytes 7077892
  54.8 12.8 %collective-permute-start.10 = (bf16[800,128]{1,0:T(8,128)(2,1)S(1)}, bf16[800,128]{1,0:T(8,128)(2,1)S(1)}, u32[]{:S(2)}, u32[]{:S(2)}) collective-permute-start(bf16[800,128]{1,0:T(8,128)(2,1)S(1)} %get-tuple-element.63), channel_id=1, source_target_pairs={{0,8},{4,12},{8,0},{12,4},{16,24},{20,28},{24,16},{28,20},{1,9},{5... | collective-permute-start | bytes 614408 | tf_op jit(solution)/shard_map/ppermute | solution.py:420
  60.0 16.2 %collective-permute-start.12 = (bf16[400,128]{1,0:T(8,128)(2,1)S(1)}, bf16[400,128]{1,0:T(8,128)(2,1)S(1)}, u32[]{:S(2)}, u32[]{:S(2)}) collective-permute-start(bf16[400,128]{1,0:T(8,128)(2,1)S(1)} %get-tuple-element.65), channel_id=1, source_target_pairs={{0,16},{4,20},{8,24},{12,28},{16,0},{20,4},{24,8},{28,12},{1,17},{... | collective-permute-start | bytes 307208 | tf_op jit(solution)/shard_map/ppermute | solution.py:420
  60.6 15.8 %collective-permute-start.13 = (bf16[400,128]{1,0:T(8,128)(2,1)S(1)}, bf16[400,128]{1,0:T(8,128)(2,1)S(1)}, u32[]{:S(2)}, u32[]{:S(2)}) collective-permute-start(bf16[400,128]{1,0:T(8,128)(2,1)S(1)} %get-tuple-element.66), channel_id=1, source_target_pairs={{0,20},{4,16},{8,28},{12,24},{16,4},{20,0},{24,12},{28,8},{1,21},{... | collective-permute-start | bytes 307208 | tf_op jit(solution)/shard_map/ppermute | solution.py:420
  63.0 13.4 %collective-permute-start.14 = (bf16[400,128]{1,0:T(8,128)(2,1)S(1)}, bf16[400,128]{1,0:T(8,128)(2,1)S(1)}, u32[]{:S(2)}, u32[]{:S(2)}) collective-permute-start(bf16[400,128]{1,0:T(8,128)(2,1)S(1)} %get-tuple-element.67), channel_id=1, source_target_pairs={{0,24},{4,28},{8,16},{12,20},{16,8},{20,12},{24,0},{28,4},{1,25},{... | collective-permute-start | bytes 307208 | tf_op jit(solution)/shard_map/ppermute | solution.py:420
  64.8 11.6 %collective-permute-start.15 = (bf16[400,128]{1,0:T(8,128)(2,1)S(1)}, bf16[400,128]{1,0:T(8,128)(2,1)S(1)}, u32[]{:S(2)}, u32[]{:S(2)}) collective-permute-start(bf16[400,128]{1,0:T(8,128)(2,1)S(1)} %get-tuple-element.68), channel_id=1, source_target_pairs={{0,28},{4,24},{8,20},{12,16},{16,12},{20,8},{24,4},{28,0},{1,29},{... | collective-permute-start | bytes 307208 | tf_op jit(solution)/shard_map/ppermute | solution.py:420
  67.7 8.7 %collective-permute-start.11 = (bf16[800,128]{1,0:T(8,128)(2,1)S(1)}, bf16[800,128]{1,0:T(8,128)(2,1)S(1)}, u32[]{:S(2)}, u32[]{:S(2)}) collective-permute-start(bf16[800,128]{1,0:T(8,128)(2,1)S(1)} %pad_maximum_fusion), channel_id=1, source_target_pairs={{0,4},{4,0},{8,12},{12,8},{16,20},{20,16},{24,28},{28,24},{1,5},{5... | collective-permute-start | bytes 614408 | tf_op jit(solution)/shard_map/ppermute | solution.py:420

commit v7 on v6

--- a/solution.py
+++ b/solution.py
@@ -426,7 +426,7 @@
     width = heads * HD
     rows = positions // seq
     me, mine = lax.axis_index("seq"), lax.axis_index("head")
-    token_group, direct = (3, 2, 5, 4), (1, 6, 7)
+    token_group, direct = (3, 2, 5, 4), (1, 7, 6)
     paired = jnp.transpose(projection, (0, 2, 1, 3))
 
     def piece(frame, owner):

time: 78.3 us -> 78.5 us (level)
  no operation moved by 1% of the time
where the time goes in v7:
time: 78.5 us; the launch traced here: 78 us
  Pallas kernels  44.3 us (56%)
  starting transfers between devices  28.8 us (37%)
  waiting for transfers between devices  2.54 us (3%)
  local copies, waits for them, and re-layouts  1.45 us (2%)
  between operations  0.82 us (1%)
    ppermute x16, starting transfers between devices, swap(): return lax.ppermute(value, axis, [(i, i ^ distance) for i in range(size)])  28.8 us
    pallas_call x1, Pallas kernels, space_peak(): pl.pallas_call(lambda *refs: space_peak_kernel(heads, *refs), in_specs=[p...  14.5 us
    pallas_call x1, Pallas kernels, early(): pl.pallas_call(lambda *refs: early_kernel(count, rows, *refs), in_specs=[...  14 us
    pallas_call x1, Pallas kernels, space_attention(): pl.pallas_call(lambda *refs: space_kernel(heads, *refs), in_specs=[place,...  7.85 us
    pallas_call x1, Pallas kernels, late(): pl.pallas_call(lambda *refs: late_kernel(heads, spots, blocks_to, rows, *...  4.1 us
    ppermute x16, waiting for transfers between devices, swap(): return lax.ppermute(value, axis, [(i, i ^ distance) for i in range(size)])  2.54 us
    pallas_call x1, Pallas kernels, project(): pl.pallas_call(lambda *refs: project_kernel(blocks, rows, *refs), in_spec...  2.2 us
  transfers between devices with their start and end apart: 16, of which 4 were waited for; matrix products, arithmetic and copies ran while one was open for 0% of the time, Pallas kernels for 49%

profile of v7, /device:TPU:0, one launch (start us, length us, event | category | flops | bytes accessed | tf_op | source)
XLA Modules:
  0.0 78.0 jit_solution(3310529671360016454)
XLA Ops:
  0.7 1.3 %constant_dynamic-slice_fusion = (bf16[1,32,3072]{2,1,0:T(8,128)(2,1)S(1)}, bf16[1,32,3072]{2,1,0:T(8,128)(2,1)S(1)}, bf16[1,32,3072]{2,1,0:T(8,128)(2,1)S(1)}, bf16[1,32,3072]{2,1,0:T(8,128)(2,1)S(1)}) fusion(bf16[4,256,3072]{2,1,0:T(8,128)(2,1)} %refs_0_.3, s32[]{:T(128)S(6)} %select_n.18, s32[]{:T(128)S(6)} %select_n.22, s32[]{:T(128)S(6)} %select_n.21, ...), kind=kLoop, calls=%fused_computation.5 | loop fusion | bytes 1572884 | tf_op jit(solution)/shard_map/dynamic_slice | solution.py:433
  1.9 4.1 %collective-permute-start.3 = (bf16[1,32,3072]{2,1,0:T(8,128)(2,1)S(1)}, bf16[1,32,3072]{2,1,0:T(8,128)(2,1)S(1)}, u32[]{:S(2)}, u32[]{:S(2)}) collective-permute-start(bf16[1,32,3072]{2,1,0:T(8,128)(2,1)S(1)} %get-tuple-element.71), channel_id=1, source_target_pairs={{0,16},{4,20},{8,24},{12,28},{16,0},{20,4},{24,8},{28,12},{1,17},{... | collective-permute-start | bytes 589832 | tf_op jit(solution)/shard_map/ppermute | solution.py:420
  6.0 1.3 %collective-permute-start.2 = (bf16[1,32,3072]{2,1,0:T(8,128)(2,1)S(1)}, bf16[1,32,3072]{2,1,0:T(8,128)(2,1)S(1)}, u32[]{:S(2)}, u32[]{:S(2)}) collective-permute-start(bf16[1,32,3072]{2,1,0:T(8,128)(2,1)S(1)} %get-tuple-element.72), channel_id=1, source_target_pairs={{0,20},{4,16},{8,28},{12,24},{16,4},{20,0},{24,12},{28,8},{1,21},{... | collective-permute-start | bytes 589832 | tf_op jit(solution)/shard_map/ppermute | solution.py:420
  7.3 1.6 %collective-permute-start.1 = (bf16[1,32,3072]{2,1,0:T(8,128)(2,1)S(1)}, bf16[1,32,3072]{2,1,0:T(8,128)(2,1)S(1)}, u32[]{:S(2)}, u32[]{:S(2)}) collective-permute-start(bf16[1,32,3072]{2,1,0:T(8,128)(2,1)S(1)} %get-tuple-element.73), channel_id=1, source_target_pairs={{0,8},{4,12},{8,0},{12,4},{16,24},{20,28},{24,16},{28,20},{1,9},{5... | collective-permute-start | bytes 589832 | tf_op jit(solution)/shard_map/ppermute | solution.py:420
  8.9 0.2 collective-permute-start
  9.0 0.1 pad_add_fusion.refs_0_
  9.1 14.0 %early.1 = (bf16[3072,1152]{1,0:T(8,128)(2,1)}, f32[8,128]{1,0:T(8,128)S(1)}, bf16[4,32,1152]{2,1,0:T(8,128)(2,1)S(1)}, bf16[4,32,1152]{2,1,0:T(8,128)(2,1)S(1)}...) custom-call(s32[4]{0:T(128)S(1)} %pad_add_fusion.refs_0_, bf16[4,256,3072]{2,1,0:T(8,128)(2,1)} %refs_0_.3, ...), custom_call_target="tpu_custom_call" | custom-call | flops 16000000000 | bytes 40000000 | tf_op jit(solution)/shard_map/early/pallas_call | solution.py:118
  23.2 0.0 collective-permute-done.3
  23.2 1.5 %collective-permute-done.2 = bf16[1,32,3072]{2,1,0:T(8,128)(2,1)S(1)} collective-permute-done((bf16[1,32,3072]{2,1,0:T(8,128)(2,1)S(1)}, bf16[1,32,3072]{2,1,0:T(8,128)(2,1)S(1)}, u32[]{:S(2)}, u32[]{:S(2)}) %collective-permute-start.2) | collective-permute-done | bytes 196640 | tf_op jit(solution)/shard_map/ppermute | solution.py:420
  24.7 0.0 collective-permute-done.1
  24.7 0.2 collective-permute-done
  25.0 1.6 %collective-permute-start.4 = (bf16[4,32,3072]{2,1,0:T(8,128)(2,1)S(1)}, bf16[4,32,3072]{2,1,0:T(8,128)(2,1)S(1)}, u32[]{:S(2)}, u32[]{:S(2)}) collective-permute-start(bf16[4,32,3072]{2,1,0:T(8,128)(2,1)S(1)} %constant_dynamic-update-slice_fusion), channel_id=1, source_target_pairs={{0,2},{1,3},{2,0},{3,1},{4,6},{5,7},{6,4},{7,5},{8,10},{9,11},{10,... | collective-permute-start | bytes 2359304 | tf_op jit(solution)/shard_map/ppermute | solution.py:420
  26.6 1.5 %collective-permute-start.7 = (bf16[4,32,1152]{2,1,0:T(8,128)(2,1)S(1)}, bf16[4,32,1152]{2,1,0:T(8,128)(2,1)S(1)}, u32[]{:S(2)}, u32[]{:S(2)}) collective-permute-start(bf16[4,32,1152]{2,1,0:T(8,128)(2,1)S(1)} %get-tuple-element.48), channel_id=1, source_target_pairs={{0,4},{4,0},{8,12},{12,8},{16,20},{20,16},{24,28},{28,24},{1,5},{5... | collective-permute-start | bytes 884744 | tf_op jit(solution)/shard_map/ppermute | solution.py:420
  28.1 4.6 %collective-permute-start.8 = (bf16[4,32,1152]{2,1,0:T(8,128)(2,1)S(1)}, bf16[4,32,1152]{2,1,0:T(8,128)(2,1)S(1)}, u32[]{:S(2)}, u32[]{:S(2)}) collective-permute-start(bf16[4,32,1152]{2,1,0:T(8,128)(2,1)S(1)} %get-tuple-element.49), channel_id=1, source_target_pairs={{0,28},{4,24},{8,20},{12,16},{16,12},{20,8},{24,4},{28,0},{1,29},{... | collective-permute-start | bytes 884744 | tf_op jit(solution)/shard_map/ppermute | solution.py:420
  32.6 0.0 collective-permute-start.9
  32.7 14.5 %space_peak.1 = (bf16[1024,768]{1,0:T(8,128)(2,1)}, bf16[3072,384]{1,0:T(8,128)(2,1)}, f32[8,384]{1,0:T(8,128)S(1)}) custom-call(bf16[4,256,3072]{2,1,0:T(8,128)(2,1)} %refs_0_.3, bf16[3072,3,2,384]{3,2,1,0:T(2,128)(2,1)} %bitcast.21, f32[8,128]{1,0:T(8,128)S(1)} %get-tuple-element.38.refs_2_), custom_call_target="tpu_custom_call" | custom-call | flops 3000000000 | bytes 8000000 | tf_op jit(solution)/shard_map/space_peak/pallas_call | solution.py:185
  47.2 0.0 collective-permute-done.4
  47.2 0.1 collective-permute-start.5
  47.3 0.5 collective-permute-start.6
  47.8 2.2 %project.1.refs_7_ = bf16[4,64,1152]{2,1,0:T(8,128)(2,1)S(1)} custom-call(bf16[128,3072]{1,0:T(8,128)(2,1)S(1)} %bitcast.14, bf16[128,3072]{1,0:T(8,128)(2,1)S(1)} %bitcast.15, bf16[3072,1152]{1,0:T(8,128)(2,1)S(1)} %bitcast.19), custom_call_target="tpu_custom_call" | custom-call | flops 16000000000 | bytes 40000000 | tf_op jit(solution)/shard_map/project/pallas_call | solution.py:291
  50.0 0.7 collective-permute-done.6
  50.7 4.1 %late.1 = (bf16[400,128]{1,0:T(8,128)(2,1)S(1)}, bf16[400,128]{1,0:T(8,128)(2,1)S(1)}, bf16[800,128]{1,0:T(8,128)(2,1)S(1)}, bf16[400,128]{1,0:T(8,128)(2,1)S(1)...) custom-call(bf16[128,3072]{1,0:T(8,128)(2,1)S(1)} %bitcast.16, ...), custom_call_target="tpu_custom_call" | custom-call | flops 16000000000 | bytes 40000000 | tf_op jit(solution)/shard_map/late/pallas_call | solution.py:360
  54.8 5.1 %collective-permute-start.10 = (bf16[800,128]{1,0:T(8,128)(2,1)S(1)}, bf16[800,128]{1,0:T(8,128)(2,1)S(1)}, u32[]{:S(2)}, u32[]{:S(2)}) collective-permute-start(bf16[800,128]{1,0:T(8,128)(2,1)S(1)} %get-tuple-element.63), channel_id=1, source_target_pairs={{0,8},{4,12},{8,0},{12,4},{16,24},{20,28},{24,16},{28,20},{1,9},{5... | collective-permute-start | bytes 614408 | tf_op jit(solution)/shard_map/ppermute | solution.py:420
  59.9 0.1 stack.47.refs_0_
  60.0 0.6 collective-permute-start.12
  60.6 2.4 %collective-permute-start.13 = (bf16[400,128]{1,0:T(8,128)(2,1)S(1)}, bf16[400,128]{1,0:T(8,128)(2,1)S(1)}, u32[]{:S(2)}, u32[]{:S(2)}) collective-permute-start(bf16[400,128]{1,0:T(8,128)(2,1)S(1)} %get-tuple-element.66), channel_id=1, source_target_pairs={{0,20},{4,16},{8,28},{12,24},{16,4},{20,0},{24,12},{28,8},{1,21},{... | collective-permute-start | bytes 307208 | tf_op jit(solution)/shard_map/ppermute | solution.py:420
  63.0 1.9 %collective-permute-start.14 = (bf16[400,128]{1,0:T(8,128)(2,1)S(1)}, bf16[400,128]{1,0:T(8,128)(2,1)S(1)}, u32[]{:S(2)}, u32[]{:S(2)}) collective-permute-start(bf16[400,128]{1,0:T(8,128)(2,1)S(1)} %get-tuple-element.67), channel_id=1, source_target_pairs={{0,24},{4,28},{8,16},{12,20},{16,8},{20,12},{24,0},{28,4},{1,25},{... | collective-permute-start | bytes 307208 | tf_op jit(solution)/shard_map/ppermute | solution.py:420
  64.9 2.8 %collective-permute-start.15 = (bf16[400,128]{1,0:T(8,128)(2,1)S(1)}, bf16[400,128]{1,0:T(8,128)(2,1)S(1)}, u32[]{:S(2)}, u32[]{:S(2)}) collective-permute-start(bf16[400,128]{1,0:T(8,128)(2,1)S(1)} %get-tuple-element.68), channel_id=1, source_target_pairs={{0,28},{4,24},{8,20},{12,16},{16,12},{20,8},{24,4},{28,0},{1,29},{... | collective-permute-start | bytes 307208 | tf_op jit(solution)/shard_map/ppermute | solution.py:420
  67.7 0.7 collective-permute-start.11
  68.4 7.9 %space_attention.1 = bf16[4,256,384]{2,1,0:T(8,128)(2,1)} custom-call(bf16[4,256,3072]{2,1,0:T(8,128)(2,1)} %refs_0_.3, bf16[3072,384]{1,0:T(8,128)(2,1)S(1)} %copy-done, bf16[1024,768]{1,0:T(8,128)(2,1)} %get-tuple-element.61.refs_2_), custom_call_target="tpu_custom_call" | custom-call | flops 16000000000 | bytes 40000000 | tf_op jit(solution)/shard_map/space_attention/pallas_call | solution.py:250
  76.3 0.1 collective-permute-done.13.refs_5_
  76.4 1.6 %finish.1 = (bf16[4,256,384]{2,1,0:T(8,128)(2,1)}, f32[2,3]{1,0:T(2,128)}) custom-call(s32[9]{0:T(128)S(1)} %stack.47.refs_0_, bf16[400,128]{1,0:T(8,128)(2,1)S(1)} %get-tuple-element.62.refs_1_, bf16[800,128]{1,0:T(8,128)(2,1)S(1)} %collective-permute-done.10.refs_2_, bf16[800,128]{1,0:T(8,128)(2,1)S(1)} %collective-permute-done.11.refs_3_, ...), custom_call_target="tpu_custom_call" | custom-call | tf_op jit(solution)/shard_map/finish/pallas_call | solution.py:406
  (22 shorter events, 0.1 us)
Async XLA Ops:
  1.9 21.2 %collective-permute-start.3 = (bf16[1,32,3072]{2,1,0:T(8,128)(2,1)S(1)}, bf16[1,32,3072]{2,1,0:T(8,128)(2,1)S(1)}, u32[]{:S(2)}, u32[]{:S(2)}) collective-permute-start(bf16[1,32,3072]{2,1,0:T(8,128)(2,1)S(1)} %get-tuple-element.71), channel_id=1, source_target_pairs={{0,16},{4,20},{8,24},{12,28},{16,0},{20,4},{24,8},{28,12},{1,17},{... | collective-permute-start | bytes 589832 | tf_op jit(solution)/shard_map/ppermute | solution.py:420
  6.0 18.6 %collective-permute-start.2 = (bf16[1,32,3072]{2,1,0:T(8,128)(2,1)S(1)}, bf16[1,32,3072]{2,1,0:T(8,128)(2,1)S(1)}, u32[]{:S(2)}, u32[]{:S(2)}) collective-permute-start(bf16[1,32,3072]{2,1,0:T(8,128)(2,1)S(1)} %get-tuple-element.72), channel_id=1, source_target_pairs={{0,20},{4,16},{8,28},{12,24},{16,4},{20,0},{24,12},{28,8},{1,21},{... | collective-permute-start | bytes 589832 | tf_op jit(solution)/shard_map/ppermute | solution.py:420
  7.3 17.4 %collective-permute-start.1 = (bf16[1,32,3072]{2,1,0:T(8,128)(2,1)S(1)}, bf16[1,32,3072]{2,1,0:T(8,128)(2,1)S(1)}, u32[]{:S(2)}, u32[]{:S(2)}) collective-permute-start(bf16[1,32,3072]{2,1,0:T(8,128)(2,1)S(1)} %get-tuple-element.73), channel_id=1, source_target_pairs={{0,8},{4,12},{8,0},{12,4},{16,24},{20,28},{24,16},{28,20},{1,9},{5... | collective-permute-start | bytes 589832 | tf_op jit(solution)/shard_map/ppermute | solution.py:420
  8.9 16.0 %collective-permute-start = (bf16[1,32,3072]{2,1,0:T(8,128)(2,1)S(1)}, bf16[1,32,3072]{2,1,0:T(8,128)(2,1)S(1)}, u32[]{:S(2)}, u32[]{:S(2)}) collective-permute-start(bf16[1,32,3072]{2,1,0:T(8,128)(2,1)S(1)} %get-tuple-element.74), channel_id=1, source_target_pairs={{0,12},{4,8},{8,4},{12,0},{16,28},{20,24},{24,20},{28,16},{1,13},{... | collective-permute-start | bytes 589832 | tf_op jit(solution)/shard_map/ppermute | solution.py:420
  25.0 22.2 %collective-permute-start.4 = (bf16[4,32,3072]{2,1,0:T(8,128)(2,1)S(1)}, bf16[4,32,3072]{2,1,0:T(8,128)(2,1)S(1)}, u32[]{:S(2)}, u32[]{:S(2)}) collective-permute-start(bf16[4,32,3072]{2,1,0:T(8,128)(2,1)S(1)} %constant_dynamic-update-slice_fusion), channel_id=1, source_target_pairs={{0,2},{1,3},{2,0},{3,1},{4,6},{5,7},{6,4},{7,5},{8,10},{9,11},{10,... | collective-permute-start | bytes 2359304 | tf_op jit(solution)/shard_map/ppermute | solution.py:420
  26.6 23.4 %collective-permute-start.7 = (bf16[4,32,1152]{2,1,0:T(8,128)(2,1)S(1)}, bf16[4,32,1152]{2,1,0:T(8,128)(2,1)S(1)}, u32[]{:S(2)}, u32[]{:S(2)}) collective-permute-start(bf16[4,32,1152]{2,1,0:T(8,128)(2,1)S(1)} %get-tuple-element.48), channel_id=1, source_target_pairs={{0,4},{4,0},{8,12},{12,8},{16,20},{20,16},{24,28},{28,24},{1,5},{5... | collective-permute-start | bytes 884744 | tf_op jit(solution)/shard_map/ppermute | solution.py:420
  28.1 21.9 %collective-permute-start.8 = (bf16[4,32,1152]{2,1,0:T(8,128)(2,1)S(1)}, bf16[4,32,1152]{2,1,0:T(8,128)(2,1)S(1)}, u32[]{:S(2)}, u32[]{:S(2)}) collective-permute-start(bf16[4,32,1152]{2,1,0:T(8,128)(2,1)S(1)} %get-tuple-element.49), channel_id=1, source_target_pairs={{0,28},{4,24},{8,20},{12,16},{16,12},{20,8},{24,4},{28,0},{1,29},{... | collective-permute-start | bytes 884744 | tf_op jit(solution)/shard_map/ppermute | solution.py:420
  32.6 15.2 %slice-start = ((s8[7077888]{0:T(1024)(128)(4,1)}), s8[4194304]{0:T(1024)(128)(4,1)S(1)}, s32[]{:S(2)}) async-start(s8[7077888]{0:T(1024)(128)(4,1)} %bitcast.18), calls=%async_computation | async-start | bytes 8388608
  32.6 15.2 %slice-start.1 = ((s8[7077888]{0:T(1024)(128)(4,1)}), s8[2883584]{0:T(1024)(128)(4,1)S(1)}, s32[]{:S(2)}) async-start(s8[7077888]{0:T(1024)(128)(4,1)} %bitcast.18), calls=%async_computation.1 | async-start | bytes 5767168
  32.6 17.4 %collective-permute-start.9 = (bf16[4,32,1152]{2,1,0:T(8,128)(2,1)S(1)}, bf16[4,32,1152]{2,1,0:T(8,128)(2,1)S(1)}, u32[]{:S(2)}, u32[]{:S(2)}) collective-permute-start(bf16[4,32,1152]{2,1,0:T(8,128)(2,1)S(1)} %get-tuple-element.50), channel_id=1, source_target_pairs={{0,24},{4,28},{8,16},{12,20},{16,8},{20,12},{24,0},{28,4},{1,25},{... | collective-permute-start | bytes 884744 | tf_op jit(solution)/shard_map/ppermute | solution.py:420
  47.2 2.8 %collective-permute-start.5 = (bf16[4,32,3072]{2,1,0:T(8,128)(2,1)S(1)}, bf16[4,32,3072]{2,1,0:T(8,128)(2,1)S(1)}, u32[]{:S(2)}, u32[]{:S(2)}) collective-permute-start(bf16[4,32,3072]{2,1,0:T(8,128)(2,1)S(1)} %constant_dynamic-update-slice_fusion), channel_id=1, source_target_pairs={{0,1},{1,0},{2,3},{3,2},{4,5},{5,4},{6,7},{7,6},{8,9},{9,8},{10,11... | collective-permute-start | bytes 2359304 | tf_op jit(solution)/shard_map/ppermute | solution.py:420
  47.3 3.4 %collective-permute-start.6 = (bf16[4,32,3072]{2,1,0:T(8,128)(2,1)S(1)}, bf16[4,32,3072]{2,1,0:T(8,128)(2,1)S(1)}, u32[]{:S(2)}, u32[]{:S(2)}) collective-permute-start(bf16[4,32,3072]{2,1,0:T(8,128)(2,1)S(1)} %collective-permute-done.4), channel_id=1, source_target_pairs={{0,1},{1,0},{2,3},{3,2},{4,5},{5,4},{6,7},{7,6},{8,9},{9,8},{10,11... | collective-permute-start | bytes 2359304 | tf_op jit(solution)/shard_map/ppermute | solution.py:420
  50.7 17.7 %copy-start = (bf16[3072,384]{1,0:T(8,128)(2,1)S(1)}, bf16[3072,384]{1,0:T(8,128)(2,1)}, u32[]{:S(2)}) copy-start(bf16[3072,384]{1,0:T(8,128)(2,1)} %get-tuple-element.39.refs_1_) | copy-start | bytes 7077892
  54.8 12.9 %collective-permute-start.10 = (bf16[800,128]{1,0:T(8,128)(2,1)S(1)}, bf16[800,128]{1,0:T(8,128)(2,1)S(1)}, u32[]{:S(2)}, u32[]{:S(2)}) collective-permute-start(bf16[800,128]{1,0:T(8,128)(2,1)S(1)} %get-tuple-element.63), channel_id=1, source_target_pairs={{0,8},{4,12},{8,0},{12,4},{16,24},{20,28},{24,16},{28,20},{1,9},{5... | collective-permute-start | bytes 614408 | tf_op jit(solution)/shard_map/ppermute | solution.py:420
  60.0 16.2 %collective-permute-start.12 = (bf16[400,128]{1,0:T(8,128)(2,1)S(1)}, bf16[400,128]{1,0:T(8,128)(2,1)S(1)}, u32[]{:S(2)}, u32[]{:S(2)}) collective-permute-start(bf16[400,128]{1,0:T(8,128)(2,1)S(1)} %get-tuple-element.65), channel_id=1, source_target_pairs={{0,16},{4,20},{8,24},{12,28},{16,0},{20,4},{24,8},{28,12},{1,17},{... | collective-permute-start | bytes 307208 | tf_op jit(solution)/shard_map/ppermute | solution.py:420
  60.6 15.8 %collective-permute-start.13 = (bf16[400,128]{1,0:T(8,128)(2,1)S(1)}, bf16[400,128]{1,0:T(8,128)(2,1)S(1)}, u32[]{:S(2)}, u32[]{:S(2)}) collective-permute-start(bf16[400,128]{1,0:T(8,128)(2,1)S(1)} %get-tuple-element.66), channel_id=1, source_target_pairs={{0,20},{4,16},{8,28},{12,24},{16,4},{20,0},{24,12},{28,8},{1,21},{... | collective-permute-start | bytes 307208 | tf_op jit(solution)/shard_map/ppermute | solution.py:420
  63.0 13.4 %collective-permute-start.14 = (bf16[400,128]{1,0:T(8,128)(2,1)S(1)}, bf16[400,128]{1,0:T(8,128)(2,1)S(1)}, u32[]{:S(2)}, u32[]{:S(2)}) collective-permute-start(bf16[400,128]{1,0:T(8,128)(2,1)S(1)} %get-tuple-element.67), channel_id=1, source_target_pairs={{0,24},{4,28},{8,16},{12,20},{16,8},{20,12},{24,0},{28,4},{1,25},{... | collective-permute-start | bytes 307208 | tf_op jit(solution)/shard_map/ppermute | solution.py:420
  64.9 11.5 %collective-permute-start.15 = (bf16[400,128]{1,0:T(8,128)(2,1)S(1)}, bf16[400,128]{1,0:T(8,128)(2,1)S(1)}, u32[]{:S(2)}, u32[]{:S(2)}) collective-permute-start(bf16[400,128]{1,0:T(8,128)(2,1)S(1)} %get-tuple-element.68), channel_id=1, source_target_pairs={{0,28},{4,24},{8,20},{12,16},{16,12},{20,8},{24,4},{28,0},{1,29},{... | collective-permute-start | bytes 307208 | tf_op jit(solution)/shard_map/ppermute | solution.py:420
  67.7 8.7 %collective-permute-start.11 = (bf16[800,128]{1,0:T(8,128)(2,1)S(1)}, bf16[800,128]{1,0:T(8,128)(2,1)S(1)}, u32[]{:S(2)}, u32[]{:S(2)}) collective-permute-start(bf16[800,128]{1,0:T(8,128)(2,1)S(1)} %pad_maximum_fusion), channel_id=1, source_target_pairs={{0,4},{4,0},{8,12},{12,8},{16,20},{20,16},{24,28},{28,24},{1,5},{5... | collective-permute-start | bytes 614408 | tf_op jit(solution)/shard_map/ppermute | solution.py:420
